TPU v7x, 32 devices: a whole 2x2x4 slice. The times are simulated.
32 devices in a mesh: crop: 1, res: 32 (over z, y, x, core).
Axes of the slice: x: 2, y: 2, z: 4, core: 2. Of those that a mesh axis runs over, the one named last changes fastest.
Arguments:
- homolog_symbol_ids: int32 [64, 128], P(('crop', 'res')), may hold values from 0 to 22
- residue_attend_mask: int32 [128], P('crop'), may hold values 0 or 1
- alignment_state: bfloat16 [64, 128, 256], P(('crop', 'res')), may hold values from -6 to 6
- pair: bfloat16 [128, 128, 128], P(('crop', 'res')), may hold values from -6 to 6
- symbol_lookup_matrix: bfloat16 [23, 256], replicated, may hold values from -3 to 3
- pair_bias_weight: bfloat16 [128, 8], replicated, may hold values from -0.5 to 0.5
- row_projection_weight: bfloat16 [256, 1024], replicated, may hold values from -8 to 8
- horizontal_readout_matrix: bfloat16 [256, 256], replicated, may hold values from -0.375 to 0.375
- column_projection_weight: bfloat16 [256, 1024], replicated, may hold values from -8 to 8
- vertical_readout_matrix: bfloat16 [256, 256], replicated, may hold values from -0.375 to 0.375
- product_factor_matrices: bfloat16 [256, 64], replicated, may hold values from -0.375 to 0.375
- outer_output_weight: bfloat16 [1024, 128], replicated, may hold values from -1.5 to 1.5
- triangle_input_weight: bfloat16 [128, 640], replicated, may hold values from -0.5 to 0.5
- triangle_output_weight: bfloat16 [128, 128], replicated, may hold values from -0.5 to 0.5
Outputs:
- alignment_output: bfloat16 [64, 128, 256], P('crop', 'res')
- pair_output: bfloat16 [128, 128, 128], P(('crop', 'res'))
All inputs are finite; a program needn't handle non-finite values.
Results may differ from a plain program's by a relative error of at most 0.013.
Values may be sent and summed in bfloat16 or wider, within the bound.
No kernel may reach another device: no remote copies, remote signals or barrier semaphores. Data moves between devices by JAX's collectives and lax.ppermute only.
A program may use at most 64 MiB of HBM per device.

v0:
```python
import jax
import jax.numpy as jnp
from jax import lax
from jax.sharding import PartitionSpec as P

EPSILON = 1e-05


def layer_normalized(input_rows, axis):
    average = jnp.mean(input_rows, axis, keepdims=True)
    centred = input_rows - average
    spread = jnp.mean(centred * centred, axis, keepdims=True)
    return centred * lax.rsqrt(spread + EPSILON)


def split_proj(input_rows, weight, head_count):
    channels = weight.shape[0]
    head_size = channels // head_count
    projected = jnp.einsum("blc,ce->ble", input_rows, weight, preferred_element_type=jnp.float32)
    lead = projected.shape[:2]
    query_tensor = (
        (projected[..., :channels] * head_size ** (-0.5))
        .astype(jnp.bfloat16)
        .reshape(lead + (head_count, head_size))
    )
    key_tensor = (
        projected[..., channels : 2 * channels]
        .astype(jnp.bfloat16)
        .reshape(lead + (head_count, head_size))
    )
    value_tensor = (
        projected[..., 2 * channels : 3 * channels]
        .astype(jnp.bfloat16)
        .reshape(lead + (head_count, head_size))
    )
    gate_values = projected[..., 3 * channels :]
    return (query_tensor, key_tensor, value_tensor, gate_values)


def attention_block_fn(query_tensor, key_tensor, value_tensor, gate_values, extra_bias, out_weight):
    scores = (
        jnp.einsum("bqhd,bkhd->bhqk", query_tensor, key_tensor, preferred_element_type=jnp.float32)
        + extra_bias
    )
    row_top = jnp.max(scores, -1, keepdims=True)
    exp_scores = jnp.exp(scores - row_top)
    weights = (exp_scores / jnp.sum(exp_scores, -1, keepdims=True)).astype(jnp.bfloat16)
    mixed = jnp.einsum("bhqk,bkhd->bqhd", weights, value_tensor, preferred_element_type=jnp.float32)
    gated = (jax.nn.sigmoid(gate_values) * mixed.reshape(gate_values.shape)).astype(jnp.bfloat16)
    return jnp.einsum("bqc,ce->bqe", gated, out_weight, preferred_element_type=jnp.float32)


def shards(
    homolog_symbol_ids,
    residue_attend_mask,
    alignment_state,
    pair,
    symbol_lookup_matrix,
    pair_bias_weight,
    row_projection_weight,
    horizontal_readout_matrix,
    column_projection_weight,
    vertical_readout_matrix,
    product_factor_matrices,
    outer_output_weight,
    triangle_input_weight,
    triangle_output_weight,
):
    residue_count = lax.axis_size("res")
    sequence_total = alignment_state.shape[0] * residue_count
    res_local = pair.shape[0]
    chain_total = pair.shape[1]
    pair_chan = pair.shape[2]
    owner_chan = pair_chan // residue_count
    outer_chan = product_factor_matrices.shape[1] // 2
    head_count = pair_bias_weight.shape[1]
    token_class_count = symbol_lookup_matrix.shape[0]
    one_hot_tokens = (
        homolog_symbol_ids[:, :, None]
        == jnp.arange(token_class_count, dtype=jnp.int32)[None, None, :]
    ).astype(jnp.bfloat16)
    alignment_initial = alignment_state.astype(jnp.float32) + jnp.einsum(
        "kly,yb->klb", one_hot_tokens, symbol_lookup_matrix, preferred_element_type=jnp.float32
    )
    pair_normed = layer_normalized(pair.astype(jnp.float32), -1).astype(jnp.bfloat16)
    bias_local = jnp.einsum(
        "ijc,ch->hij", pair_normed, pair_bias_weight, preferred_element_type=jnp.float32
    ).astype(jnp.bfloat16)
    mask_bias = (residue_attend_mask.astype(jnp.float32) - 1.0) * 10000.0
    row_input = layer_normalized(alignment_initial, -1).astype(jnp.bfloat16)
    query_tensor, key_tensor, value_tensor, gate_values = split_proj(
        row_input, row_projection_weight, head_count
    )
    bias_all = lax.all_gather(bias_local, "res", axis=1, tiled=True)
    extra_bias = bias_all.astype(jnp.float32)[None] + mask_bias[None, None, None, :]
    row_attention_update = attention_block_fn(
        query_tensor, key_tensor, value_tensor, gate_values, extra_bias, horizontal_readout_matrix
    )
    alignment_after_rows = (alignment_initial + row_attention_update).astype(jnp.bfloat16)
    alignment_columns = lax.all_to_all(
        alignment_after_rows, "res", split_axis=1, concat_axis=0, tiled=True
    )
    column_start = jnp.swapaxes(alignment_columns, 0, 1).astype(jnp.float32)
    col_in = layer_normalized(column_start, -1).astype(jnp.bfloat16)
    col_queries, col_keys, col_values, col_gating = split_proj(
        col_in, column_projection_weight, head_count
    )
    alignment_after_columns = column_start + attention_block_fn(
        col_queries, col_keys, col_values, col_gating, jnp.float32(0.0), vertical_readout_matrix
    )
    alignment_output = jnp.swapaxes(alignment_after_columns, 0, 1).astype(jnp.bfloat16)
    outer_input = layer_normalized(alignment_after_columns, -1).astype(jnp.bfloat16)
    factor_ab = jnp.einsum(
        "rsc,ce->rse", outer_input, product_factor_matrices, preferred_element_type=jnp.float32
    )
    left = factor_ab[..., :outer_chan].astype(jnp.bfloat16)
    latter_factor = (
        factor_ab[..., outer_chan:]
        .astype(jnp.bfloat16)
        .reshape(res_local, sequence_total * outer_chan)
    )
    piece = lax.all_gather(latter_factor, "res", axis=0, tiled=True)
    count = piece.shape[0]
    right_rows = piece.reshape(count, sequence_total, outer_chan)
    cross_product_result = (
        jnp.einsum("isc,jsd->ijcd", left, right_rows, preferred_element_type=jnp.float32)
        / sequence_total
    ).astype(jnp.bfloat16)
    update = jnp.einsum(
        "ije,ez->ijz",
        cross_product_result.reshape(res_local, count, outer_chan * outer_chan),
        outer_output_weight,
        preferred_element_type=jnp.float32,
    )
    pair_one = pair.astype(jnp.float32) + update
    tri_normed = layer_normalized(pair_one, -1).astype(jnp.bfloat16)
    factors = jnp.einsum(
        "ijc,ce->eij",
        tri_normed,
        triangle_input_weight[:, : 4 * pair_chan],
        preferred_element_type=jnp.float32,
    )
    gate_out = jnp.einsum(
        "ijc,ce->ije",
        tri_normed,
        triangle_input_weight[:, 4 * pair_chan :],
        preferred_element_type=jnp.float32,
    )
    left_f = (jax.nn.sigmoid(factors[pair_chan : 2 * pair_chan]) * factors[:pair_chan]).astype(
        jnp.bfloat16
    )
    right_f = (
        jax.nn.sigmoid(factors[3 * pair_chan :]) * factors[2 * pair_chan : 3 * pair_chan]
    ).astype(jnp.bfloat16)
    left_f = left_f.reshape(residue_count, owner_chan, res_local, chain_total)
    right_f = right_f.reshape(residue_count, owner_chan, res_local, chain_total)
    combined = jnp.einsum(
        "xcik,xcjk->xcij",
        lax.all_to_all(left_f, "res", split_axis=0, concat_axis=2, tiled=True),
        lax.all_to_all(right_f, "res", split_axis=0, concat_axis=2, tiled=True),
        preferred_element_type=jnp.float32,
    ).astype(jnp.bfloat16)
    back_rows = lax.all_to_all(combined, "res", split_axis=2, concat_axis=0, tiled=True)
    back_rows = back_rows.reshape(pair_chan, res_local, chain_total)
    comb_normed = layer_normalized(back_rows.astype(jnp.float32), 0).astype(jnp.bfloat16)
    tri_update = jnp.einsum(
        "cij,cz->ijz", comb_normed, triangle_output_weight, preferred_element_type=jnp.float32
    )
    pair_output = (pair_one + jax.nn.sigmoid(gate_out) * tri_update).astype(jnp.bfloat16)
    return (alignment_output, pair_output)


def solution(mesh):
    placed = (
        P(("crop", "res"), None),
        P("crop"),
        P(("crop", "res"), None, None),
        P(("crop", "res"), None, None),
        P(),
        P(),
        P(),
        P(),
        P(),
        P(),
        P(),
        P(),
        P(),
        P(),
    )
    return jax.shard_map(
        shards,
        mesh=mesh,
        in_specs=placed,
        out_specs=(P("crop", "res", None), P(("crop", "res"), None, None)),
        check_vma=False,
    )
```

profile of v0, /device:TPU:0, one launch (start us, length us, event | category | flops | bytes accessed | tf_op | source)
XLA Modules:
  0.0 155.4 jit_solution(11216174859262117624)
XLA Ops:
  0.7 0.7 add_multiply_fusion
  1.4 1.0 copy.74
  2.5 0.8 fusion.14
  3.4 43.9 %all_gather.6 = bf16[8,128,128]{2,0,1:T(8,128)(2,1)S(1)} all-gather(bf16[8,4,128]{2,0,1:T(8,128)(2,1)S(1)} %fusion.14), channel_id=1, replica_groups=mesh['crop'=1,'res'=32] {'res'}, dimensions={1}, use_global_device_ids=true | all-gather | bytes 270336 | tf_op jit(solution)/shard_map/all_gather | solution.py:94
  47.3 0.2 copy.76
  47.6 0.3 fusion.84
  48.1 0.3 fusion.85
  48.5 0.7 fusion.83
  49.4 0.5 copy-done.1
  50.1 0.5 fusion.86
  50.6 1.3 convolution_add_fusion
  51.9 1.0 copy.71
  52.9 1.0 fusion.20
  54.0 1.1 copy.78
  55.1 1.1 fusion.11
  56.4 9.9 %all_to_all.48 = bf16[2,128,256]{2,0,1:T(2,128)(2,1)S(1)} all-to-all(bf16[2,128,256]{2,0,1:T(2,128)(2,1)S(1)} %copy.79), channel_id=1, replica_groups=mesh['crop'=1,'res'=32] {'res'}, dimensions={1} | all-to-all | bytes 262144 | tf_op jit(solution)/shard_map/all_to_all | solution.py:100
  66.7 0.2 multiply_reduce_fusion.2
  66.9 0.3 fusion.87
  67.3 0.7 fusion.82
  68.3 0.5 fusion.88
  68.8 0.3 fusion.90
  69.2 1.1 copy.81
  70.3 1.2 fusion.19
  71.4 1.2 copy.85
  72.7 1.1 fusion.46
  73.9 0.2 multiply_reduce_fusion.1
  74.1 0.3 convolution_convert_fusion.1
  74.7 39.3 %all-gather = bf16[32,4,2048]{2,1,0:T(4,128)(2,1)S(1)} all-gather(bf16[1,4,2048]{2,1,0:T(4,128)(2,1)S(1)} %reshape.173), channel_id=1, replica_groups=mesh['crop'=1,'res'=32] {'res'}, dimensions={0}, use_global_device_ids=true | all-gather | bytes 540672 | tf_op jit(solution)/shard_map/all_gather | solution.py:122
  114.0 1.2 reshape.160
  115.2 2.6 %copy.109 = bf16[128,64,32,1]{0,1,3,2:T(8,128)(2,1)S(1)} copy(bf16[128,64,32,1]{2,1,0,3:T(8,128)(2,1)S(1)} %bitcast.133) | data formatting | bytes 1048576 | tf_op jit(solution)/shard_map/reshape | solution.py:124
  117.8 0.4 fusion.6
  118.2 0.7 copy.88
  118.9 0.4 fusion.89
  119.4 0.3 convolution_bitcast_fusion
  120.0 0.7 copy.98
  120.7 2.6 %all-to-all-start.2 = ((bf16[32,4,4,128]{3,1,2,0:T(4,128)(2,1)}), bf16[32,4,4,128]{3,1,2,0:T(4,128)(2,1)S(1)}, u32[]{:S(2)}, u32[]{:S(2)}) async-start(bf16[32,4,4,128]{3,1,2,0:T(4,128)(2,1)} %copy.98), calls=%async_computation.2 | async-start | bytes 262144 | tf_op jit(solution)/shard_map/all_to_all | solution.py:160
  123.4 0.7 copy.95
  124.1 7.4 %all-to-all-done.2 = bf16[32,4,4,128]{3,1,2,0:T(4,128)(2,1)S(1)} async-done(((bf16[32,4,4,128]{3,1,2,0:T(4,128)(2,1)}), bf16[32,4,4,128]{3,1,2,0:T(4,128)(2,1)S(1)}, u32[]{:S(2)}, u32[]{:S(2)}) %all-to-all-start.2) | async-done | bytes 131104 | tf_op jit(solution)/shard_map/all_to_all | solution.py:160
  131.5 2.6 %all-to-all-start.1 = ((bf16[32,4,4,128]{3,1,2,0:T(4,128)(2,1)}), bf16[32,4,4,128]{3,1,2,0:T(4,128)(2,1)S(1)}, u32[]{:S(2)}, u32[]{:S(2)}) async-start(bf16[32,4,4,128]{3,1,2,0:T(4,128)(2,1)} %copy.95), calls=%async_computation.1 | async-start | bytes 262144 | tf_op jit(solution)/shard_map/all_to_all | solution.py:159
  134.1 8.2 %all-to-all-done.1 = bf16[32,4,4,128]{3,1,2,0:T(4,128)(2,1)S(1)} async-done(((bf16[32,4,4,128]{3,1,2,0:T(4,128)(2,1)}), bf16[32,4,4,128]{3,1,2,0:T(4,128)(2,1)S(1)}, u32[]{:S(2)}, u32[]{:S(2)}) %all-to-all-start.1) | async-done | bytes 131104 | tf_op jit(solution)/shard_map/all_to_all | solution.py:159
  142.4 0.2 fusion.13
  142.6 0.8 copy.100
  143.3 2.6 %all-to-all-start.3 = ((bf16[1,4,128,128]{3,1,0,2:T(4,128)(2,1)}), bf16[1,4,128,128]{3,1,0,2:T(4,128)(2,1)S(1)}, u32[]{:S(2)}, u32[]{:S(2)}) async-start(bf16[1,4,128,128]{3,1,0,2:T(4,128)(2,1)} %copy.100), calls=%async_computation.3 | async-start | bytes 262144 | tf_op jit(solution)/shard_map/all_to_all | solution.py:163
  145.9 0.8 copy.104
  146.7 0.3 fusion.10
  147.0 7.2 %all-to-all-done.3 = bf16[1,4,128,128]{3,1,0,2:T(4,128)(2,1)S(1)} async-done(((bf16[1,4,128,128]{3,1,0,2:T(4,128)(2,1)}), bf16[1,4,128,128]{3,1,0,2:T(4,128)(2,1)S(1)}, u32[]{:S(2)}, u32[]{:S(2)}) %all-to-all-start.3) | async-done | bytes 131104 | tf_op jit(solution)/shard_map/all_to_all | solution.py:163
  154.4 0.2 fusion.12
  154.6 0.8 copy.105
  (60 shorter events, 2.9 us)
Async XLA Ops:
  0.6 47.5 %copy-start = (bf16[256,1024]{1,0:T(8,128)(2,1)S(1)}, bf16[256,1024]{1,0:T(8,128)(2,1)}, u32[]{:S(2)}) copy-start(bf16[256,1024]{1,0:T(8,128)(2,1)} %param.20) | copy-start | bytes 1572868
  0.6 46.9 %copy-start.9 = (bf16[23,256]{1,0:T(8,128)(2,1)S(1)}, bf16[23,256]{1,0:T(8,128)(2,1)}, u32[]{:S(2)}) copy-start(bf16[23,256]{1,0:T(8,128)(2,1)} %param.18) | copy-start | bytes 35332
  0.7 46.9 %copy-start.5 = (bf16[2,128,256]{2,1,0:T(8,128)(2,1)S(1)}, bf16[2,128,256]{2,1,0:T(8,128)(2,1)}, u32[]{:S(2)}) copy-start(bf16[2,128,256]{2,1,0:T(8,128)(2,1)} %param.16) | copy-start | bytes 393220
  0.7 46.9 %copy-start.10 = (s32[2,128]{1,0:T(2,128)S(1)}, s32[2,128]{1,0:T(2,128)}, u32[]{:S(2)}) copy-start(s32[2,128]{1,0:T(2,128)} %param.14) | copy-start | bytes 3076
  49.3 0.6 copy-start.1
  49.4 0.7 copy-start.2
  54.0 13.0 %copy-start.3 = (bf16[256,1024]{1,0:T(8,128)(2,1)S(1)}, bf16[256,1024]{1,0:T(8,128)(2,1)}, u32[]{:S(2)}) copy-start(bf16[256,1024]{1,0:T(8,128)(2,1)} %param.22) | copy-start | bytes 1572868
  71.4 2.7 %copy-start.7 = (bf16[256,64]{0,1:T(8,128)(2,1)S(1)}, bf16[256,64]{0,1:T(8,128)(2,1)}, u32[]{:S(2)}) copy-start(bf16[256,64]{0,1:T(8,128)(2,1)} %param.24) | copy-start | bytes 98308
  117.8 1.1 copy-start.4
  118.2 1.2 copy-start.6
  120.7 10.8 %all-to-all-start.2 = ((bf16[32,4,4,128]{3,1,2,0:T(4,128)(2,1)}), bf16[32,4,4,128]{3,1,2,0:T(4,128)(2,1)S(1)}, u32[]{:S(2)}, u32[]{:S(2)}) async-start(bf16[32,4,4,128]{3,1,2,0:T(4,128)(2,1)} %copy.98), calls=%async_computation.2 | async-start | bytes 262144 | tf_op jit(solution)/shard_map/all_to_all | solution.py:160
  123.4 31.0 %copy-start.8 = (bf16[128,128]{1,0:T(8,128)(2,1)S(1)}, bf16[128,128]{1,0:T(8,128)(2,1)}, u32[]{:S(2)}) copy-start(bf16[128,128]{1,0:T(8,128)(2,1)} %param.27) | copy-start | bytes 98308
  131.5 10.8 %all-to-all-start.1 = ((bf16[32,4,4,128]{3,1,2,0:T(4,128)(2,1)}), bf16[32,4,4,128]{3,1,2,0:T(4,128)(2,1)S(1)}, u32[]{:S(2)}, u32[]{:S(2)}) async-start(bf16[32,4,4,128]{3,1,2,0:T(4,128)(2,1)} %copy.95), calls=%async_computation.1 | async-start | bytes 262144 | tf_op jit(solution)/shard_map/all_to_all | solution.py:159
  143.3 10.8 %all-to-all-start.3 = ((bf16[1,4,128,128]{3,1,0,2:T(4,128)(2,1)}), bf16[1,4,128,128]{3,1,0,2:T(4,128)(2,1)S(1)}, u32[]{:S(2)}, u32[]{:S(2)}) async-start(bf16[1,4,128,128]{3,1,0,2:T(4,128)(2,1)} %copy.100), calls=%async_computation.3 | async-start | bytes 262144 | tf_op jit(solution)/shard_map/all_to_all | solution.py:163
where the time goes:
time: 156 us; the launch traced here: 155 us
  blocking collectives  93.2 us (60%)
  waiting for transfers between devices  22.7 us (15%)
  local copies, waits for them, and re-layouts  17.4 us (11%)
  matrix products  11 us (7%)
  starting transfers between devices  7.73 us (5%)
  other arithmetic  2.2 us (1%)
    all_gather x1, blocking collectives, shards(): bias_all = lax.all_gather(bias_local, 'res', axis=1, tiled=True)  43.9 us
    all_gather x1, blocking collectives, shards(): piece = lax.all_gather(latter_factor, 'res', axis=0, tiled=True)  39.3 us
    all_to_all x1, blocking collectives, shards(): lax.all_to_all(alignment_after_rows, 'res', split_axis=1, concat_axis=0,...  9.93 us
    all_to_all x1, waiting for transfers between devices, shards(): lax.all_to_all(left_f, 'res', split_axis=0, concat_axis=2, tiled=True)  8.17 us
    all_to_all x1, waiting for transfers between devices, shards(): lax.all_to_all(right_f, 'res', split_axis=0, concat_axis=2, tiled=True)  7.38 us
    all_to_all x1, waiting for transfers between devices, shards(): lax.all_to_all(combined, 'res', split_axis=2, concat_axis=0, tiled=True)  7.2 us
    reshape x2, local copies, waits for them, and re-layouts, shards(): right_rows = piece.reshape(count, sequence_total, outer_chan)  3.78 us
    unnamed x26, local copies, waits for them, and re-layouts  3.38 us
  transfers between devices with their start and end apart: 3, of which 3 were waited for; matrix products, arithmetic and copies ran while one was open for 1% of the time, Pallas kernels for 0%

commit v1 on v0

--- a/solution.py
+++ b/solution.py
@@ -48,6 +48,11 @@
     mixed = jnp.einsum("bhqk,bkhd->bqhd", weights, value_tensor, preferred_element_type=jnp.float32)
     gated = (jax.nn.sigmoid(gate_values) * mixed.reshape(gate_values.shape)).astype(jnp.bfloat16)
     return jnp.einsum("bqc,ce->bqe", gated, out_weight, preferred_element_type=jnp.float32)
+
+
+def gathered(block, axis_name):
+    copies = jnp.broadcast_to(block[None], (lax.axis_size(axis_name),) + block.shape)
+    return lax.all_to_all(copies, axis_name, split_axis=0, concat_axis=0, tiled=True)
 
 
 def shards(
@@ -91,7 +96,9 @@
     query_tensor, key_tensor, value_tensor, gate_values = split_proj(
         row_input, row_projection_weight, head_count
     )
-    bias_all = lax.all_gather(bias_local, "res", axis=1, tiled=True)
+    bias_all = jnp.moveaxis(gathered(bias_local, "res"), 0, 1).reshape(
+        head_count, chain_total, chain_total
+    )
     extra_bias = bias_all.astype(jnp.float32)[None] + mask_bias[None, None, None, :]
     row_attention_update = attention_block_fn(
         query_tensor, key_tensor, value_tensor, gate_values, extra_bias, horizontal_readout_matrix
@@ -119,8 +126,8 @@
         .astype(jnp.bfloat16)
         .reshape(res_local, sequence_total * outer_chan)
     )
-    piece = lax.all_gather(latter_factor, "res", axis=0, tiled=True)
-    count = piece.shape[0]
+    piece = gathered(latter_factor, "res")
+    count = chain_total
     right_rows = piece.reshape(count, sequence_total, outer_chan)
     cross_product_result = (
         jnp.einsum("isc,jsd->ijcd", left, right_rows, preferred_element_type=jnp.float32)
@@ -154,12 +161,13 @@
     ).astype(jnp.bfloat16)
     left_f = left_f.reshape(residue_count, owner_chan, res_local, chain_total)
     right_f = right_f.reshape(residue_count, owner_chan, res_local, chain_total)
+    both = lax.all_to_all(
+        jnp.stack([left_f, right_f], 1), "res", split_axis=0, concat_axis=0, tiled=True
+    )
+    both = jnp.moveaxis(both, 0, 2).reshape(2, owner_chan, chain_total, chain_total)
     combined = jnp.einsum(
-        "xcik,xcjk->xcij",
-        lax.all_to_all(left_f, "res", split_axis=0, concat_axis=2, tiled=True),
-        lax.all_to_all(right_f, "res", split_axis=0, concat_axis=2, tiled=True),
-        preferred_element_type=jnp.float32,
-    ).astype(jnp.bfloat16)
+        "cik,cjk->cij", both[0], both[1], preferred_element_type=jnp.float32
+    ).astype(jnp.bfloat16)[None]
     back_rows = lax.all_to_all(combined, "res", split_axis=2, concat_axis=0, tiled=True)
     back_rows = back_rows.reshape(pair_chan, res_local, chain_total)
     comb_normed = layer_normalized(back_rows.astype(jnp.float32), 0).astype(jnp.bfloat16)

time: 156 us -> 98.1 us (0.63)
  blocking collectives: 93.2 us -> 41.2 us
  waiting for transfers between devices: 22.7 us -> 14.8 us
  starting transfers between devices: 7.73 us -> 9.86 us
  matrix products: 11 us -> 12.6 us
    all_gather x2 -> x0, blocking collectives: 83.2 us -> none  [the longest x1 43.9 us: shards(): bias_all = lax.all_gather(bias_local, 'res', axis=1, tiled=True)]
    all_to_all x0 -> x2, blocking collectives: none -> 30.8 us  [the longest x1 17.3 us: gathered(): lax.all_to_all(copies, axis_name, split_axis=0, concat_axis=0, tiled=True)]
    all_to_all x2 -> x1, waiting for transfers between devices: 15.5 us -> 7.65 us  [gathered(): lax.all_to_all(copies, axis_name, split_axis=0, concat_axis=0, tiled=True)]
    all_to_all x2 -> x1, starting transfers between devices: 5.15 us -> 7.3 us  [gathered(): lax.all_to_all(copies, axis_name, split_axis=0, concat_axis=0, tiled=True)]
    broadcast_in_dim x0 -> x4, local copies, waits for them, and re-layouts: none -> 1.83 us  [the longest x3 1.09 us: gathered(): jnp.broadcast_to(block[None], (lax.axis_size(axis_name),) + block.shape)]
    unnamed x26 -> x29, local copies, waits for them, and re-layouts: 3.38 us -> 3.3 us
  transfers between devices with their start and end apart: 3 -> 2, of which waited for: 3 -> 2; matrix products, arithmetic and copies ran while one was open for 1% -> 4% of each run, Pallas kernels for 0% -> 0%
where the time goes in v1:
time: 98.1 us; the launch traced here: 97.7 us
  blocking collectives  41.2 us (42%)
  local copies, waits for them, and re-layouts  16.3 us (17%)
  waiting for transfers between devices  14.8 us (15%)
  matrix products  12.6 us (13%)
  starting transfers between devices  9.86 us (10%)
  other arithmetic  1.66 us (2%)
  between operations  1.21 us (1%)
    all_to_all x1, blocking collectives, gathered(): lax.all_to_all(copies, axis_name, split_axis=0, concat_axis=0, tiled=True)  17.3 us
    all_to_all x1, blocking collectives, shards(): lax.all_to_all(jnp.stack([left_f, right_f], 1), 'res', split_axis=0, conc...  13.5 us
    all_to_all x1, blocking collectives, shards(): lax.all_to_all(alignment_after_rows, 'res', split_axis=1, concat_axis=0,...  10.4 us
    all_to_all x1, waiting for transfers between devices, gathered(): lax.all_to_all(copies, axis_name, split_axis=0, concat_axis=0, tiled=True)  7.65 us
    all_to_all x1, starting transfers between devices, gathered(): lax.all_to_all(copies, axis_name, split_axis=0, concat_axis=0, tiled=True)  7.3 us
    all_to_all x1, waiting for transfers between devices, shards(): lax.all_to_all(combined, 'res', split_axis=2, concat_axis=0, tiled=True)  7.19 us
    reshape x2, local copies, waits for them, and re-layouts, shards(): right_rows = piece.reshape(count, sequence_total, outer_chan)  3.78 us
    unnamed x29, local copies, waits for them, and re-layouts  3.3 us
  transfers between devices with their start and end apart: 2, of which 2 were waited for; matrix products, arithmetic and copies ran while one was open for 4% of the time, Pallas kernels for 0%

profile of v1, /device:TPU:0, one launch (start us, length us, event | category | flops | bytes accessed | tf_op | source)
XLA Modules:
  0.0 97.7 jit_solution(18122057268983419979)
XLA Ops:
  0.6 1.1 %copy.74 = bf16[4,128,128]{1,2,0:T(8,128)(2,1)S(1)} copy(bf16[4,128,128]{2,1,0:T(8,128)(2,1)} %param.17) | data formatting | bytes 262144 | tf_op args[3]
  1.8 0.8 fusion.14
  2.7 0.7 broadcast_in_dim.8
  3.4 7.3 %all-to-all-start = ((bf16[32,8,4,128]{3,1,2,0:T(8,128)(2,1)}), bf16[32,8,4,128]{3,1,2,0:T(8,128)(2,1)S(1)}, u32[]{:S(2)}, u32[]{:S(2)}) async-start(bf16[32,8,4,128]{3,1,2,0:T(8,128)(2,1)} %broadcast_in_dim.8), calls=%async_computation | async-start | bytes 524288 | tf_op jit(solution)/shard_map/all_to_all | solution.py:55
  10.7 1.2 %fusion.85 = (f32[2,128]{1,0:T(2,128)S(1)}, f32[2,128,256]{2,1,0:T(8,128)S(1)}) fusion(bf16[23,256]{1,0:T(8,128)(2,1)} %param.18, s32[2,128]{1,0:T(2,128)} %param.14, bf16[2,128,256]{2,1,0:T(8,128)(2,1)} %param.16), kind=kOutput, calls=%fused_computation.137 | convolution fusion | flops 3216896 | bytes 407040 | tf_op jit(solution)/shard_map/kly,yb->klb/dot_general | solution.py:87
  12.0 0.2 multiply_reduce_fusion.3
  12.2 0.3 fusion.86
  12.7 0.8 copy.71
  13.7 7.7 %all-to-all-done = bf16[32,8,4,128]{3,1,2,0:T(8,128)(2,1)S(1)} async-done(((bf16[32,8,4,128]{3,1,2,0:T(8,128)(2,1)}), bf16[32,8,4,128]{3,1,2,0:T(8,128)(2,1)S(1)}, u32[]{:S(2)}, u32[]{:S(2)}) %all-to-all-start) | async-done | bytes 262176 | tf_op jit(solution)/shard_map/all_to_all | solution.py:55
  21.4 0.2 copy.76
  21.6 0.5 fusion.87
  22.1 1.3 %convolution_add_fusion = f32[2,8,128,128]{2,3,1,0:T(8,128)S(1)} fusion(bf16[2,128,8,32]{1,3,2,0:T(8,128)(2,1)} %bitcast.146, bf16[2,128,8,32]{1,3,2,0:T(8,128)(2,1)} %bitcast.144, f32[8,128,128]{1,2,0:T(8,128)S(1)} %copy.76), kind=kOutput, calls=%fused_computation.9 | convolution fusion | flops 17039360 | bytes 1835008 | tf_op jit(solution)/shard_map/bqhd,bkhd->bhqk/dot_general | solution.py:42
  23.4 1.9 %fusion.20 = f32[2,8,32,128]{3,2,1,0:T(8,128)} fusion(bf16[2,128,8,32]{1,3,2,0:T(8,128)(2,1)} %bitcast.155, f32[2,8,128]{2,1,0:T(8,128)S(1)} %fusion.87, f32[2,8,128,128]{2,3,1,0:T(8,128)S(1)} %convolution_add_fusion), kind=kOutput, calls=%fused_computation.34 | convolution fusion | flops 17565824 | bytes 1449984 | tf_op jit(solution)/shard_map/bhqk,bkhd->bqhd/dot_general | solution.py:48
  25.4 1.1 %copy.78 = f32[2,128,256]{2,1,0:T(8,128)S(1)} copy(f32[2,128,256]{1,2,0:T(8,128)} %bitcast.154) | data formatting | bytes 524288 | tf_op jit(solution)/shard_map/reshape | solution.py:49
  26.5 1.1 %fusion.11 = bf16[2,128,256]{2,1,0:T(8,128)(2,1)S(1)} fusion(f32[2,128,256]{2,1,0:T(8,128)S(1)} %get-tuple-element.17, f32[2,128,256]{2,1,0:T(8,128)S(1)} %copy.78, f32[2,128,1024]{2,1,0:T(8,128)S(1)} %get-tuple-element.19, bf16[256,256]{1,0:T(8,128)(2,1)} %param.21), kind=kOutput, calls=%fused_computation.19 | convolution fusion | flops 34013184 | bytes 1048576 | tf_op jit(solution)/shard_map/bqc,ce->bqe/dot_general | solution.py:50
  27.8 10.4 %all_to_all.33 = bf16[2,128,256]{2,0,1:T(2,128)(2,1)S(1)} all-to-all(bf16[2,128,256]{2,0,1:T(2,128)(2,1)S(1)} %copy.79), channel_id=1, replica_groups=mesh['crop'=1,'res'=32] {'res'}, dimensions={1} | all-to-all | bytes 262144 | tf_op jit(solution)/shard_map/all_to_all | solution.py:107
  38.3 0.2 reshape.159
  38.6 0.2 multiply_reduce_fusion.2
  38.8 0.3 fusion.88
  39.2 0.7 fusion.82
  40.1 0.2 copy.82
  40.3 0.5 fusion.89
  40.8 0.3 fusion.91
  41.1 1.1 %copy.81 = bf16[4,64,256]{1,2,0:T(8,128)(2,1)S(1)} copy(bf16[4,64,256]{2,1,0:T(8,128)(2,1)} %get-tuple-element.11) | data formatting | bytes 262144 | tf_op jit(solution)/shard_map/slice | solution.py:32
  42.2 1.1 %fusion.19 = f32[4,8,32,64]{3,2,1,0:T(8,128)} fusion(bf16[4,64,8,32]{1,3,2,0:T(8,128)(2,1)S(1)} %bitcast.153, f32[4,8,64]{2,1,0:T(8,128)S(1)} %fusion.89, f32[4,8,64,64]{2,3,1,0:T(8,128)S(1)} %fusion.91), kind=kOutput, calls=%fused_computation.33 | convolution fusion | flops 8783935 | bytes 925696 | tf_op jit(solution)/shard_map/bhqk,bkhd->bqhd/dot_general | solution.py:48
  43.3 1.2 %copy.85 = f32[4,64,256]{2,1,0:T(8,128)S(1)} copy(f32[4,64,256]{1,2,0:T(8,128)} %bitcast.150) | data formatting | bytes 524288 | tf_op jit(solution)/shard_map/reshape | solution.py:49
  44.6 0.9 fusion.46
  45.6 0.2 multiply_reduce_fusion.1
  45.8 0.3 convolution_convert_fusion.1
  46.1 0.6 copy-done.4
  47.0 0.2 broadcast_in_dim.10
  47.2 17.3 %all_to_all.34 = bf16[32,4,2048]{2,1,0:T(4,128)(2,1)S(1)} all-to-all(bf16[32,4,2048]{2,1,0:T(4,128)(2,1)S(1)} %broadcast_in_dim.10), channel_id=1, replica_groups=mesh['crop'=1,'res'=32] {'res'}, dimensions={0} | all-to-all | bytes 1048576 | tf_op jit(solution)/shard_map/all_to_all | solution.py:55
  64.5 1.2 %reshape.155 = bf16[128,64,32]{2,1,0:T(8,128)(2,1)S(1)} reshape(bf16[32,4,2048]{2,1,0:T(4,128)(2,1)S(1)} %all_to_all.34) | data formatting | bytes 1048576 | tf_op jit(solution)/shard_map/reshape | solution.py:131
  65.7 2.6 %copy.108 = bf16[128,64,32,1]{0,1,3,2:T(8,128)(2,1)S(1)} copy(bf16[128,64,32,1]{2,1,0,3:T(8,128)(2,1)S(1)} %bitcast.132) | data formatting | bytes 1048576 | tf_op jit(solution)/shard_map/reshape | solution.py:131
  68.3 0.4 fusion.6
  68.8 0.7 copy.88
  69.5 0.4 fusion.90
  69.9 0.3 convolution_bitcast_fusion
  70.7 0.2 pad_maximum_fusion
  71.0 13.5 %all_to_all.35 = bf16[32,2,4,4,128]{4,2,3,1,0:T(4,128)(2,1)S(1)} all-to-all(bf16[32,2,4,4,128]{4,2,3,1,0:T(4,128)(2,1)S(1)} %copy.96), channel_id=1, replica_groups=mesh['crop'=1,'res'=32] {'res'}, dimensions={0} | all-to-all | bytes 524288 | tf_op jit(solution)/shard_map/all_to_all | solution.py:164
  84.7 0.2 fusion.13
  84.9 0.7 copy.99
  85.6 2.6 %all-to-all-start.4 = ((bf16[1,4,128,128]{3,1,0,2:T(4,128)(2,1)}), bf16[1,4,128,128]{3,1,0,2:T(4,128)(2,1)S(1)}, u32[]{:S(2)}, u32[]{:S(2)}) async-start(bf16[1,4,128,128]{3,1,0,2:T(4,128)(2,1)} %copy.99), calls=%async_computation.4 | async-start | bytes 262144 | tf_op jit(solution)/shard_map/all_to_all | solution.py:171
  88.2 0.8 copy.103
  89.0 0.3 fusion.10
  89.2 7.2 %all-to-all-done.4 = bf16[1,4,128,128]{3,1,0,2:T(4,128)(2,1)S(1)} async-done(((bf16[1,4,128,128]{3,1,0,2:T(4,128)(2,1)}), bf16[1,4,128,128]{3,1,0,2:T(4,128)(2,1)S(1)}, u32[]{:S(2)}, u32[]{:S(2)}) %all-to-all-start.4) | async-done | bytes 131104 | tf_op jit(solution)/shard_map/all_to_all | solution.py:171
  96.7 0.2 fusion.12
  96.9 0.8 copy.104
  (65 shorter events, 2.4 us)
Async XLA Ops:
  0.6 11.6 %copy-start = (bf16[256,1024]{1,0:T(8,128)(2,1)S(1)}, bf16[256,1024]{1,0:T(8,128)(2,1)}, u32[]{:S(2)}) copy-start(bf16[256,1024]{1,0:T(8,128)(2,1)} %param.20) | copy-start | bytes 1572868
  3.4 17.9 %all-to-all-start = ((bf16[32,8,4,128]{3,1,2,0:T(8,128)(2,1)}), bf16[32,8,4,128]{3,1,2,0:T(8,128)(2,1)S(1)}, u32[]{:S(2)}, u32[]{:S(2)}) async-start(bf16[32,8,4,128]{3,1,2,0:T(8,128)(2,1)} %broadcast_in_dim.8), calls=%async_computation | async-start | bytes 524288 | tf_op jit(solution)/shard_map/all_to_all | solution.py:55
  12.2 1.5 %copy-start.12 = (s32[128]{0:T(128)S(1)}, s32[128]{0:T(128)}, u32[]{:S(2)}) copy-start(s32[128]{0:T(128)} %param.15) | copy-start | bytes 1540
  12.7 8.9 %copy-start.1 = (bf16[2,128,256]{1,2,0:T(8,128)(2,1)}, bf16[2,128,256]{1,2,0:T(8,128)(2,1)S(1)}, u32[]{:S(2)}) copy-start(bf16[2,128,256]{1,2,0:T(8,128)(2,1)S(1)} %copy.73) | copy-start | bytes 393220
  13.6 8.0 %copy-start.2 = (bf16[2,128,256]{1,2,0:T(8,128)(2,1)}, bf16[2,128,256]{1,2,0:T(8,128)(2,1)S(1)}, u32[]{:S(2)}) copy-start(bf16[2,128,256]{1,2,0:T(8,128)(2,1)S(1)} %copy.72) | copy-start | bytes 393220
  25.4 13.5 %copy-start.3 = (bf16[256,1024]{1,0:T(8,128)(2,1)S(1)}, bf16[256,1024]{1,0:T(8,128)(2,1)}, u32[]{:S(2)}) copy-start(bf16[256,1024]{1,0:T(8,128)(2,1)} %param.22) | copy-start | bytes 1572868
  42.2 2.4 %copy-start.11 = (bf16[256,256]{1,0:T(8,128)(2,1)S(1)}, bf16[256,256]{1,0:T(8,128)(2,1)}, u32[]{:S(2)}) copy-start(bf16[256,256]{1,0:T(8,128)(2,1)} %param.23) | copy-start | bytes 393220
  43.3 2.5 %copy-start.9 = (bf16[256,64]{0,1:T(8,128)(2,1)S(1)}, bf16[256,64]{0,1:T(8,128)(2,1)}, u32[]{:S(2)}) copy-start(bf16[256,64]{0,1:T(8,128)(2,1)} %param.24) | copy-start | bytes 98308
  46.1 0.6 copy-start.4
  64.5 3.8 %copy-start.5 = (bf16[4,64,64]{1,2,0:T(8,128)(2,1)S(1)}, bf16[4,64,64]{1,2,0:T(8,128)(2,1)}, u32[]{:S(2)}) copy-start(bf16[4,64,64]{1,2,0:T(8,128)(2,1)} %copy-done.4) | copy-start | bytes 98308
  68.3 1.1 %copy-start.6 = (bf16[1024,128]{1,0:T(8,128)(2,1)S(1)}, bf16[1024,128]{1,0:T(8,128)(2,1)}, u32[]{:S(2)}) copy-start(bf16[1024,128]{1,0:T(8,128)(2,1)} %param.25) | copy-start | bytes 786436
  68.8 1.2 %copy-start.8 = (bf16[128,640]{1,0:T(8,128)(2,1)S(1)}, bf16[128,640]{1,0:T(8,128)(2,1)}, u32[]{:S(2)}) copy-start(bf16[128,640]{1,0:T(8,128)(2,1)} %param.26) | copy-start | bytes 491524
  70.4 17.8 %copy-start.7 = (bf16[64,4,256]{2,0,1:T(8,128)(2,1)S(1)}, bf16[64,4,256]{2,0,1:T(8,128)(2,1)}, u32[]{:S(2)}) copy-start(bf16[64,4,256]{2,0,1:T(8,128)(2,1)} %get-tuple-element.22) | copy-start | bytes 393220
  84.5 12.2 %copy-start.10 = (bf16[128,128]{1,0:T(8,128)(2,1)S(1)}, bf16[128,128]{1,0:T(8,128)(2,1)}, u32[]{:S(2)}) copy-start(bf16[128,128]{1,0:T(8,128)(2,1)} %param.27) | copy-start | bytes 98308
  85.6 10.8 %all-to-all-start.4 = ((bf16[1,4,128,128]{3,1,0,2:T(4,128)(2,1)}), bf16[1,4,128,128]{3,1,0,2:T(4,128)(2,1)S(1)}, u32[]{:S(2)}, u32[]{:S(2)}) async-start(bf16[1,4,128,128]{3,1,0,2:T(4,128)(2,1)} %copy.99), calls=%async_computation.4 | async-start | bytes 262144 | tf_op jit(solution)/shard_map/all_to_all | solution.py:171

commit v2 on v0

v2 whole, which is shorter than its diff:
```python
import functools

import jax
import jax.numpy as jnp
from jax import lax
from jax.experimental import pallas as pl
from jax.experimental.pallas import tpu as pltpu
from jax.sharding import PartitionSpec as P

EPSILON = 1e-05
F32 = jnp.float32
BF16 = jnp.bfloat16
VMEM_BYTES = 48 * 1024 * 1024


def normalized(rows, axis):
    average = jnp.mean(rows, axis, keepdims=True)
    centred = rows - average
    spread = jnp.mean(centred * centred, axis, keepdims=True)
    return centred * lax.rsqrt(spread + EPSILON)


def dot(a, b):
    return jnp.dot(a, b, preferred_element_type=F32)


def dot_t(a, b):
    return lax.dot_general(a, b, (((1,), (1,)), ((), ())), preferred_element_type=F32)


def t_dot(a, b):
    return lax.dot_general(a, b, (((0,), (0,)), ((), ())), preferred_element_type=F32)


def iota(shape, axis):
    return lax.broadcasted_iota(jnp.int32, shape, axis)


def selector(size, source_of):
    shape = (size, size)
    return (iota(shape, 1) == source_of(iota(shape, 0))).astype(F32).astype(BF16)


def swapped(outer, inner):
    return lambda p: (p % outer) * inner + p // outer


def head_mask(heads, channels, lead):
    width = channels // heads
    shape = (heads, channels)
    mask = (iota(shape, 0) == iota(shape, 1) // width).astype(F32)
    return mask[None] if lead else mask


def kernel_call(body, outs, args, name, flops=0, nbytes=0):
    spec = pl.BlockSpec(memory_space=pltpu.VMEM)
    return pl.pallas_call(
        body,
        out_shape=tuple(jax.ShapeDtypeStruct(s, d) for s, d in outs),
        in_specs=[spec] * len(args),
        out_specs=(spec,) * len(outs),
        compiler_params=pltpu.CompilerParams(vmem_limit_bytes=VMEM_BYTES),
        cost_estimate=pl.CostEstimate(flops=flops, bytes_accessed=nbytes, transcendentals=0),
        name=name,
    )(*args)


def bias_kernel(pair_ref, weight_ref, out_ref):
    rows, columns, channels = pair_ref.shape
    heads = weight_ref.shape[1]
    x = pair_ref[...].reshape(rows * columns, channels).astype(F32)
    normed = normalized(x, -1).astype(BF16)
    bias = lax.dot_general(
        weight_ref[...], normed, (((0,), (1,)), ((), ())), preferred_element_type=F32
    )
    block = jnp.concatenate(
        [bias[:, i * columns : (i + 1) * columns] for i in range(rows)], 0
    ).astype(BF16)
    for d in range(out_ref.shape[0]):
        out_ref[d] = block


def row_scores_kernel(
    ids_ref, mask_ref, state_ref, table_ref, weight_ref,
    scores_ref, value_ref, gate_ref, start_ref,
    *, heads,
):
    sequences, length, channels = state_ref.shape
    tokens = table_ref.shape[0]
    starts = []
    for s in range(sequences):
        hot = (iota((tokens, length), 0) == ids_ref[s : s + 1, :]).astype(F32).astype(BF16)
        starts.append(state_ref[s].astype(F32) + t_dot(hot, table_ref[...]))
    start = jnp.concatenate(starts, 0)
    start_ref[...] = start
    projected = dot(normalized(start, -1).astype(BF16), weight_ref[...])
    query = (projected[:, :channels] * (channels // heads) ** (-0.5)).astype(BF16).astype(F32)
    key = projected[:, channels : 2 * channels].astype(BF16)
    value_ref[...] = projected[:, 2 * channels : 3 * channels].astype(BF16)
    gate_ref[...] = jax.nn.sigmoid(projected[:, 3 * channels :])
    mask = head_mask(heads, channels, True)
    extra = (mask_ref[...].astype(F32) - 1.0) * 10000.0
    for s in range(sequences):
        rows = slice(s * length, (s + 1) * length)
        spread = (query[rows][:, None, :] * mask).reshape(length * heads, channels).astype(BF16)
        scores_ref[s] = dot_t(spread, key[rows]) + extra


def softmax(scores):
    top = jnp.max(scores, -1, keepdims=True)
    e = jnp.exp(scores - top)
    return (e * (1.0 / jnp.sum(e, -1, keepdims=True))).astype(BF16)


def row_mix_kernel(
    scores_ref, bias_ref, value_ref, gate_ref, start_ref, weight_ref, out_ref, *, heads
):
    sequences, expanded, length = scores_ref.shape
    channels = value_ref.shape[1]
    devices = out_ref.shape[0]
    bias = bias_ref[...].reshape(expanded, length).astype(F32)
    mask = head_mask(heads, channels, True)
    shape = (length, expanded)
    gather = (iota(shape, 0) == iota(shape, 1) // heads).astype(F32).astype(BF16)
    mixed = []
    for s in range(sequences):
        rows = slice(s * length, (s + 1) * length)
        weights = softmax(scores_ref[s] + bias)
        whole = dot(weights, value_ref[rows])
        own = (whole.reshape(length, heads, channels) * mask).reshape(expanded, channels)
        mixed.append(dot(gather, own.astype(BF16)))
    mixed = jnp.concatenate(mixed, 0)
    gated = (gate_ref[...] * mixed).astype(BF16)
    after = (start_ref[...] + dot(gated, weight_ref[...])).astype(BF16)
    own_rows = length // devices
    size = sequences * length
    block = sequences * own_rows
    order = selector(
        size, lambda p: (p % block) // own_rows * length + p // block * own_rows + p % own_rows
    )
    out_ref[...] = dot(order, after).astype(BF16).reshape(out_ref.shape)


def column_kernel(
    state_ref, weight_ref, readout_ref, factor_ref, out_ref, left_ref, right_ref, *, heads, own_rows
):
    devices, block, channels = state_ref.shape
    size = devices * block
    sequences = size // own_rows
    to_rows = selector(size, swapped(sequences, own_rows))
    to_sequences = selector(size, swapped(own_rows, sequences))
    start = state_ref[...].reshape(size, channels).astype(F32)
    normed = dot(to_rows, normalized(start, -1).astype(BF16)).astype(BF16)
    projected = dot(normed, weight_ref[...])
    query = (projected[:, :channels] * (channels // heads) ** (-0.5)).astype(BF16).astype(F32)
    key = projected[:, channels : 2 * channels].astype(BF16)
    value = projected[:, 2 * channels : 3 * channels].astype(BF16)
    gate = jax.nn.sigmoid(projected[:, 3 * channels :])
    mask = head_mask(heads, channels, False)
    gated = []
    for r in range(own_rows):
        rows = slice(r * sequences, (r + 1) * sequences)
        spread = jnp.concatenate(
            [(query[rows] * mask[h : h + 1]).astype(BF16) for h in range(heads)], 0
        )
        whole = dot(softmax(dot_t(spread, key[rows])), value[rows])
        mixed = whole[:sequences] * mask[:1]
        for h in range(1, heads):
            mixed += whole[h * sequences : (h + 1) * sequences] * mask[h : h + 1]
        gated.append((gate[rows] * mixed).astype(BF16))
    gated = dot(to_sequences, jnp.concatenate(gated, 0)).astype(BF16)
    after = start + dot(gated, readout_ref[...])
    out_ref[...] = after.astype(BF16).reshape(out_ref.shape)
    normed = dot(to_rows, normalized(after, -1).astype(BF16)).astype(BF16)
    width = factor_ref.shape[1] // 2
    left_ref[...] = dot(normed, factor_ref[:, :width]).astype(BF16)
    fold = max(1, 128 // sequences)
    part = width // fold
    pieces = []
    for r in range(own_rows):
        right = lax.dot_general(
            factor_ref[:, width:],
            normed[r * sequences : (r + 1) * sequences],
            (((0,), (1,)), ((), ())),
            preferred_element_type=F32,
        )
        pieces.append(
            jnp.concatenate([right[f * part : (f + 1) * part] for f in range(fold)], 1)
        )
    pieces = jnp.concatenate(pieces, 0).astype(BF16)
    pieces = dot(selector(own_rows * part, swapped(own_rows, part)), pieces)
    lanes = fold * sequences
    packed = jnp.concatenate(
        [pieces[q * own_rows : (q + 1) * own_rows] for q in range(part)], 1
    ).astype(BF16)
    for d in range(right_ref.shape[0]):
        right_ref[d] = packed


def spread_kernel(left_ref, weight_ref, out_ref, *, own_rows):
    size, width = left_ref.shape
    sequences = size // own_rows
    channels = weight_ref.shape[1] // width
    fold = max(1, 128 // sequences)
    part = width // fold
    product = dot(left_ref[...], weight_ref[...])
    for d in range(width):
        at = (d % part * fold + d // part) * sequences
        for r in range(own_rows):
            out_ref[at : at + sequences, r * channels : (r + 1) * channels] = product[
                r * sequences : (r + 1) * sequences, d * channels : (d + 1) * channels
            ].astype(BF16)


def pair_kernel(
    right_ref, spread_ref, pair_ref, weight_ref, one_ref, normed_ref, out_ref, *, sequences
):
    own_rows, columns, channels = pair_ref.shape
    right = right_ref[...].reshape(columns, right_ref.shape[-1])
    update = dot(right, spread_ref[...]) * (1.0 / sequences)
    ones = [
        pair_ref[i].astype(F32) + update[:, i * channels : (i + 1) * channels]
        for i in range(own_rows)
    ]
    one = jnp.concatenate(ones, 0)
    one_ref[...] = one
    normed = normalized(one, -1).astype(BF16)
    normed_ref[...] = normed
    factors = dot_t(weight_ref[...], normed)
    left = jax.nn.sigmoid(factors[channels : 2 * channels]) * factors[:channels]
    right = jax.nn.sigmoid(factors[3 * channels :]) * factors[2 * channels : 3 * channels]
    both = jnp.concatenate([left.astype(BF16), right.astype(BF16)], 1)
    out_ref[...] = both.reshape(out_ref.shape)


def gate_kernel(normed_ref, weight_ref, out_ref):
    out_ref[...] = jax.nn.sigmoid(dot(normed_ref[...], weight_ref[...]))


def triangle_kernel(both_ref, out_ref, *, own_rows):
    devices, own_channels, lanes = both_ref.shape
    columns = lanes // 2 // own_rows
    size = devices * own_channels
    both = both_ref[...].reshape(size, lanes)
    left = jnp.concatenate([both[:, i * columns : (i + 1) * columns] for i in range(own_rows)], 0)
    right = jnp.concatenate(
        [both[:, (own_rows + i) * columns : (own_rows + i + 1) * columns] for i in range(own_rows)],
        0,
    )
    total = size * own_rows
    order = selector(
        total,
        lambda p: p % own_rows * size + p % columns // own_rows * own_channels + p // columns,
    )
    right = dot(order, right).astype(BF16)
    channel = iota((total, 1), 0) % own_channels
    combined = jnp.zeros((total, columns), F32)
    for c in range(own_channels):
        part = dot_t(left, right[c * columns : (c + 1) * columns])
        combined = jnp.where(channel == c, part, combined)
    combined = combined.astype(BF16)
    out_ref[...] = jnp.concatenate(
        [combined[i * size : (i + 1) * size] for i in range(own_rows)], 1
    ).reshape(out_ref.shape)


def final_kernel(back_ref, one_ref, gate_ref, weight_ref, out_ref):
    channels = weight_ref.shape[0]
    combined = back_ref[...].reshape(channels, back_ref.shape[-1]).astype(F32)
    normed = normalized(combined, 0).astype(BF16)
    update = t_dot(normed, weight_ref[...])
    out_ref[...] = (one_ref[...] + gate_ref[...] * update).astype(BF16).reshape(out_ref.shape)


def exchanged(x):
    return lax.all_to_all(x, "res", split_axis=0, concat_axis=0, tiled=True)


def shards(
    homolog_symbol_ids,
    residue_attend_mask,
    alignment_state,
    pair,
    symbol_lookup_matrix,
    pair_bias_weight,
    row_projection_weight,
    horizontal_readout_matrix,
    column_projection_weight,
    vertical_readout_matrix,
    product_factor_matrices,
    outer_output_weight,
    triangle_input_weight,
    triangle_output_weight,
):
    devices = lax.axis_size("res")
    own_sequences, length, channels = alignment_state.shape
    sequences = own_sequences * devices
    own_rows, columns, pair_channels = pair.shape
    heads = pair_bias_weight.shape[1]
    width = product_factor_matrices.shape[1] // 2
    own_channels = pair_channels // devices
    rows = own_sequences * length

    (bias,) = kernel_call(
        bias_kernel,
        [((devices, own_rows * heads, columns), BF16)],
        (pair, pair_bias_weight),
        "bias",
    )
    bias = exchanged(bias)
    scores, value, gate, start = kernel_call(
        functools.partial(row_scores_kernel, heads=heads),
        [
            ((own_sequences, length * heads, length), F32),
            ((rows, channels), BF16),
            ((rows, channels), F32),
            ((rows, channels), F32),
        ],
        (
            homolog_symbol_ids,
            residue_attend_mask.reshape(1, length),
            alignment_state,
            symbol_lookup_matrix,
            row_projection_weight,
        ),
        "row_scores",
        flops=2 * rows * channels * 4 * channels,
        nbytes=1 << 21,
    )
    (after_rows,) = kernel_call(
        functools.partial(row_mix_kernel, heads=heads),
        [((devices, own_sequences * own_rows, channels), BF16)],
        (scores, bias, value, gate, start, horizontal_readout_matrix),
        "row_mix",
    )
    by_residue = exchanged(after_rows)
    alignment_output, left, right = kernel_call(
        functools.partial(column_kernel, heads=heads, own_rows=own_rows),
        [
            ((sequences, own_rows, channels), BF16),
            ((sequences * own_rows, width), BF16),
            ((devices, own_rows, width * sequences), BF16),
        ],
        (
            by_residue,
            column_projection_weight,
            vertical_readout_matrix,
            product_factor_matrices,
        ),
        "column",
    )
    right = exchanged(right)
    (spread,) = kernel_call(
        functools.partial(spread_kernel, own_rows=own_rows),
        [((width * sequences, own_rows * pair_channels), BF16)],
        (left, outer_output_weight.reshape(width, width * pair_channels)),
        "spread",
        flops=2 * own_rows * sequences * width * width * pair_channels,
        nbytes=1 << 21,
    )
    pair_one, normed, both = kernel_call(
        functools.partial(pair_kernel, sequences=sequences),
        [
            ((own_rows * columns, pair_channels), F32),
            ((own_rows * columns, pair_channels), BF16),
            ((devices, own_channels, 2 * own_rows * columns), BF16),
        ],
        (right, spread, pair, triangle_input_weight[:, : 4 * pair_channels].T),
        "pair",
    )
    both = exchanged(both)
    (gate_out,) = kernel_call(
        gate_kernel,
        [((own_rows * columns, pair_channels), F32)],
        (normed, triangle_input_weight[:, 4 * pair_channels :]),
        "gate",
        flops=2 * own_rows * columns * pair_channels * pair_channels,
        nbytes=1 << 19,
    )
    (combined,) = kernel_call(
        functools.partial(triangle_kernel, own_rows=own_rows),
        [((devices, own_channels, own_rows * columns), BF16)],
        (both,),
        "triangle",
    )
    back = exchanged(combined)
    (pair_output,) = kernel_call(
        final_kernel,
        [((own_rows, columns, pair_channels), BF16)],
        (back, pair_one, gate_out, triangle_output_weight),
        "final",
    )
    return (alignment_output, pair_output)


def solution(mesh):
    placed = (
        P(("crop", "res"), None),
        P("crop"),
        P(("crop", "res"), None, None),
        P(("crop", "res"), None, None),
    ) + (P(),) * 10
    return jax.shard_map(
        shards,
        mesh=mesh,
        in_specs=placed,
        out_specs=(P("crop", "res", None), P(("crop", "res"), None, None)),
        check_vma=False,
    )
```

time: 156 us -> 85.6 us (0.55)
  blocking collectives: 93.2 us -> 13.4 us
  waiting for transfers between devices: 22.7 us -> 36.3 us
  Pallas kernels: 0 us -> 12.2 us
  matrix products: 11 us -> 0 us
  local copies, waits for them, and re-layouts: 17.4 us -> 6.98 us
  starting transfers between devices: 7.73 us -> 15.3 us
  other arithmetic: 2.2 us -> 0 us
    all_gather x2 -> x0, blocking collectives: 83.2 us -> none  [the longest x1 43.9 us: shards(): bias_all = lax.all_gather(bias_local, 'res', axis=1, tiled=True)]
    all_to_all x3 -> x4, waiting for transfers between devices: 22.7 us -> 36.3 us  [exchanged(): return lax.all_to_all(x, 'res', split_axis=0, concat_axis=0, tiled=True)]
    pallas_call x0 -> x9, Pallas kernels: none -> 12.2 us  [kernel_call(): pl.pallas_call(body, out_shape=tuple((jax.ShapeDtypeStruct(s, d) for s, d...]
    dot_general x17 -> x0, matrix products: 10 us -> none  [the longest x2 2.23 us: attention_block_fn(): jnp.einsum('bqc,ce->bqe', gated, out_weight, preferred_element_type=jnp.f...]
    all_to_all x3 -> x4, starting transfers between devices: 7.73 us -> 15.3 us  [exchanged(): return lax.all_to_all(x, 'res', split_axis=0, concat_axis=0, tiled=True)]
    reshape x6 -> x1, local copies, waits for them, and re-layouts: 7.55 us -> 0.12 us  [shards(): outer_output_weight.reshape(width, width * pair_channels)]
    slice x8 -> x3, local copies, waits for them, and re-layouts: 3.84 us -> 0.01 us  [the longest x1 0.01 us: shards(): triangle_input_weight[:, 4 * pair_channels:]]
    unnamed x26 -> x31, local copies, waits for them, and re-layouts: 3.38 us -> 6.85 us
  transfers between devices with their start and end apart: 3 -> 4, of which waited for: 3 -> 4; matrix products, arithmetic and copies ran while one was open for 1% -> 0% of each run, Pallas kernels for 0% -> 2%
where the time goes in v2:
time: 85.6 us; the launch traced here: 85 us
  waiting for transfers between devices  36.3 us (42%)
  starting transfers between devices  15.3 us (18%)
  blocking collectives  13.4 us (16%)
  Pallas kernels  12.2 us (14%)
  local copies, waits for them, and re-layouts  6.98 us (8%)
    all_to_all x4, waiting for transfers between devices, exchanged(): return lax.all_to_all(x, 'res', split_axis=0, concat_axis=0, tiled=True)  36.3 us
    all_to_all x4, starting transfers between devices, exchanged(): return lax.all_to_all(x, 'res', split_axis=0, concat_axis=0, tiled=True)  15.3 us
    all_to_all x1, blocking collectives, exchanged(): return lax.all_to_all(x, 'res', split_axis=0, concat_axis=0, tiled=True)  13.4 us
    pallas_call x9, Pallas kernels, kernel_call(): pl.pallas_call(body, out_shape=tuple((jax.ShapeDtypeStruct(s, d) for s, d...  12.2 us
    unnamed x31, local copies, waits for them, and re-layouts  6.85 us
  transfers between devices with their start and end apart: 4, of which 4 were waited for; matrix products, arithmetic and copies ran while one was open for 0% of the time, Pallas kernels for 2%

profile of v2, /device:TPU:0, one launch (start us, length us, event | category | flops | bytes accessed | tf_op | source)
XLA Modules:
  0.0 85.0 jit_solution(12526963265584002482)
XLA Ops:
  0.6 0.0 copy-start.13
  0.6 0.8 copy.16.weight_ref
  1.4 0.0 copy-start
  1.4 0.9 %copy-done = bf16[4,128,128]{2,1,0:T(8,128)(2,1)S(1)} copy-done((bf16[4,128,128]{2,1,0:T(8,128)(2,1)S(1)}, bf16[4,128,128]{2,1,0:T(8,128)(2,1)}, u32[]{:S(2)}) %copy-start) | copy-done | bytes 131096
  2.4 0.0 copy-start.3
  2.4 0.0 copy-start.6
  2.4 1.1 %bias.1 = bf16[32,32,128]{2,1,0:T(8,128)(2,1)} custom-call(bf16[4,128,128]{2,1,0:T(8,128)(2,1)S(1)} %copy-done, bf16[128,8]{1,0:T(8,128)(2,1)S(1)} %copy.16.weight_ref), custom_call_target="tpu_custom_call" | custom-call | tf_op jit(solution)/shard_map/bias/pallas_call | solution.py:57
  3.4 7.3 %all-to-all-start = ((bf16[32,32,128]{2,1,0:T(8,128)(2,1)}), bf16[32,32,128]{2,1,0:T(8,128)(2,1)S(1)}, u32[]{:S(2)}, u32[]{:S(2)}) async-start(bf16[32,32,128]{2,1,0:T(8,128)(2,1)} %bias.1), calls=%async_computation | async-start | bytes 524288 | tf_op jit(solution)/shard_map/all_to_all | solution.py:276
  10.7 0.0 copy-start.2
  10.7 1.0 %copy-done.2 = bf16[256,1024]{1,0:T(8,128)(2,1)S(1)} copy-done((bf16[256,1024]{1,0:T(8,128)(2,1)S(1)}, bf16[256,1024]{1,0:T(8,128)(2,1)}, u32[]{:S(2)}) %copy-start.2) | copy-done | bytes 524312
  11.8 0.0 copy-start.5
  11.8 0.9 %copy-done.5 = bf16[2,128,256]{2,1,0:T(8,128)(2,1)S(1)} copy-done((bf16[2,128,256]{2,1,0:T(8,128)(2,1)S(1)}, bf16[2,128,256]{2,1,0:T(8,128)(2,1)}, u32[]{:S(2)}) %copy-start.5) | copy-done | bytes 131096
  12.7 0.0 copy-start.8
  12.7 0.7 copy-done.8
  13.4 0.0 copy-start.9
  13.4 0.7 copy-done.9
  14.1 0.0 copy-start.10
  14.1 0.7 copy-done.10
  14.7 1.0 %row_scores.1 = (f32[2,1024,128]{2,1,0:T(8,128)S(1)}, bf16[256,256]{1,0:T(8,128)(2,1)S(1)}, f32[256,256]{1,0:T(8,128)S(1)}, f32[256,256]{1,0:T(8,128)S(1)}) custom-call(s32[2,128]{1,0:T(2,128)S(1)} %copy-done.9, s32[1,128]{1,0:T(1,128)S(1)} %bitcast.3, bf16[2,128,256]{2,1,0:T(8,128)(2,1)S(1)} %copy-done.5, bf16[23,256]{1,0:T(8,128)(2,1)S(1)} %copy-done.8, ...), custom_call_target="tpu_custom_call" | custom-call | flops 134217728 | bytes 2097152 | tf_op jit(solution)/shard_map/row_scores/pallas_call | solution.py:57
  15.7 5.6 %all-to-all-done.bias_ref = bf16[32,32,128]{2,1,0:T(8,128)(2,1)S(1)} async-done(((bf16[32,32,128]{2,1,0:T(8,128)(2,1)}), bf16[32,32,128]{2,1,0:T(8,128)(2,1)S(1)}, u32[]{:S(2)}, u32[]{:S(2)}) %all-to-all-start) | async-done | bytes 262176 | tf_op jit(solution)/shard_map/all_to_all | solution.py:276
  21.3 0.0 copy-start.4
  21.3 0.9 %copy-done.4 = bf16[256,256]{1,0:T(8,128)(2,1)S(1)} copy-done((bf16[256,256]{1,0:T(8,128)(2,1)S(1)}, bf16[256,256]{1,0:T(8,128)(2,1)}, u32[]{:S(2)}) %copy-start.4) | copy-done | bytes 131096
  22.2 2.5 %row_mix.1 = bf16[32,8,256]{2,1,0:T(8,128)(2,1)} custom-call(f32[2,1024,128]{2,1,0:T(8,128)S(1)} %get-tuple-element.12.scores_ref, bf16[32,32,128]{2,1,0:T(8,128)(2,1)S(1)} %all-to-all-done.bias_ref, bf16[256,256]{1,0:T(8,128)(2,1)S(1)} %get-tuple-element.13.value_ref, f32[256,256]{1,0:T(8,128)S(1)} %get-tuple-element.14.gate_ref, ...), custom_call_target="tpu_custom_call" | custom-call | tf_op jit(solution)/shard_map/row_mix/pallas_call | solution.py:57
  24.7 2.7 %all-to-all-start.1 = ((bf16[32,8,256]{2,1,0:T(8,128)(2,1)}), bf16[32,8,256]{2,1,0:T(8,128)(2,1)S(1)}, u32[]{:S(2)}, u32[]{:S(2)}) async-start(bf16[32,8,256]{2,1,0:T(8,128)(2,1)} %row_mix.1), calls=%async_computation.1 | async-start | bytes 262144 | tf_op jit(solution)/shard_map/all_to_all | solution.py:276
  27.4 0.0 copy-done.13
  27.4 0.1 copy.17.factor_ref
  27.5 8.1 %all-to-all-done.1.state_ref = bf16[32,8,256]{2,1,0:T(8,128)(2,1)S(1)} async-done(((bf16[32,8,256]{2,1,0:T(8,128)(2,1)}), bf16[32,8,256]{2,1,0:T(8,128)(2,1)S(1)}, u32[]{:S(2)}, u32[]{:S(2)}) %all-to-all-start.1) | async-done | bytes 131104 | tf_op jit(solution)/shard_map/all_to_all | solution.py:276
  35.6 0.0 copy-done.3
  35.6 0.0 copy-done.6
  35.6 3.6 %column.1 = (bf16[64,4,256]{2,1,0:T(4,128)(2,1)}, bf16[256,32]{1,0:T(8,128)(2,1)S(1)}, bf16[32,4,2048]{2,1,0:T(4,128)(2,1)}) custom-call(bf16[32,8,256]{2,1,0:T(8,128)(2,1)S(1)} %all-to-all-done.1.state_ref, bf16[256,1024]{1,0:T(8,128)(2,1)S(1)} %copy-done.3, bf16[256,256]{1,0:T(8,128)(2,1)S(1)} %copy-done.6, bf16[256,64]{1,0:T(8,128)(2,1)S(1)} %copy.17.factor_ref), custom_call_target="tpu_custom_call" | custom-call | tf_op jit(solution)/shard_map/column/pallas_call | solution.py:57
  39.3 2.7 %all-to-all-start.2 = ((bf16[32,4,2048]{2,1,0:T(4,128)(2,1)}), bf16[32,4,2048]{2,1,0:T(4,128)(2,1)S(1)}, u32[]{:S(2)}, u32[]{:S(2)}) async-start(bf16[32,4,2048]{2,1,0:T(4,128)(2,1)} %get-tuple-element.17), calls=%async_computation.2 | async-start | bytes 1048576 | tf_op jit(solution)/shard_map/all_to_all | solution.py:276
  42.0 0.0 copy-done.12
  42.0 0.1 reshape.11.weight_ref
  42.1 0.0 slice-done
  42.2 0.1 copy.19
  42.3 0.7 spread.1.spread_ref
  43.0 0.0 copy-start.11
  43.0 14.6 %all-to-all-done.2.right_ref = bf16[32,4,2048]{2,1,0:T(4,128)(2,1)S(1)} async-done(((bf16[32,4,2048]{2,1,0:T(4,128)(2,1)}), bf16[32,4,2048]{2,1,0:T(4,128)(2,1)S(1)}, u32[]{:S(2)}, u32[]{:S(2)}) %all-to-all-start.2) | async-done | bytes 524320 | tf_op jit(solution)/shard_map/all_to_all | solution.py:276
  57.6 0.0 copy-done.1
  57.6 0.9 %pair.1 = (f32[512,128]{1,0:T(8,128)S(1)}, bf16[512,128]{1,0:T(8,128)(2,1)S(1)}, bf16[32,4,1024]{2,1,0:T(4,128)(2,1)S(1)}) custom-call(bf16[32,4,2048]{2,1,0:T(4,128)(2,1)S(1)} %all-to-all-done.2.right_ref, bf16[2048,512]{1,0:T(8,128)(2,1)S(1)} %spread.1.spread_ref, bf16[4,128,128]{2,1,0:T(8,128)(2,1)S(1)} %copy-done.1, bf16[512,128]{1,0:T(8,128)(2,1)S(1)} %bitcast.2), custom_call_target="tpu_custom_call" | custom-call | tf_op jit(solution)/shard_map/pair/pallas_call | solution.py:57
  58.5 13.4 %all_to_all.25.both_ref = bf16[32,4,1024]{2,1,0:T(4,128)(2,1)S(1)} all-to-all(bf16[32,4,1024]{2,1,0:T(4,128)(2,1)S(1)} %get-tuple-element.19), channel_id=1, replica_groups=mesh['crop'=1,'res'=32] {'res'}, dimensions={0} | all-to-all | bytes 524288 | tf_op jit(solution)/shard_map/all_to_all | solution.py:276
  71.9 1.4 %triangle.1 = bf16[32,4,512]{2,1,0:T(4,128)(2,1)} custom-call(bf16[32,4,1024]{2,1,0:T(4,128)(2,1)S(1)} %all_to_all.25.both_ref), custom_call_target="tpu_custom_call" | custom-call | tf_op jit(solution)/shard_map/triangle/pallas_call | solution.py:57
  73.2 2.6 %all-to-all-start.4 = ((bf16[32,4,512]{2,1,0:T(4,128)(2,1)}), bf16[32,4,512]{2,1,0:T(4,128)(2,1)S(1)}, u32[]{:S(2)}, u32[]{:S(2)}) async-start(bf16[32,4,512]{2,1,0:T(4,128)(2,1)} %triangle.1), calls=%async_computation.4 | async-start | bytes 262144 | tf_op jit(solution)/shard_map/all_to_all | solution.py:276
  75.8 0.0 copy-done.11
  75.9 0.2 gate.1.gate_ref
  76.0 8.0 %all-to-all-done.4.back_ref = bf16[32,4,512]{2,1,0:T(4,128)(2,1)S(1)} async-done(((bf16[32,4,512]{2,1,0:T(4,128)(2,1)}), bf16[32,4,512]{2,1,0:T(4,128)(2,1)S(1)}, u32[]{:S(2)}, u32[]{:S(2)}) %all-to-all-start.4) | async-done | bytes 131104 | tf_op jit(solution)/shard_map/all_to_all | solution.py:276
  84.1 0.0 copy-done.7
  84.1 1.0 %final.1 = bf16[4,128,128]{2,1,0:T(8,128)(2,1)} custom-call(bf16[32,4,512]{2,1,0:T(4,128)(2,1)S(1)} %all-to-all-done.4.back_ref, f32[512,128]{1,0:T(8,128)S(1)} %get-tuple-element.20.one_ref, f32[512,128]{1,0:T(8,128)S(1)} %gate.1.gate_ref, bf16[128,128]{1,0:T(8,128)(2,1)S(1)} %copy-done.7), custom_call_target="tpu_custom_call" | custom-call | tf_op jit(solution)/shard_map/final/pallas_call | solution.py:57
  (5 shorter events, 0.0 us)
Async XLA Ops:
  0.6 26.8 %copy-start.13 = (bf16[256,64]{0,1:T(8,128)(2,1)S(1)}, bf16[256,64]{0,1:T(8,128)(2,1)}, u32[]{:S(2)}) copy-start(bf16[256,64]{0,1:T(8,128)(2,1)} %param.24) | copy-start | bytes 98308
  1.4 0.9 %copy-start = (bf16[4,128,128]{2,1,0:T(8,128)(2,1)S(1)}, bf16[4,128,128]{2,1,0:T(8,128)(2,1)}, u32[]{:S(2)}) copy-start(bf16[4,128,128]{2,1,0:T(8,128)(2,1)} %pair_ref.3) | copy-start | bytes 393220
  2.4 33.3 %copy-start.3 = (bf16[256,1024]{1,0:T(8,128)(2,1)S(1)}, bf16[256,1024]{1,0:T(8,128)(2,1)}, u32[]{:S(2)}) copy-start(bf16[256,1024]{1,0:T(8,128)(2,1)} %weight_ref.7) | copy-start | bytes 1572868
  2.4 33.3 %copy-start.6 = (bf16[256,256]{1,0:T(8,128)(2,1)S(1)}, bf16[256,256]{1,0:T(8,128)(2,1)}, u32[]{:S(2)}) copy-start(bf16[256,256]{1,0:T(8,128)(2,1)} %readout_ref.1) | copy-start | bytes 393220
  3.4 17.9 %all-to-all-start = ((bf16[32,32,128]{2,1,0:T(8,128)(2,1)}), bf16[32,32,128]{2,1,0:T(8,128)(2,1)S(1)}, u32[]{:S(2)}, u32[]{:S(2)}) async-start(bf16[32,32,128]{2,1,0:T(8,128)(2,1)} %bias.1), calls=%async_computation | async-start | bytes 524288 | tf_op jit(solution)/shard_map/all_to_all | solution.py:276
  10.7 1.0 %copy-start.2 = (bf16[256,1024]{1,0:T(8,128)(2,1)S(1)}, bf16[256,1024]{1,0:T(8,128)(2,1)}, u32[]{:S(2)}) copy-start(bf16[256,1024]{1,0:T(8,128)(2,1)} %weight_ref.5) | copy-start | bytes 1572868
  11.8 0.9 %copy-start.5 = (bf16[2,128,256]{2,1,0:T(8,128)(2,1)S(1)}, bf16[2,128,256]{2,1,0:T(8,128)(2,1)}, u32[]{:S(2)}) copy-start(bf16[2,128,256]{2,1,0:T(8,128)(2,1)} %state_ref.1) | copy-start | bytes 393220
  12.7 0.7 copy-start.8
  13.4 0.7 copy-start.9
  14.1 0.7 copy-start.10
  21.3 0.9 %copy-start.4 = (bf16[256,256]{1,0:T(8,128)(2,1)S(1)}, bf16[256,256]{1,0:T(8,128)(2,1)}, u32[]{:S(2)}) copy-start(bf16[256,256]{1,0:T(8,128)(2,1)} %weight_ref.6) | copy-start | bytes 393220
  22.2 19.9 %slice-start = ((bf16[128,640]{1,0:T(8,128)(2,1)}), bf16[128,512]{1,0:T(8,128)(2,1)S(1)}, s32[]{:S(2)}) async-start(bf16[128,640]{1,0:T(8,128)(2,1)} %param.26), calls=%async_computation.5 | async-start | bytes 262144 | tf_op jit(solution)/shard_map/slice | solution.py:368
  24.7 17.3 %copy-start.12 = (bf16[1024,128]{1,0:T(8,128)(2,1)S(1)}, bf16[1024,128]{1,0:T(8,128)(2,1)}, u32[]{:S(2)}) copy-start(bf16[1024,128]{1,0:T(8,128)(2,1)} %param.25) | copy-start | bytes 786436
  24.7 10.9 %all-to-all-start.1 = ((bf16[32,8,256]{2,1,0:T(8,128)(2,1)}), bf16[32,8,256]{2,1,0:T(8,128)(2,1)S(1)}, u32[]{:S(2)}, u32[]{:S(2)}) async-start(bf16[32,8,256]{2,1,0:T(8,128)(2,1)} %row_mix.1), calls=%async_computation.1 | async-start | bytes 262144 | tf_op jit(solution)/shard_map/all_to_all | solution.py:276
  39.3 18.3 %copy-start.1 = (bf16[4,128,128]{2,1,0:T(8,128)(2,1)S(1)}, bf16[4,128,128]{2,1,0:T(8,128)(2,1)}, u32[]{:S(2)}) copy-start(bf16[4,128,128]{2,1,0:T(8,128)(2,1)} %pair_ref.3) | copy-start | bytes 393220
  39.3 18.3 %all-to-all-start.2 = ((bf16[32,4,2048]{2,1,0:T(4,128)(2,1)}), bf16[32,4,2048]{2,1,0:T(4,128)(2,1)S(1)}, u32[]{:S(2)}, u32[]{:S(2)}) async-start(bf16[32,4,2048]{2,1,0:T(4,128)(2,1)} %get-tuple-element.17), calls=%async_computation.2 | async-start | bytes 1048576 | tf_op jit(solution)/shard_map/all_to_all | solution.py:276
  43.0 32.9 %copy-start.11 = (bf16[128,640]{1,0:T(8,128)(2,1)S(1)}, bf16[128,640]{1,0:T(8,128)(2,1)}, u32[]{:S(2)}) copy-start(bf16[128,640]{1,0:T(8,128)(2,1)} %param.26) | copy-start | bytes 491524
  57.6 26.5 %copy-start.7 = (bf16[128,128]{1,0:T(8,128)(2,1)S(1)}, bf16[128,128]{1,0:T(8,128)(2,1)}, u32[]{:S(2)}) copy-start(bf16[128,128]{1,0:T(8,128)(2,1)} %weight_ref.8) | copy-start | bytes 98308
  73.2 10.8 %all-to-all-start.4 = ((bf16[32,4,512]{2,1,0:T(4,128)(2,1)}), bf16[32,4,512]{2,1,0:T(4,128)(2,1)S(1)}, u32[]{:S(2)}, u32[]{:S(2)}) async-start(bf16[32,4,512]{2,1,0:T(4,128)(2,1)} %triangle.1), calls=%async_computation.4 | async-start | bytes 262144 | tf_op jit(solution)/shard_map/all_to_all | solution.py:276

commit v3 on v2

--- a/solution.py
+++ b/solution.py
@@ -52,12 +52,13 @@
     return mask[None] if lead else mask
 
 
-def kernel_call(body, outs, args, name, flops=0, nbytes=0):
+def kernel_call(body, outs, args, name, flops=0, nbytes=0, scalars=0):
     spec = pl.BlockSpec(memory_space=pltpu.VMEM)
+    scalar = pl.BlockSpec(memory_space=pltpu.SMEM)
     return pl.pallas_call(
         body,
         out_shape=tuple(jax.ShapeDtypeStruct(s, d) for s, d in outs),
-        in_specs=[spec] * len(args),
+        in_specs=[scalar] * scalars + [spec] * (len(args) - scalars),
         out_specs=(spec,) * len(outs),
         compiler_params=pltpu.CompilerParams(vmem_limit_bytes=VMEM_BYTES),
         cost_estimate=pl.CostEstimate(flops=flops, bytes_accessed=nbytes, transcendentals=0),
@@ -65,14 +66,18 @@
     )(*args)
 
 
-def bias_kernel(pair_ref, weight_ref, out_ref):
-    rows, columns, channels = pair_ref.shape
-    heads = weight_ref.shape[1]
+def bias_kernel(pair_hbm, weight_hbm, out_ref, pair_ref, weight_ref, sems):
+    rows = pair_ref.shape[0]
+    copies = [pltpu.make_async_copy(weight_hbm, weight_ref, sems.at[rows])] + [
+        pltpu.make_async_copy(pair_hbm.at[i], pair_ref.at[i], sems.at[i]) for i in range(rows)
+    ]
+    for copy in copies:
+        copy.start()
+    for copy in copies:
+        copy.wait()
+    _, columns, channels = pair_ref.shape
     x = pair_ref[...].reshape(rows * columns, channels).astype(F32)
-    normed = normalized(x, -1).astype(BF16)
-    bias = lax.dot_general(
-        weight_ref[...], normed, (((0,), (1,)), ((), ())), preferred_element_type=F32
-    )
+    bias = dot_t(weight_ref[...], normalized(x, -1).astype(BF16))
     block = jnp.concatenate(
         [bias[:, i * columns : (i + 1) * columns] for i in range(rows)], 0
     ).astype(BF16)
@@ -81,12 +86,13 @@
 
 
 def row_scores_kernel(
-    ids_ref, mask_ref, state_ref, table_ref, weight_ref,
-    scores_ref, value_ref, gate_ref, start_ref,
+    ids_ref, mask_ref, state_ref, table_ref, weight_ref, readout_ref,
+    scores_ref, value_ref, gate_ref, start_ref, held_ref,
     *, heads,
 ):
     sequences, length, channels = state_ref.shape
     tokens = table_ref.shape[0]
+    held_ref[...] = readout_ref[...]
     starts = []
     for s in range(sequences):
         hot = (iota((tokens, length), 0) == ids_ref[s : s + 1, :]).astype(F32).astype(BF16)
@@ -172,24 +178,18 @@
     after = start + dot(gated, readout_ref[...])
     out_ref[...] = after.astype(BF16).reshape(out_ref.shape)
     normed = dot(to_rows, normalized(after, -1).astype(BF16)).astype(BF16)
-    width = factor_ref.shape[1] // 2
-    left_ref[...] = dot(normed, factor_ref[:, :width]).astype(BF16)
+    width = factor_ref.shape[0] // 2
+    left_ref[...] = dot_t(normed, factor_ref[:width]).astype(BF16)
     fold = max(1, 128 // sequences)
     part = width // fold
     pieces = []
     for r in range(own_rows):
-        right = lax.dot_general(
-            factor_ref[:, width:],
-            normed[r * sequences : (r + 1) * sequences],
-            (((0,), (1,)), ((), ())),
-            preferred_element_type=F32,
-        )
+        right = dot_t(factor_ref[width:], normed[r * sequences : (r + 1) * sequences])
         pieces.append(
             jnp.concatenate([right[f * part : (f + 1) * part] for f in range(fold)], 1)
         )
     pieces = jnp.concatenate(pieces, 0).astype(BF16)
     pieces = dot(selector(own_rows * part, swapped(own_rows, part)), pieces)
-    lanes = fold * sequences
     packed = jnp.concatenate(
         [pieces[q * own_rows : (q + 1) * own_rows] for q in range(part)], 1
     ).astype(BF16)
@@ -213,10 +213,15 @@
 
 
 def pair_kernel(
-    right_ref, spread_ref, pair_ref, weight_ref, one_ref, normed_ref, out_ref, *, sequences
+    second_ref, right_ref, other_ref, spread_ref, pair_ref, weight_ref, gate_weight_ref,
+    one_ref, gate_ref, out_ref,
+    *, sequences,
 ):
     own_rows, columns, channels = pair_ref.shape
-    right = right_ref[...].reshape(columns, right_ref.shape[-1])
+    flip = jnp.full(right_ref.shape, second_ref[0], jnp.int32) == 1
+    mine, other = right_ref[...].astype(F32), other_ref[...].astype(F32)
+    right = jnp.concatenate([jnp.where(flip, other, mine), jnp.where(flip, mine, other)], 1)
+    right = right.reshape(columns, right_ref.shape[-1]).astype(BF16)
     update = dot(right, spread_ref[...]) * (1.0 / sequences)
     ones = [
         pair_ref[i].astype(F32) + update[:, i * channels : (i + 1) * channels]
@@ -225,16 +230,12 @@
     one = jnp.concatenate(ones, 0)
     one_ref[...] = one
     normed = normalized(one, -1).astype(BF16)
-    normed_ref[...] = normed
+    gate_ref[...] = jax.nn.sigmoid(dot(normed, gate_weight_ref[...]))
     factors = dot_t(weight_ref[...], normed)
     left = jax.nn.sigmoid(factors[channels : 2 * channels]) * factors[:channels]
     right = jax.nn.sigmoid(factors[3 * channels :]) * factors[2 * channels : 3 * channels]
     both = jnp.concatenate([left.astype(BF16), right.astype(BF16)], 1)
     out_ref[...] = both.reshape(out_ref.shape)
-
-
-def gate_kernel(normed_ref, weight_ref, out_ref):
-    out_ref[...] = jax.nn.sigmoid(dot(normed_ref[...], weight_ref[...]))
 
 
 def triangle_kernel(both_ref, out_ref, *, own_rows):
@@ -301,20 +302,28 @@
     own_channels = pair_channels // devices
     rows = own_sequences * length
 
-    (bias,) = kernel_call(
+    outside = pl.BlockSpec(memory_space=pl.ANY)
+    bias = pl.pallas_call(
         bias_kernel,
-        [((devices, own_rows * heads, columns), BF16)],
-        (pair, pair_bias_weight),
-        "bias",
-    )
+        out_shape=jax.ShapeDtypeStruct((devices, own_rows * heads, columns), BF16),
+        in_specs=[outside, outside],
+        out_specs=pl.BlockSpec(memory_space=pltpu.VMEM),
+        scratch_shapes=[
+            pltpu.VMEM(pair.shape, BF16),
+            pltpu.VMEM(pair_bias_weight.shape[::-1], BF16),
+            pltpu.SemaphoreType.DMA((own_rows + 1,)),
+        ],
+        name="bias",
+    )(pair, pair_bias_weight.T)
     bias = exchanged(bias)
-    scores, value, gate, start = kernel_call(
+    scores, value, gate, start, readout = kernel_call(
         functools.partial(row_scores_kernel, heads=heads),
         [
             ((own_sequences, length * heads, length), F32),
             ((rows, channels), BF16),
             ((rows, channels), F32),
             ((rows, channels), F32),
+            ((channels, channels), BF16),
         ],
         (
             homolog_symbol_ids,
@@ -322,6 +331,7 @@
             alignment_state,
             symbol_lookup_matrix,
             row_projection_weight,
+            horizontal_readout_matrix,
         ),
         "row_scores",
         flops=2 * rows * channels * 4 * channels,
@@ -330,7 +340,7 @@
     (after_rows,) = kernel_call(
         functools.partial(row_mix_kernel, heads=heads),
         [((devices, own_sequences * own_rows, channels), BF16)],
-        (scores, bias, value, gate, start, horizontal_readout_matrix),
+        (scores, bias, value, gate, start, readout),
         "row_mix",
     )
     by_residue = exchanged(after_rows)
@@ -339,17 +349,20 @@
         [
             ((sequences, own_rows, channels), BF16),
             ((sequences * own_rows, width), BF16),
-            ((devices, own_rows, width * sequences), BF16),
+            ((devices // 2, own_rows, width * sequences), BF16),
         ],
         (
             by_residue,
             column_projection_weight,
             vertical_readout_matrix,
-            product_factor_matrices,
+            product_factor_matrices.T,
         ),
         "column",
     )
-    right = exchanged(right)
+    groups = [list(range(first, devices, 2)) for first in range(2)]
+    right = lax.all_to_all(right, "res", 0, 0, axis_index_groups=groups, tiled=True)
+    other = lax.ppermute(right, "res", [(i, i ^ 1) for i in range(devices)])
+    second = (lax.axis_index("res") % 2).reshape(1)
     (spread,) = kernel_call(
         functools.partial(spread_kernel, own_rows=own_rows),
         [((width * sequences, own_rows * pair_channels), BF16)],
@@ -358,25 +371,26 @@
         flops=2 * own_rows * sequences * width * width * pair_channels,
         nbytes=1 << 21,
     )
-    pair_one, normed, both = kernel_call(
+    pair_one, gate_out, both = kernel_call(
         functools.partial(pair_kernel, sequences=sequences),
         [
             ((own_rows * columns, pair_channels), F32),
-            ((own_rows * columns, pair_channels), BF16),
+            ((own_rows * columns, pair_channels), F32),
             ((devices, own_channels, 2 * own_rows * columns), BF16),
         ],
-        (right, spread, pair, triangle_input_weight[:, : 4 * pair_channels].T),
+        (
+            second,
+            right,
+            other,
+            spread,
+            pair,
+            triangle_input_weight[:, : 4 * pair_channels].T,
+            triangle_input_weight[:, 4 * pair_channels :],
+        ),
         "pair",
+        scalars=1,
     )
     both = exchanged(both)
-    (gate_out,) = kernel_call(
-        gate_kernel,
-        [((own_rows * columns, pair_channels), F32)],
-        (normed, triangle_input_weight[:, 4 * pair_channels :]),
-        "gate",
-        flops=2 * own_rows * columns * pair_channels * pair_channels,
-        nbytes=1 << 19,
-    )
     (combined,) = kernel_call(
         functools.partial(triangle_kernel, own_rows=own_rows),
         [((devices, own_channels, own_rows * columns), BF16)],

time: 85.6 us -> 77.2 us (0.902)
  blocking collectives: 13.4 us -> 47 us
  waiting for transfers between devices: 36.3 us -> 5.26 us
  starting transfers between devices: 15.3 us -> 7.31 us
  local copies, waits for them, and re-layouts: 6.98 us -> 5.16 us
  Pallas kernels: 12.2 us -> 11.3 us
    all_to_all x4 -> x1, waiting for transfers between devices: 36.3 us -> 4.7 us  [exchanged(): return lax.all_to_all(x, 'res', split_axis=0, concat_axis=0, tiled=True)]
    all_to_all x1 -> x3, blocking collectives: 13.4 us -> 33.8 us  [exchanged(): return lax.all_to_all(x, 'res', split_axis=0, concat_axis=0, tiled=True)]
    all_to_all x0 -> x1, blocking collectives: none -> 13.2 us  [shards(): lax.all_to_all(right, 'res', 0, 0, axis_index_groups=groups, tiled=True)]
    all_to_all x4 -> x1, starting transfers between devices: 15.3 us -> 7.3 us  [exchanged(): return lax.all_to_all(x, 'res', split_axis=0, concat_axis=0, tiled=True)]
    pallas_call x9 -> x7, Pallas kernels: 12.2 us -> 9.29 us  [kernel_call(): pl.pallas_call(body, out_shape=tuple((jax.ShapeDtypeStruct(s, d) for s, d...]
    pallas_call x0 -> x1, Pallas kernels: none -> 1.99 us  [shards(): pl.pallas_call(bias_kernel, out_shape=jax.ShapeDtypeStruct((devices, own_...]
    unnamed x31 -> x27, local copies, waits for them, and re-layouts: 6.85 us -> 5.03 us
  transfers between devices with their start and end apart: 4 -> 2, of which waited for: 4 -> 2; matrix products, arithmetic and copies ran while one was open for 0% -> 0% of each run, Pallas kernels for 2% -> 2%
where the time goes in v3:
time: 77.2 us; the launch traced here: 76.8 us
  blocking collectives  47 us (61%)
  Pallas kernels  11.3 us (15%)
  starting transfers between devices  7.31 us (9%)
  waiting for transfers between devices  5.26 us (7%)
  local copies, waits for them, and re-layouts  5.16 us (7%)
  between operations  0.78 us (1%)
    all_to_all x3, blocking collectives, exchanged(): return lax.all_to_all(x, 'res', split_axis=0, concat_axis=0, tiled=True)  33.8 us
    all_to_all x1, blocking collectives, shards(): lax.all_to_all(right, 'res', 0, 0, axis_index_groups=groups, tiled=True)  13.2 us
    pallas_call x7, Pallas kernels, kernel_call(): pl.pallas_call(body, out_shape=tuple((jax.ShapeDtypeStruct(s, d) for s, d...  9.29 us
    all_to_all x1, starting transfers between devices, exchanged(): return lax.all_to_all(x, 'res', split_axis=0, concat_axis=0, tiled=True)  7.3 us
    unnamed x27, local copies, waits for them, and re-layouts  5.03 us
    all_to_all x1, waiting for transfers between devices, exchanged(): return lax.all_to_all(x, 'res', split_axis=0, concat_axis=0, tiled=True)  4.7 us
    pallas_call x1, Pallas kernels, shards(): pl.pallas_call(bias_kernel, out_shape=jax.ShapeDtypeStruct((devices, own_...  1.99 us
  transfers between devices with their start and end apart: 2, of which 2 were waited for; matrix products, arithmetic and copies ran while one was open for 0% of the time, Pallas kernels for 2%

profile of v3, /device:TPU:0, one launch (start us, length us, event | category | flops | bytes accessed | tf_op | source)
XLA Modules:
  0.0 76.8 jit_solution(6725922457043699446)
XLA Ops:
  0.6 0.0 copy-start.2
  0.6 0.0 copy-start.3
  0.7 0.0 copy-start.6
  0.7 2.0 %bias.1 = bf16[32,32,128]{2,1,0:T(8,128)(2,1)} custom-call(bf16[4,128,128]{2,1,0:T(8,128)(2,1)} %pair_ref.1, bf16[8,128]{1,0:T(8,128)(2,1)} %bitcast.8), custom_call_target="tpu_custom_call" | custom-call | tf_op jit(solution)/shard_map/bias/pallas_call | solution.py:306
  2.7 7.3 %all-to-all-start = ((bf16[32,32,128]{2,1,0:T(8,128)(2,1)}), bf16[32,32,128]{2,1,0:T(8,128)(2,1)S(1)}, u32[]{:S(2)}, u32[]{:S(2)}) async-start(bf16[32,32,128]{2,1,0:T(8,128)(2,1)} %bias.1), calls=%async_computation | async-start | bytes 524288 | tf_op jit(solution)/shard_map/all_to_all | solution.py:277
  10.0 0.0 copy-start.1
  10.0 1.0 %copy-done.1 = bf16[256,1024]{1,0:T(8,128)(2,1)S(1)} copy-done((bf16[256,1024]{1,0:T(8,128)(2,1)S(1)}, bf16[256,1024]{1,0:T(8,128)(2,1)}, u32[]{:S(2)}) %copy-start.1) | copy-done | bytes 524312
  11.0 0.0 copy-start.4
  11.0 0.9 %copy-done.4 = bf16[2,128,256]{2,1,0:T(8,128)(2,1)S(1)} copy-done((bf16[2,128,256]{2,1,0:T(8,128)(2,1)S(1)}, bf16[2,128,256]{2,1,0:T(8,128)(2,1)}, u32[]{:S(2)}) %copy-start.4) | copy-done | bytes 131096
  11.9 0.0 copy-start.5
  11.9 0.9 %copy-done.5 = bf16[256,256]{1,0:T(8,128)(2,1)S(1)} copy-done((bf16[256,256]{1,0:T(8,128)(2,1)S(1)}, bf16[256,256]{1,0:T(8,128)(2,1)}, u32[]{:S(2)}) %copy-start.5) | copy-done | bytes 131096
  12.8 0.0 copy-start.8
  12.8 0.7 copy-done.8
  13.5 0.0 copy-start.9
  13.5 0.7 copy-done.9
  14.2 0.0 copy-start.10
  14.2 0.7 copy-done.10
  14.9 1.0 %row_scores.1 = (f32[2,1024,128]{2,1,0:T(8,128)S(1)}, bf16[256,256]{1,0:T(8,128)(2,1)S(1)}, f32[256,256]{1,0:T(8,128)S(1)}, f32[256,256]{1,0:T(8,128)S(1)}, bf16[256,256]{1,0:T(8,128)(2,1)S(1)}) custom-call(s32[2,128]{1,0:T(2,128)S(1)} %copy-done.9, s32[1,128]{1,0:T(1,128)S(1)} %bitcast.7, bf16[2,128,256]{2,1,0:T(8,128)(2,1)S(1)} %copy-done.4, ...), custom_call_target="tpu_custom_call" | custom-call | flops 134217728 | bytes 2097152 | tf_op jit(solution)/shard_map/row_scores/pallas_call | solution.py:58
  15.9 0.0 copy-start.11
  15.9 4.7 %all-to-all-done.bias_ref = bf16[32,32,128]{2,1,0:T(8,128)(2,1)S(1)} async-done(((bf16[32,32,128]{2,1,0:T(8,128)(2,1)}), bf16[32,32,128]{2,1,0:T(8,128)(2,1)S(1)}, u32[]{:S(2)}, u32[]{:S(2)}) %all-to-all-start) | async-done | bytes 262176 | tf_op jit(solution)/shard_map/all_to_all | solution.py:277
  20.6 0.0 slice-start
  20.6 0.0 copy-start.12
  20.6 1.8 %row_mix.1 = bf16[32,8,256]{2,1,0:T(8,128)(2,1)S(1)} custom-call(f32[2,1024,128]{2,1,0:T(8,128)S(1)} %get-tuple-element.13.scores_ref, bf16[32,32,128]{2,1,0:T(8,128)(2,1)S(1)} %all-to-all-done.bias_ref, bf16[256,256]{1,0:T(8,128)(2,1)S(1)} %get-tuple-element.14.value_ref, f32[256,256]{1,0:T(8,128)S(1)} %get-tuple-element.15.gate_ref, ...), custom_call_target="tpu_custom_call" | custom-call | tf_op jit(solution)/shard_map/row_mix/pallas_call | solution.py:58
  22.4 10.4 %all_to_all.25.state_ref = bf16[32,8,256]{2,1,0:T(8,128)(2,1)S(1)} all-to-all(bf16[32,8,256]{2,1,0:T(8,128)(2,1)S(1)} %row_mix.1), channel_id=1, replica_groups=mesh['crop'=1,'res'=32] {'res'}, dimensions={0} | all-to-all | bytes 262144 | tf_op jit(solution)/shard_map/all_to_all | solution.py:277
  32.8 0.0 copy-done.2
  32.8 0.0 copy-done.3
  32.8 0.0 copy-done.6
  32.8 3.2 %column.1 = (bf16[64,4,256]{2,1,0:T(4,128)(2,1)}, bf16[256,32]{1,0:T(8,128)(2,1)S(1)}, bf16[16,4,2048]{2,1,0:T(4,128)(2,1)S(1)}) custom-call(bf16[32,8,256]{2,1,0:T(8,128)(2,1)S(1)} %all_to_all.25.state_ref, bf16[256,1024]{1,0:T(8,128)(2,1)S(1)} %copy-done.2, bf16[256,256]{1,0:T(8,128)(2,1)S(1)} %copy-done.3, bf16[64,256]{1,0:T(8,128)(2,1)S(1)} %bitcast.6), custom_call_target="tpu_custom_call" | custom-call | tf_op jit(solution)/shard_map/column/pallas_call | solution.py:58
  36.1 0.0 copy-start
  36.1 13.2 %all_to_all.26.right_ref = bf16[16,4,2048]{2,1,0:T(4,128)(2,1)S(1)} all-to-all(bf16[16,4,2048]{2,1,0:T(4,128)(2,1)S(1)} %get-tuple-element.19), channel_id=1, replica_groups={{0,2,4,6,8,10,12,14,16,18,20,22,24,26,28,30},{1,3,5,7,9,11,13,15,17,19,..., dimensions={0} | all-to-all | bytes 524288 | tf_op jit(solution)/shard_map/all_to_all | solution.py:363
  49.3 0.0 collective-permute-start
  49.3 0.0 copy-done.11
  49.3 0.0 slice-done
  49.3 0.1 copy.17
  49.4 0.0 copy-done.12
  49.4 0.1 reshape.15.weight_ref
  49.6 0.7 spread.1.spread_ref
  50.3 0.0 copy-start.7
  50.3 0.6 collective-permute-done.other_ref
  50.8 0.0 copy-done
  50.8 0.9 %pair.1 = (f32[512,128]{1,0:T(8,128)S(1)}, f32[512,128]{1,0:T(8,128)S(1)}, bf16[32,4,1024]{2,1,0:T(4,128)(2,1)S(1)}) custom-call(s32[1]{0:T(128)} %bitcast.3.second_ref, bf16[16,4,2048]{2,1,0:T(4,128)(2,1)S(1)} %all_to_all.26.right_ref, bf16[16,4,2048]{2,1,0:T(4,128)(2,1)S(1)} %collective-permute-done.other_ref, bf16[2048,512]{1,0:T(8,128)(2,1)S(1)} %spread.1.spread_ref, ...), custom_call_target="tpu_custom_call" | custom-call | tf_op jit(solution)/shard_map/pair/pallas_call | solution.py:58
  51.8 12.9 %all_to_all.27.both_ref = bf16[32,4,1024]{2,1,0:T(4,128)(2,1)S(1)} all-to-all(bf16[32,4,1024]{2,1,0:T(4,128)(2,1)S(1)} %get-tuple-element.21), channel_id=1, replica_groups=mesh['crop'=1,'res'=32] {'res'}, dimensions={0} | all-to-all | bytes 524288 | tf_op jit(solution)/shard_map/all_to_all | solution.py:277
  64.7 0.7 triangle.1
  65.4 10.4 %all_to_all.28.back_ref = bf16[32,4,512]{2,1,0:T(4,128)(2,1)S(1)} all-to-all(bf16[32,4,512]{2,1,0:T(4,128)(2,1)S(1)} %triangle.1), channel_id=1, replica_groups=mesh['crop'=1,'res'=32] {'res'}, dimensions={0} | all-to-all | bytes 262144 | tf_op jit(solution)/shard_map/all_to_all | solution.py:277
  75.8 0.0 copy-done.7
  75.8 1.0 %final.1 = bf16[4,128,128]{2,1,0:T(8,128)(2,1)} custom-call(bf16[32,4,512]{2,1,0:T(4,128)(2,1)S(1)} %all_to_all.28.back_ref, f32[512,128]{1,0:T(8,128)S(1)} %get-tuple-element.22.one_ref, f32[512,128]{1,0:T(8,128)S(1)} %get-tuple-element.23.gate_ref, bf16[128,128]{1,0:T(8,128)(2,1)S(1)} %copy-done.7), custom_call_target="tpu_custom_call" | custom-call | tf_op jit(solution)/shard_map/final/pallas_call | solution.py:58
  (1 shorter events, 0.0 us)
Async XLA Ops:
  0.6 32.2 %copy-start.2 = (bf16[256,1024]{1,0:T(8,128)(2,1)S(1)}, bf16[256,1024]{1,0:T(8,128)(2,1)}, u32[]{:S(2)}) copy-start(bf16[256,1024]{1,0:T(8,128)(2,1)} %weight_ref.4) | copy-start | bytes 1572868
  0.6 32.2 %copy-start.3 = (bf16[256,256]{1,0:T(8,128)(2,1)S(1)}, bf16[256,256]{1,0:T(8,128)(2,1)}, u32[]{:S(2)}) copy-start(bf16[256,256]{1,0:T(8,128)(2,1)} %readout_ref.3) | copy-start | bytes 393220
  0.7 32.2 %copy-start.6 = (bf16[256,64]{0,1:T(8,128)(2,1)S(1)}, bf16[256,64]{0,1:T(8,128)(2,1)}, u32[]{:S(2)}) copy-start(bf16[256,64]{0,1:T(8,128)(2,1)} %param.24) | copy-start | bytes 98308
  2.7 17.9 %all-to-all-start = ((bf16[32,32,128]{2,1,0:T(8,128)(2,1)}), bf16[32,32,128]{2,1,0:T(8,128)(2,1)S(1)}, u32[]{:S(2)}, u32[]{:S(2)}) async-start(bf16[32,32,128]{2,1,0:T(8,128)(2,1)} %bias.1), calls=%async_computation | async-start | bytes 524288 | tf_op jit(solution)/shard_map/all_to_all | solution.py:277
  10.0 1.0 %copy-start.1 = (bf16[256,1024]{1,0:T(8,128)(2,1)S(1)}, bf16[256,1024]{1,0:T(8,128)(2,1)}, u32[]{:S(2)}) copy-start(bf16[256,1024]{1,0:T(8,128)(2,1)} %weight_ref.3) | copy-start | bytes 1572868
  11.0 0.9 %copy-start.4 = (bf16[2,128,256]{2,1,0:T(8,128)(2,1)S(1)}, bf16[2,128,256]{2,1,0:T(8,128)(2,1)}, u32[]{:S(2)}) copy-start(bf16[2,128,256]{2,1,0:T(8,128)(2,1)} %state_ref.1) | copy-start | bytes 393220
  11.9 0.9 %copy-start.5 = (bf16[256,256]{1,0:T(8,128)(2,1)S(1)}, bf16[256,256]{1,0:T(8,128)(2,1)}, u32[]{:S(2)}) copy-start(bf16[256,256]{1,0:T(8,128)(2,1)} %readout_ref.2) | copy-start | bytes 393220
  12.8 0.7 copy-start.8
  13.5 0.7 copy-start.9
  14.2 0.7 copy-start.10
  15.9 33.4 %copy-start.11 = (bf16[128,640]{1,0:T(8,128)(2,1)S(1)}, bf16[128,640]{1,0:T(8,128)(2,1)}, u32[]{:S(2)}) copy-start(bf16[128,640]{1,0:T(8,128)(2,1)} %param.26) | copy-start | bytes 491524
  20.6 28.7 %slice-start = ((bf16[128,640]{1,0:T(8,128)(2,1)}), bf16[128,512]{1,0:T(8,128)(2,1)S(1)}, s32[]{:S(2)}) async-start(bf16[128,640]{1,0:T(8,128)(2,1)} %param.26), calls=%async_computation.5 | async-start | bytes 262144 | tf_op jit(solution)/shard_map/slice | solution.py:387
  20.6 28.9 %copy-start.12 = (bf16[1024,128]{1,0:T(8,128)(2,1)S(1)}, bf16[1024,128]{1,0:T(8,128)(2,1)}, u32[]{:S(2)}) copy-start(bf16[1024,128]{1,0:T(8,128)(2,1)} %param.25) | copy-start | bytes 786436
  36.1 14.8 %copy-start = (bf16[4,128,128]{2,1,0:T(8,128)(2,1)S(1)}, bf16[4,128,128]{2,1,0:T(8,128)(2,1)}, u32[]{:S(2)}) copy-start(bf16[4,128,128]{2,1,0:T(8,128)(2,1)} %pair_ref.1) | copy-start | bytes 393220
  49.3 1.5 %collective-permute-start = (bf16[16,4,2048]{2,1,0:T(4,128)(2,1)S(1)}, bf16[16,4,2048]{2,1,0:T(4,128)(2,1)S(1)}, u32[]{:S(2)}, u32[]{:S(2)}) collective-permute-start(bf16[16,4,2048]{2,1,0:T(4,128)(2,1)S(1)} %all_to_all.26.right_ref), channel_id=1, source_target_pairs={{0,1},{1,0},{2,3},{3,2},{4,5},{5,4},{6,7},{7,6},{8,9},{9,8},{10,11... | collective-permute-start | bytes 786440 | tf_op jit(solution)/shard_map/ppermute | solution.py:364
  50.3 25.6 %copy-start.7 = (bf16[128,128]{1,0:T(8,128)(2,1)S(1)}, bf16[128,128]{1,0:T(8,128)(2,1)}, u32[]{:S(2)}) copy-start(bf16[128,128]{1,0:T(8,128)(2,1)} %weight_ref.5) | copy-start | bytes 98308

commit v4 on v3

v4 whole, which is shorter than its diff:
```python
import functools

import jax
import jax.numpy as jnp
from jax import lax
from jax.experimental import pallas as pl
from jax.experimental.pallas import tpu as pltpu
from jax.sharding import PartitionSpec as P

EPSILON = 1e-05
F32 = jnp.float32
BF16 = jnp.bfloat16
VMEM_BYTES = 48 * 1024 * 1024


def normalized(rows, axis):
    average = jnp.mean(rows, axis, keepdims=True)
    centred = rows - average
    spread = jnp.mean(centred * centred, axis, keepdims=True)
    return centred * lax.rsqrt(spread + EPSILON)


def dot(a, b):
    return jnp.dot(a, b, preferred_element_type=F32)


def dot_t(a, b):
    return lax.dot_general(a, b, (((1,), (1,)), ((), ())), preferred_element_type=F32)


def t_dot(a, b):
    return lax.dot_general(a, b, (((0,), (0,)), ((), ())), preferred_element_type=F32)


def iota(shape, axis):
    return lax.broadcasted_iota(jnp.int32, shape, axis)


def selector(size, source_of):
    shape = (size, size)
    return (iota(shape, 1) == source_of(iota(shape, 0))).astype(F32).astype(BF16)


def swapped(outer, inner):
    return lambda p: (p % outer) * inner + p // outer


def head_mask(heads, channels, lead):
    width = channels // heads
    shape = (heads, channels)
    mask = (iota(shape, 0) == iota(shape, 1) // width).astype(F32)
    return mask[None] if lead else mask


def kernel_call(body, outs, args, name, flops=0, nbytes=0, scalars=0, fetched=()):
    inside = pl.BlockSpec(memory_space=pltpu.VMEM)
    outside = pl.BlockSpec(memory_space=pl.ANY)
    scalar = pl.BlockSpec(memory_space=pltpu.SMEM)
    args = [
        pltpu.with_memory_space_constraint(a, pltpu.HBM) if i in fetched else a
        for i, a in enumerate(args)
    ]

    def fetching(*refs):
        refs, held, sems = list(refs[: len(args) + len(outs)]), refs[len(args) + len(outs) : -1], refs[-1]
        copies = []
        for k, i in enumerate(fetched):
            copies.append(pltpu.make_async_copy(refs[i], held[k], sems.at[k]))
            copies[-1].start()
            refs[i] = held[k]
        for copy in copies:
            copy.wait()
        body(*refs)

    scratch = [pltpu.VMEM(args[i].shape, args[i].dtype) for i in fetched]
    return pl.pallas_call(
        fetching if fetched else body,
        out_shape=tuple(jax.ShapeDtypeStruct(s, d) for s, d in outs),
        in_specs=[
            scalar if i < scalars else outside if i in fetched else inside
            for i in range(len(args))
        ],
        out_specs=(inside,) * len(outs),
        scratch_shapes=scratch + [pltpu.SemaphoreType.DMA((len(fetched),))] if fetched else [],
        compiler_params=pltpu.CompilerParams(vmem_limit_bytes=VMEM_BYTES),
        cost_estimate=pl.CostEstimate(flops=flops, bytes_accessed=nbytes, transcendentals=0),
        name=name,
    )(*args)


def bias_kernel(pair_ref, weight_ref, out_ref):
    rows, columns, channels = pair_ref.shape
    x = pair_ref[...].reshape(rows * columns, channels).astype(F32)
    bias = dot_t(weight_ref[...], normalized(x, -1).astype(BF16))
    block = jnp.concatenate(
        [bias[:, i * columns : (i + 1) * columns] for i in range(rows)], 0
    ).astype(BF16)
    for d in range(out_ref.shape[0]):
        out_ref[d] = block


def ordered(second, mine, other):
    flip = jnp.full(mine.shape, second, jnp.int32) == 1
    return jnp.where(flip, other, mine), jnp.where(flip, mine, other)


def row_scores_kernel(
    second_ref, ids_ref, other_ids_ref, mask_ref, state_ref, other_ref, table_ref, weight_ref,
    readout_ref, factor_ref,
    scores_ref, value_ref, gate_ref, start_ref, held_ref, wide_ref,
    *, heads, own_rows,
):
    own_sequences, length, channels = state_ref.shape
    tokens = table_ref.shape[0]
    second = second_ref[0]
    held_ref[...] = readout_ref[...]
    ids = jnp.concatenate(ordered(second, ids_ref[...], other_ids_ref[...]), 0)
    states = jnp.concatenate(
        ordered(second, state_ref[...].astype(F32), other_ref[...].astype(F32)), 0
    )
    sequences = 2 * own_sequences
    starts = []
    for s in range(sequences):
        hot = (iota((tokens, length), 0) == ids[s : s + 1, :]).astype(F32).astype(BF16)
        starts.append(states[s] + t_dot(hot, table_ref[...]))
    start = jnp.concatenate(starts, 0)
    normed = normalized(start, -1)
    projected = dot(normed.astype(BF16), weight_ref[:, channels : 3 * channels])
    key = projected[:, :channels].astype(BF16)
    value_ref[...] = projected[:, channels:].astype(BF16)

    def mine(x):
        pairs = x.reshape(sequences * length // (2 * own_rows), 2 * own_rows, channels)
        low, high = pairs[:, :own_rows], pairs[:, own_rows:]
        return ordered(second, low, high)[0].reshape(sequences * length // 2, channels)

    start_ref[...] = mine(start)
    own = mine(normed).astype(BF16)
    query = dot(own, weight_ref[:, :channels]) * (channels // heads) ** (-0.5)
    query = query.astype(BF16).astype(F32)
    gate_ref[...] = jax.nn.sigmoid(dot(own, weight_ref[:, 3 * channels :]))
    mask = head_mask(heads, channels, True)
    extra = (mask_ref[...].astype(F32) - 1.0) * 10000.0
    half = length // 2
    for s in range(sequences):
        rows = query[s * half : (s + 1) * half]
        spread = (rows[:, None, :] * mask).reshape(half * heads, channels).astype(BF16)
        scores_ref[s] = dot_t(spread, key[s * length : (s + 1) * length]) + extra
    width = factor_ref.shape[0] // 2
    right = factor_ref[width:].astype(F32)
    repeated = jnp.broadcast_to(right[:, None, :], (width, own_rows, channels)).reshape(
        width * own_rows, channels
    )
    row = iota(repeated.shape, 0) % own_rows
    for r in range(own_rows):
        wide_ref[:, r * channels : (r + 1) * channels] = jnp.where(row == r, repeated, 0.0).astype(
            BF16
        )


def softmax_parts(scores):
    e = jnp.exp(scores - jnp.max(scores, -1, keepdims=True))
    return e.astype(BF16), 1.0 / jnp.sum(e, -1, keepdims=True)


def row_mix_kernel(
    scores_ref, bias_ref, value_ref, gate_ref, start_ref, weight_ref, out_ref, *, heads
):
    sequences, expanded, length = scores_ref.shape
    channels = value_ref.shape[1]
    devices = out_ref.shape[0]
    rows = expanded // heads
    bias = bias_ref[...].reshape(expanded, length).astype(F32)
    mask = head_mask(heads, channels, True)
    shape = (rows, expanded)
    gather = (iota(shape, 0) == iota(shape, 1) // heads).astype(F32).astype(BF16)
    mixed = []
    for s in range(sequences):
        weights, scale = softmax_parts(scores_ref[s] + bias)
        whole = dot(weights, value_ref[s * length : (s + 1) * length]) * scale
        own = (whole.reshape(rows, heads, channels) * mask).reshape(expanded, channels)
        mixed.append(dot(gather, own.astype(BF16)))
    mixed = jnp.concatenate(mixed, 0)
    gated = (gate_ref[...] * mixed).astype(BF16)
    after = start_ref[...] + dot(gated, weight_ref[...])
    blocks = [
        after[s * rows : (s + 1) * rows].reshape(devices, rows // devices, channels)
        for s in range(sequences)
    ]
    out_ref[...] = jnp.concatenate(blocks, 1).astype(BF16)


def column_kernel(
    state_ref, weight_ref, readout_ref, factor_ref, wide_ref, out_ref, left_ref, right_ref,
    *, heads, own_rows,
):
    devices, block, channels = state_ref.shape
    size = devices * block
    sequences = size // own_rows
    to_rows = selector(size, swapped(sequences, own_rows))
    to_sequences = selector(size, swapped(own_rows, sequences))
    start = dot(to_rows, state_ref[...].reshape(size, channels))
    projected = dot(normalized(start, -1).astype(BF16), weight_ref[...])
    query = (projected[:, :channels] * (channels // heads) ** (-0.5)).astype(BF16).astype(F32)
    key = projected[:, channels : 2 * channels].astype(BF16)
    value = projected[:, 2 * channels : 3 * channels].astype(BF16)
    gate = jax.nn.sigmoid(projected[:, 3 * channels :])
    mask = head_mask(heads, channels, False)
    gated = []
    for r in range(own_rows):
        rows = slice(r * sequences, (r + 1) * sequences)
        spread = jnp.concatenate(
            [(query[rows] * mask[h : h + 1]).astype(BF16) for h in range(heads)], 0
        )
        weights, scale = softmax_parts(dot_t(spread, key[rows]))
        whole = dot(weights, value[rows]) * scale
        mixed = whole[:sequences] * mask[:1]
        for h in range(1, heads):
            mixed += whole[h * sequences : (h + 1) * sequences] * mask[h : h + 1]
        gated.append((gate[rows] * mixed).astype(BF16))
    after = start + dot(jnp.concatenate(gated, 0), readout_ref[...])
    normed = normalized(after, -1).astype(BF16)
    width = factor_ref.shape[0] // 2
    fold = max(1, 128 // sequences)
    part = width // fold
    side = jnp.concatenate(
        [normed[r * sequences : (r + 1) * sequences] for r in range(own_rows)], 1
    )
    right = dot_t(wide_ref[...], side)
    cut = part * own_rows
    right = jnp.concatenate([right[f * cut : (f + 1) * cut] for f in range(fold)], 1)
    tall = right_ref.shape[1]
    packed = jnp.concatenate(
        [right[t * tall : (t + 1) * tall] for t in range(cut // tall)], 1
    ).astype(BF16)
    for d in range(right_ref.shape[0]):
        right_ref[d] = packed
    left_ref[...] = dot_t(normed, factor_ref[:width]).astype(BF16)
    out_ref[...] = dot(to_sequences, after.astype(BF16)).astype(BF16).reshape(out_ref.shape)


def spread_kernel(aligned_ref, left_ref, weight_ref, out_ref, final_ref, sem, *, own_rows, per):
    store = pltpu.make_async_copy(aligned_ref, final_ref, sem)
    store.start()
    size, width = left_ref.shape
    sequences = size // own_rows
    channels = weight_ref.shape[1] // width
    fold = max(1, 128 // sequences)
    part = width // fold
    product = dot(left_ref[...], weight_ref[...])
    for d in range(width):
        f, t, e = d // part, d % part // per, d % per
        at = ((e * (part // per) + t) * fold + f) * sequences
        for r in range(own_rows):
            out_ref[at : at + sequences, r * channels : (r + 1) * channels] = product[
                r * sequences : (r + 1) * sequences, d * channels : (d + 1) * channels
            ].astype(BF16)
    store.wait()


def pair_kernel(
    second_ref, right_ref, other_ref, spread_ref, pair_ref, weight_ref, gate_weight_ref,
    one_ref, gate_ref, out_ref,
    *, sequences,
):
    own_rows, columns, channels = pair_ref.shape
    first, second = ordered(
        second_ref[0], right_ref[...].astype(F32), other_ref[...].astype(F32)
    )
    right = [
        jnp.concatenate([first[:, e : e + own_rows], second[:, e : e + own_rows]], 1).reshape(
            columns, right_ref.shape[-1]
        )
        for e in range(0, right_ref.shape[1], own_rows)
    ]
    right = jnp.concatenate(right, 1).astype(BF16)
    update = dot(right, spread_ref[...]) * (1.0 / sequences)
    ones = [
        pair_ref[i].astype(F32) + update[:, i * channels : (i + 1) * channels]
        for i in range(own_rows)
    ]
    one = jnp.concatenate(ones, 0)
    one_ref[...] = one
    normed = normalized(one, -1).astype(BF16)
    gate_ref[...] = jax.nn.sigmoid(dot(normed, gate_weight_ref[...]))
    factors = dot_t(weight_ref[...], normed)
    left = jax.nn.sigmoid(factors[channels : 2 * channels]) * factors[:channels]
    right = jax.nn.sigmoid(factors[3 * channels :]) * factors[2 * channels : 3 * channels]
    both = jnp.concatenate([left.astype(BF16), right.astype(BF16)], 1)
    out_ref[...] = both.reshape(out_ref.shape)


def triangle_kernel(both_ref, out_ref, *, own_rows):
    devices, own_channels, lanes = both_ref.shape
    columns = lanes // 2 // own_rows
    size = devices * own_channels
    both = both_ref[...].reshape(size, lanes)
    left = jnp.concatenate([both[:, i * columns : (i + 1) * columns] for i in range(own_rows)], 0)
    right = jnp.concatenate(
        [both[:, (own_rows + i) * columns : (own_rows + i + 1) * columns] for i in range(own_rows)],
        0,
    )
    total = size * own_rows
    order = selector(
        total,
        lambda p: p % own_rows * size + p % columns // own_rows * own_channels + p // columns,
    )
    right = dot(order, right).astype(BF16)
    channel = iota((total, 1), 0) % own_channels
    combined = jnp.zeros((total, columns), F32)
    for c in range(own_channels):
        part = dot_t(left, right[c * columns : (c + 1) * columns])
        combined = jnp.where(channel == c, part, combined)
    combined = combined.astype(BF16)
    out_ref[...] = jnp.concatenate(
        [combined[i * size : (i + 1) * size] for i in range(own_rows)], 1
    ).reshape(out_ref.shape)


def final_kernel(back_ref, one_ref, gate_ref, weight_ref, out_ref):
    channels = weight_ref.shape[0]
    combined = back_ref[...].reshape(channels, back_ref.shape[-1]).astype(F32)
    normed = normalized(combined, 0).astype(BF16)
    update = t_dot(normed, weight_ref[...])
    out_ref[...] = (one_ref[...] + gate_ref[...] * update).astype(BF16).reshape(out_ref.shape)


def exchanged(x):
    return lax.all_to_all(x, "res", split_axis=0, concat_axis=0, tiled=True)


def shards(
    homolog_symbol_ids,
    residue_attend_mask,
    alignment_state,
    pair,
    symbol_lookup_matrix,
    pair_bias_weight,
    row_projection_weight,
    horizontal_readout_matrix,
    column_projection_weight,
    vertical_readout_matrix,
    product_factor_matrices,
    outer_output_weight,
    triangle_input_weight,
    triangle_output_weight,
):
    devices = lax.axis_size("res")
    own_sequences, length, channels = alignment_state.shape
    sequences = own_sequences * devices
    own_rows, columns, pair_channels = pair.shape
    heads = pair_bias_weight.shape[1]
    width = product_factor_matrices.shape[1] // 2
    own_channels = pair_channels // devices
    rows = own_sequences * length

    groups = [list(range(first, devices, 2)) for first in range(2)]
    half = devices // 2
    second = (lax.axis_index("res") % 2).reshape(1)

    def among_class(x):
        return lax.all_to_all(x, "res", 0, 0, axis_index_groups=groups, tiled=True)

    def from_other_core(x):
        return lax.ppermute(x, "res", [(i, i ^ 1) for i in range(devices)])

    (bias,) = kernel_call(
        bias_kernel,
        [((half, own_rows * heads, columns), BF16)],
        (pair, pair_bias_weight.T),
        "bias",
        fetched=(0, 1),
    )
    bias = among_class(bias)
    factors = product_factor_matrices.T
    scores, value, gate, start, readout, wide = kernel_call(
        functools.partial(row_scores_kernel, heads=heads, own_rows=own_rows),
        [
            ((2 * own_sequences, length // 2 * heads, length), F32),
            ((2 * rows, channels), BF16),
            ((rows, channels), F32),
            ((rows, channels), F32),
            ((channels, channels), BF16),
            ((width * own_rows, own_rows * channels), BF16),
        ],
        (
            second,
            homolog_symbol_ids,
            from_other_core(homolog_symbol_ids),
            residue_attend_mask.reshape(1, length),
            alignment_state,
            from_other_core(alignment_state),
            symbol_lookup_matrix,
            row_projection_weight,
            horizontal_readout_matrix,
            factors,
        ),
        "row_scores",
        flops=2 * rows * channels * 4 * channels,
        nbytes=1 << 21,
        scalars=1,
        fetched=(1, 3, 4, 6, 7, 8, 9),
    )
    (after_rows,) = kernel_call(
        functools.partial(row_mix_kernel, heads=heads),
        [((half, 2 * own_sequences * own_rows, channels), BF16)],
        (scores, bias, value, gate, start, readout),
        "row_mix",
    )
    by_residue = among_class(after_rows)
    per = max(1, 8 // own_rows)
    aligned, left, right = kernel_call(
        functools.partial(column_kernel, heads=heads, own_rows=own_rows),
        [
            ((sequences, own_rows, channels), BF16),
            ((sequences * own_rows, width), BF16),
            ((half, per * own_rows, width * sequences // per), BF16),
        ],
        (by_residue, column_projection_weight, vertical_readout_matrix, factors, wide),
        "column",
    )
    right = among_class(right)
    other = from_other_core(right)
    inside = pl.BlockSpec(memory_space=pltpu.VMEM)
    outside = pl.BlockSpec(memory_space=pl.ANY)
    spread, alignment_output = pl.pallas_call(
        functools.partial(spread_kernel, own_rows=own_rows, per=per),
        out_shape=(
            jax.ShapeDtypeStruct((width * sequences, own_rows * pair_channels), BF16),
            jax.ShapeDtypeStruct(aligned.shape, BF16),
        ),
        in_specs=[inside] * 3,
        out_specs=(inside, outside),
        scratch_shapes=[pltpu.SemaphoreType.DMA],
        compiler_params=pltpu.CompilerParams(vmem_limit_bytes=VMEM_BYTES),
        cost_estimate=pl.CostEstimate(
            flops=2 * own_rows * sequences * width * width * pair_channels,
            bytes_accessed=1 << 21,
            transcendentals=0,
        ),
        name="spread",
    )(aligned, left, outer_output_weight.reshape(width, width * pair_channels))
    pair_one, gate_out, both = kernel_call(
        functools.partial(pair_kernel, sequences=sequences),
        [
            ((own_rows * columns, pair_channels), F32),
            ((own_rows * columns, pair_channels), F32),
            ((devices, own_channels, 2 * own_rows * columns), BF16),
        ],
        (
            second,
            right,
            other,
            spread,
            pair,
            triangle_input_weight[:, : 4 * pair_channels].T,
            triangle_input_weight[:, 4 * pair_channels :],
        ),
        "pair",
        scalars=1,
    )
    both = exchanged(both)
    (combined,) = kernel_call(
        functools.partial(triangle_kernel, own_rows=own_rows),
        [((devices, own_channels, own_rows * columns), BF16)],
        (both,),
        "triangle",
    )
    back = exchanged(combined)
    (pair_output,) = kernel_call(
        final_kernel,
        [((own_rows, columns, pair_channels), BF16)],
        (back, pair_one, gate_out, triangle_output_weight),
        "final",
    )
    return (alignment_output, pair_output)


def solution(mesh):
    placed = (
        P(("crop", "res"), None),
        P("crop"),
        P(("crop", "res"), None, None),
        P(("crop", "res"), None, None),
    ) + (P(),) * 10
    return jax.shard_map(
        shards,
        mesh=mesh,
        in_specs=placed,
        out_specs=(P("crop", "res", None), P(("crop", "res"), None, None)),
        check_vma=False,
    )
```

time: 77.2 us -> 73.9 us (0.957)
  local copies, waits for them, and re-layouts: 5.16 us -> 0.28 us
  starting transfers between devices: 7.31 us -> 8.9 us
    all_to_all x1 -> x2, blocking collectives: 13.2 us -> 23.7 us  [among_class(): return lax.all_to_all(x, 'res', 0, 0, axis_index_groups=groups, tiled=True)]
    all_to_all x3 -> x2, blocking collectives: 33.8 us -> 23.4 us  [exchanged(): return lax.all_to_all(x, 'res', split_axis=0, concat_axis=0, tiled=True)]
    unnamed x27 -> x15, local copies, waits for them, and re-layouts: 5.03 us -> 0.16 us
    all_to_all x1, waiting for transfers between devices: 4.7 us -> 3.65 us  [among_class(): return lax.all_to_all(x, 'res', 0, 0, axis_index_groups=groups, tiled=True)]
    ppermute x1 -> x3, waiting for transfers between devices: 0.56 us -> 1.59 us  [from_other_core(): return lax.ppermute(x, 'res', [(i, i ^ 1) for i in range(devices)])]
    all_to_all x1, starting transfers between devices: 7.3 us -> 8.32 us  [among_class(): return lax.all_to_all(x, 'res', 0, 0, axis_index_groups=groups, tiled=True)]
  transfers between devices with their start and end apart: 2 -> 4, of which waited for: 2 -> 3; matrix products, arithmetic and copies ran while one was open for 0% -> 0% of each run, Pallas kernels for 2% -> 4%
where the time goes in v4:
time: 73.9 us; the launch traced here: 73.5 us
  blocking collectives  47.1 us (64%)
  Pallas kernels  11.2 us (15%)
  starting transfers between devices  8.9 us (12%)
  waiting for transfers between devices  5.24 us (7%)
  between operations  0.8 us (1%)
    all_to_all x2, blocking collectives, among_class(): return lax.all_to_all(x, 'res', 0, 0, axis_index_groups=groups, tiled=True)  23.7 us
    all_to_all x2, blocking collectives, exchanged(): return lax.all_to_all(x, 'res', split_axis=0, concat_axis=0, tiled=True)  23.4 us
    pallas_call x7, Pallas kernels, kernel_call(): pl.pallas_call(fetching if fetched else body, out_shape=tuple((jax.ShapeD...  10.5 us
    all_to_all x1, starting transfers between devices, among_class(): return lax.all_to_all(x, 'res', 0, 0, axis_index_groups=groups, tiled=True)  8.32 us
    all_to_all x1, waiting for transfers between devices, among_class(): return lax.all_to_all(x, 'res', 0, 0, axis_index_groups=groups, tiled=True)  3.65 us
    ppermute x3, waiting for transfers between devices, from_other_core(): return lax.ppermute(x, 'res', [(i, i ^ 1) for i in range(devices)])  1.59 us
  transfers between devices with their start and end apart: 4, of which 3 were waited for; matrix products, arithmetic and copies ran while one was open for 0% of the time, Pallas kernels for 4%

profile of v4, /device:TPU:0, one launch (start us, length us, event | category | flops | bytes accessed | tf_op | source)
XLA Modules:
  0.0 73.5 jit_solution(16988679960998711758)
XLA Ops:
  0.6 0.0 copy-start.3
  0.6 0.0 copy-start.2
  0.7 0.0 copy-start.1
  0.7 2.0 %bias.1 = bf16[16,32,128]{2,1,0:T(8,128)(2,1)} custom-call(bf16[4,128,128]{2,1,0:T(8,128)(2,1)} %pair_ref.1, bf16[8,128]{1,0:T(8,128)(2,1)} %bitcast.8), custom_call_target="tpu_custom_call" | custom-call | tf_op jit(solution)/shard_map/bias/pallas_call | solution.py:76
  2.7 8.3 %all-to-all-start = ((bf16[16,32,128]{2,1,0:T(8,128)(2,1)}), bf16[16,32,128]{2,1,0:T(8,128)(2,1)S(1)}, u32[]{:S(2)}, u32[]{:S(2)}) async-start(bf16[16,32,128]{2,1,0:T(8,128)(2,1)} %bias.1), calls=%async_computation | async-start | bytes 262144 | tf_op jit(solution)/shard_map/all_to_all | solution.py:362
  11.0 0.1 collective-permute-start.1
  11.1 0.5 collective-permute-start
  11.6 1.0 %collective-permute-done.refs_2_ = s32[2,128]{1,0:T(2,128)S(1)} collective-permute-done((s32[2,128]{1,0:T(2,128)}, s32[2,128]{1,0:T(2,128)S(1)}, u32[]{:S(2)}, u32[]{:S(2)}) %collective-permute-start) | collective-permute-done | bytes 1056 | tf_op jit(solution)/shard_map/ppermute | solution.py:365
  12.6 0.0 collective-permute-done.1.refs_5_
  12.6 2.5 %row_scores.1 = (f32[4,512,128]{2,1,0:T(8,128)S(1)}, bf16[512,256]{1,0:T(8,128)(2,1)S(1)}, f32[256,256]{1,0:T(8,128)S(1)}, f32[256,256]{1,0:T(8,128)S(1)}, bf16[...) custom-call(s32[1]{0:T(128)} %bitcast.refs_0_.second_ref, s32[2,128]{1,0:T(2,128)} %refs_1_.1, ...), custom_call_target="tpu_custom_call" | custom-call | flops 134217728 | bytes 2097152 | tf_op jit(solution)/shard_map/row_scores/pallas_call | solution.py:76
  15.1 0.0 copy-start.5
  15.2 3.6 %all-to-all-done.bias_ref = bf16[16,32,128]{2,1,0:T(8,128)(2,1)S(1)} async-done(((bf16[16,32,128]{2,1,0:T(8,128)(2,1)}), bf16[16,32,128]{2,1,0:T(8,128)(2,1)S(1)}, u32[]{:S(2)}, u32[]{:S(2)}) %all-to-all-start) | async-done | bytes 131104 | tf_op jit(solution)/shard_map/all_to_all | solution.py:362
  18.8 0.0 slice-start
  18.8 1.4 %row_mix.1 = bf16[16,16,256]{2,1,0:T(8,128)(2,1)S(1)} custom-call(f32[4,512,128]{2,1,0:T(8,128)S(1)} %get-tuple-element.16.scores_ref, bf16[16,32,128]{2,1,0:T(8,128)(2,1)S(1)} %all-to-all-done.bias_ref, bf16[512,256]{1,0:T(8,128)(2,1)S(1)} %get-tuple-element.17.value_ref, f32[256,256]{1,0:T(8,128)S(1)} %get-tuple-element.18.gate_ref, ...), custom_call_target="tpu_custom_call" | custom-call | tf_op jit(solution)/shard_map/row_mix/pallas_call | solution.py:76
  20.2 0.0 copy-start.6
  20.2 0.0 copy-start
  20.2 11.0 %all_to_all.25.state_ref = bf16[16,16,256]{2,1,0:T(8,128)(2,1)S(1)} all-to-all(bf16[16,16,256]{2,1,0:T(8,128)(2,1)S(1)} %row_mix.1), channel_id=1, replica_groups={{0,2,4,6,8,10,12,14,16,18,20,22,24,26,28,30},{1,3,5,7,9,11,13,15,17,19,..., dimensions={0} | all-to-all | bytes 262144 | tf_op jit(solution)/shard_map/all_to_all | solution.py:362
  31.3 0.0 copy-done.3
  31.3 0.0 copy-done.2
  31.3 0.0 copy-done.1
  31.3 1.9 %column.1 = (bf16[64,4,256]{2,1,0:T(4,128)(2,1)S(1)}, bf16[256,32]{1,0:T(8,128)(2,1)S(1)}, bf16[16,8,1024]{2,1,0:T(8,128)(2,1)S(1)}) custom-call(bf16[16,16,256]{2,1,0:T(8,128)(2,1)S(1)} %all_to_all.25.state_ref, bf16[256,1024]{1,0:T(8,128)(2,1)S(1)} %copy-done.1, bf16[256,256]{1,0:T(8,128)(2,1)S(1)} %copy-done.2, bf16[64,256]{1,0:T(8,128)(2,1)S(1)} %bitcast.7, ...), custom_call_target="tpu_custom_call" | custom-call | tf_op jit(solution)/shard_map/column/pallas_call | solution.py:76
  33.2 12.7 %all_to_all.26.right_ref = bf16[16,8,1024]{2,1,0:T(8,128)(2,1)S(1)} all-to-all(bf16[16,8,1024]{2,1,0:T(8,128)(2,1)S(1)} %get-tuple-element.25), channel_id=1, replica_groups={{0,2,4,6,8,10,12,14,16,18,20,22,24,26,28,30},{1,3,5,7,9,11,13,15,17,19,..., dimensions={0} | all-to-all | bytes 524288 | tf_op jit(solution)/shard_map/all_to_all | solution.py:362
  45.9 0.0 collective-permute-start.2
  45.9 0.0 copy-done.5
  45.9 0.0 slice-done
  45.9 0.1 copy.17
  46.1 0.0 copy-done.6
  46.1 0.1 reshape.15.weight_ref
  46.2 0.7 spread.1
  46.9 0.0 copy-start.4
  46.9 0.5 collective-permute-done.2.other_ref
  47.5 0.0 copy-done
  47.5 1.0 %pair.1 = (f32[512,128]{1,0:T(8,128)S(1)}, f32[512,128]{1,0:T(8,128)S(1)}, bf16[32,4,1024]{2,1,0:T(4,128)(2,1)S(1)}) custom-call(s32[1]{0:T(128)} %bitcast.refs_0_.second_ref, bf16[16,8,1024]{2,1,0:T(8,128)(2,1)S(1)} %all_to_all.26.right_ref, bf16[16,8,1024]{2,1,0:T(8,128)(2,1)S(1)} %collective-permute-done.2.other_ref, ...), custom_call_target="tpu_custom_call" | custom-call | tf_op jit(solution)/shard_map/pair/pallas_call | solution.py:76
  48.5 12.9 %all_to_all.27.both_ref = bf16[32,4,1024]{2,1,0:T(4,128)(2,1)S(1)} all-to-all(bf16[32,4,1024]{2,1,0:T(4,128)(2,1)S(1)} %get-tuple-element.27), channel_id=1, replica_groups=mesh['crop'=1,'res'=32] {'res'}, dimensions={0} | all-to-all | bytes 524288 | tf_op jit(solution)/shard_map/all_to_all | solution.py:329
  61.4 0.7 triangle.1
  62.1 10.4 %all_to_all.28.back_ref = bf16[32,4,512]{2,1,0:T(4,128)(2,1)S(1)} all-to-all(bf16[32,4,512]{2,1,0:T(4,128)(2,1)S(1)} %triangle.1), channel_id=1, replica_groups=mesh['crop'=1,'res'=32] {'res'}, dimensions={0} | all-to-all | bytes 262144 | tf_op jit(solution)/shard_map/all_to_all | solution.py:329
  72.6 0.0 copy-done.4
  72.6 1.0 %final.1 = bf16[4,128,128]{2,1,0:T(8,128)(2,1)} custom-call(bf16[32,4,512]{2,1,0:T(4,128)(2,1)S(1)} %all_to_all.28.back_ref, f32[512,128]{1,0:T(8,128)S(1)} %get-tuple-element.28.one_ref, f32[512,128]{1,0:T(8,128)S(1)} %get-tuple-element.29.gate_ref, bf16[128,128]{1,0:T(8,128)(2,1)S(1)} %copy-done.4), custom_call_target="tpu_custom_call" | custom-call | tf_op jit(solution)/shard_map/final/pallas_call | solution.py:76
  (1 shorter events, 0.0 us)
Async XLA Ops:
  0.6 30.7 %copy-start.3 = (bf16[256,64]{0,1:T(8,128)(2,1)S(1)}, bf16[256,64]{0,1:T(8,128)(2,1)}, u32[]{:S(2)}) copy-start(bf16[256,64]{0,1:T(8,128)(2,1)} %param.24) | copy-start | bytes 98308
  0.6 30.6 %copy-start.2 = (bf16[256,256]{1,0:T(8,128)(2,1)S(1)}, bf16[256,256]{1,0:T(8,128)(2,1)}, u32[]{:S(2)}) copy-start(bf16[256,256]{1,0:T(8,128)(2,1)} %readout_ref.1) | copy-start | bytes 393220
  0.7 30.6 %copy-start.1 = (bf16[256,1024]{1,0:T(8,128)(2,1)S(1)}, bf16[256,1024]{1,0:T(8,128)(2,1)}, u32[]{:S(2)}) copy-start(bf16[256,1024]{1,0:T(8,128)(2,1)} %weight_ref.2) | copy-start | bytes 1572868
  2.7 16.1 %all-to-all-start = ((bf16[16,32,128]{2,1,0:T(8,128)(2,1)}), bf16[16,32,128]{2,1,0:T(8,128)(2,1)S(1)}, u32[]{:S(2)}, u32[]{:S(2)}) async-start(bf16[16,32,128]{2,1,0:T(8,128)(2,1)} %bias.1), calls=%async_computation | async-start | bytes 262144 | tf_op jit(solution)/shard_map/all_to_all | solution.py:362
  11.0 1.6 %collective-permute-start.1 = (bf16[2,128,256]{2,1,0:T(8,128)(2,1)}, bf16[2,128,256]{2,1,0:T(8,128)(2,1)S(1)}, u32[]{:S(2)}, u32[]{:S(2)}) collective-permute-start(bf16[2,128,256]{2,1,0:T(8,128)(2,1)} %refs_4_.1), channel_id=1, source_target_pairs={{0,1},{1,0},{2,3},{3,2},{4,5},{5,4},{6,7},{7,6},{8,9},{9,8},{10,11... | collective-permute-start | bytes 393224 | tf_op jit(solution)/shard_map/ppermute | solution.py:365
  11.1 1.5 %collective-permute-start = (s32[2,128]{1,0:T(2,128)}, s32[2,128]{1,0:T(2,128)S(1)}, u32[]{:S(2)}, u32[]{:S(2)}) collective-permute-start(s32[2,128]{1,0:T(2,128)} %refs_1_.1), channel_id=1, source_target_pairs={{0,1},{1,0},{2,3},{3,2},{4,5},{5,4},{6,7},{7,6},{8,9},{9,8},{10,11... | collective-permute-start | bytes 3080 | tf_op jit(solution)/shard_map/ppermute | solution.py:365
  15.1 30.8 %copy-start.5 = (bf16[128,640]{1,0:T(8,128)(2,1)S(1)}, bf16[128,640]{1,0:T(8,128)(2,1)}, u32[]{:S(2)}) copy-start(bf16[128,640]{1,0:T(8,128)(2,1)} %param.26) | copy-start | bytes 491524
  18.8 27.1 %slice-start = ((bf16[128,640]{1,0:T(8,128)(2,1)}), bf16[128,512]{1,0:T(8,128)(2,1)S(1)}, s32[]{:S(2)}) async-start(bf16[128,640]{1,0:T(8,128)(2,1)} %param.26), calls=%async_computation.5 | async-start | bytes 262144 | tf_op jit(solution)/shard_map/slice | solution.py:456
  20.2 25.8 %copy-start.6 = (bf16[1024,128]{1,0:T(8,128)(2,1)S(1)}, bf16[1024,128]{1,0:T(8,128)(2,1)}, u32[]{:S(2)}) copy-start(bf16[1024,128]{1,0:T(8,128)(2,1)} %param.25) | copy-start | bytes 786436
  20.2 27.2 %copy-start = (bf16[4,128,128]{2,1,0:T(8,128)(2,1)S(1)}, bf16[4,128,128]{2,1,0:T(8,128)(2,1)}, u32[]{:S(2)}) copy-start(bf16[4,128,128]{2,1,0:T(8,128)(2,1)} %pair_ref.1) | copy-start | bytes 393220
  45.9 1.5 %collective-permute-start.2 = (bf16[16,8,1024]{2,1,0:T(8,128)(2,1)S(1)}, bf16[16,8,1024]{2,1,0:T(8,128)(2,1)S(1)}, u32[]{:S(2)}, u32[]{:S(2)}) collective-permute-start(bf16[16,8,1024]{2,1,0:T(8,128)(2,1)S(1)} %all_to_all.26.right_ref), channel_id=1, source_target_pairs={{0,1},{1,0},{2,3},{3,2},{4,5},{5,4},{6,7},{7,6},{8,9},{9,8},{10,11... | collective-permute-start | bytes 786440 | tf_op jit(solution)/shard_map/ppermute | solution.py:365
  46.9 25.7 %copy-start.4 = (bf16[128,128]{1,0:T(8,128)(2,1)S(1)}, bf16[128,128]{1,0:T(8,128)(2,1)}, u32[]{:S(2)}) copy-start(bf16[128,128]{1,0:T(8,128)(2,1)} %weight_ref.3) | copy-start | bytes 98308

commit v5 on v4

--- a/solution.py
+++ b/solution.py
@@ -38,18 +38,28 @@
 
 def selector(size, source_of):
     shape = (size, size)
-    return (iota(shape, 1) == source_of(iota(shape, 0))).astype(F32).astype(BF16)
+    return (iota(shape, 1) == source_of(iota((size, 1), 0))).astype(F32).astype(BF16)
 
 
 def swapped(outer, inner):
     return lambda p: (p % outer) * inner + p // outer
 
 
-def head_mask(heads, channels, lead):
-    width = channels // heads
-    shape = (heads, channels)
-    mask = (iota(shape, 0) == iota(shape, 1) // width).astype(F32)
-    return mask[None] if lead else mask
+def lane_parts(channels, heads):
+    lanes = min(128, channels)
+    return [slice(at, at + lanes) for at in range(0, channels, lanes)], lanes * heads // channels
+
+
+def own_channels_of(rows, lanes, width, first, own_rows):
+    shape = (rows, lanes)
+    return iota(shape, 0) // own_rows + first == iota(shape, 1) // width
+
+
+def picked(pieces, masks):
+    total = jnp.zeros_like(pieces[0])
+    for piece, mask in zip(pieces, masks):
+        total = jnp.where(jnp.broadcast_to(mask, piece.shape), piece, total)
+    return total
 
 
 def kernel_call(body, outs, args, name, flops=0, nbytes=0, scalars=0, fetched=()):
@@ -91,10 +101,17 @@
 def bias_kernel(pair_ref, weight_ref, out_ref):
     rows, columns, channels = pair_ref.shape
     x = pair_ref[...].reshape(rows * columns, channels).astype(F32)
-    bias = dot_t(weight_ref[...], normalized(x, -1).astype(BF16))
-    block = jnp.concatenate(
-        [bias[:, i * columns : (i + 1) * columns] for i in range(rows)], 0
-    ).astype(BF16)
+    normed = normalized(x, -1).astype(BF16)
+    weight = weight_ref[...].astype(F32)
+    heads = weight.shape[0]
+    weight = jnp.broadcast_to(weight[:, None, :], (heads, rows, channels))
+    weight = weight.reshape(heads * rows, channels).astype(BF16)
+    bias = dot_t(weight, normed)
+    row = iota((heads * rows, columns), 0) % rows
+    block = bias[:, :columns]
+    for i in range(1, rows):
+        block = jnp.where(row == i, bias[:, i * columns : (i + 1) * columns], block)
+    block = block.astype(BF16)
     for d in range(out_ref.shape[0]):
         out_ref[d] = block
 
@@ -135,17 +152,32 @@
         return ordered(second, low, high)[0].reshape(sequences * length // 2, channels)
 
     start_ref[...] = mine(start)
-    own = mine(normed).astype(BF16)
+    own = mine(normed)
+    per = max(1, 8 // own_rows)
+    own = own.reshape(own.shape[0] // own_rows, own_rows, channels)
+    own = jnp.concatenate([own] * per, 1).reshape(-1, channels).astype(BF16)
     query = dot(own, weight_ref[:, :channels]) * (channels // heads) ** (-0.5)
     query = query.astype(BF16).astype(F32)
     gate_ref[...] = jax.nn.sigmoid(dot(own, weight_ref[:, 3 * channels :]))
-    mask = head_mask(heads, channels, True)
     extra = (mask_ref[...].astype(F32) - 1.0) * 10000.0
-    half = length // 2
+    tall = query.shape[0] // sequences
+    block = per * own_rows
+    parts, inner = lane_parts(channels, heads)
+    masks = [
+        own_channels_of(block, channels // len(parts), channels // heads, h, own_rows)[None]
+        for h in range(0, inner, per)
+    ]
+    size = len(masks) * tall
     for s in range(sequences):
-        rows = query[s * half : (s + 1) * half]
-        spread = (rows[:, None, :] * mask).reshape(half * heads, channels).astype(BF16)
-        scores_ref[s] = dot_t(spread, key[s * length : (s + 1) * length]) + extra
+        for u, part in enumerate(parts):
+            rows = query[s * tall : (s + 1) * tall, part]
+            rows = rows.reshape(tall // block, block, rows.shape[1])
+            spread = [
+                picked([rows], [mask]).reshape(tall, rows.shape[2]).astype(BF16) for mask in masks
+            ]
+            scores_ref[s, u * size : (u + 1) * size] = (
+                dot_t(jnp.concatenate(spread, 0), key[s * length : (s + 1) * length, part]) + extra
+            )
     width = factor_ref.shape[0] // 2
     right = factor_ref[width:].astype(F32)
     repeated = jnp.broadcast_to(right[:, None, :], (width, own_rows, channels)).reshape(
@@ -164,30 +196,51 @@
 
 
 def row_mix_kernel(
-    scores_ref, bias_ref, value_ref, gate_ref, start_ref, weight_ref, out_ref, *, heads
+    scores_ref, bias_ref, value_ref, gate_ref, start_ref, weight_ref, out_ref, *, heads, own_rows
 ):
     sequences, expanded, length = scores_ref.shape
     channels = value_ref.shape[1]
-    devices = out_ref.shape[0]
-    rows = expanded // heads
-    bias = bias_ref[...].reshape(expanded, length).astype(F32)
-    mask = head_mask(heads, channels, True)
-    shape = (rows, expanded)
-    gather = (iota(shape, 0) == iota(shape, 1) // heads).astype(F32).astype(BF16)
-    mixed = []
+    groups = out_ref.shape[0]
+    per = max(1, 8 // own_rows)
+    tiles = heads // per
+    block = per * own_rows
+    tall = groups * block
+    bias = bias_ref[...].astype(F32)
+    bias = jnp.concatenate(
+        [
+            bias[:, t * block : (t + 1) * block].reshape(tall, length)
+            for t in range(tiles)
+        ],
+        0,
+    )
+    parts, inner = lane_parts(channels, heads)
+    masks = [
+        own_channels_of(block, channels // len(parts), channels // heads, h, own_rows)[None]
+        for h in range(0, inner, per)
+    ]
+    size = len(masks) * tall
+    pieces = []
     for s in range(sequences):
         weights, scale = softmax_parts(scores_ref[s] + bias)
-        whole = dot(weights, value_ref[s * length : (s + 1) * length]) * scale
-        own = (whole.reshape(rows, heads, channels) * mask).reshape(expanded, channels)
-        mixed.append(dot(gather, own.astype(BF16)))
-    mixed = jnp.concatenate(mixed, 0)
-    gated = (gate_ref[...] * mixed).astype(BF16)
-    after = start_ref[...] + dot(gated, weight_ref[...])
-    blocks = [
-        after[s * rows : (s + 1) * rows].reshape(devices, rows // devices, channels)
-        for s in range(sequences)
-    ]
-    out_ref[...] = jnp.concatenate(blocks, 1).astype(BF16)
+        mixed = []
+        for u, part in enumerate(parts):
+            rows = slice(u * size, (u + 1) * size)
+            whole = dot(weights[rows], value_ref[s * length : (s + 1) * length, part])
+            whole = whole * scale[rows]
+            whole = whole.reshape(len(masks), groups, block, whole.shape[1])
+            mixed.append(
+                picked([whole[t] for t in range(len(masks))], masks).reshape(tall, whole.shape[3])
+            )
+        mixed = jnp.concatenate(mixed, 1)
+        gated = (gate_ref[s * tall : (s + 1) * tall] * mixed).astype(BF16)
+        update = dot(gated, weight_ref[...]).reshape(groups, block, channels)
+        after = start_ref[s * groups * own_rows : (s + 1) * groups * own_rows].reshape(
+            groups, own_rows, channels
+        )
+        for h in range(per):
+            after = after + update[:, h * own_rows : (h + 1) * own_rows]
+        pieces.append(after)
+    out_ref[...] = jnp.concatenate(pieces, 1).astype(BF16)
 
 
 def column_kernel(
@@ -205,19 +258,24 @@
     key = projected[:, channels : 2 * channels].astype(BF16)
     value = projected[:, 2 * channels : 3 * channels].astype(BF16)
     gate = jax.nn.sigmoid(projected[:, 3 * channels :])
-    mask = head_mask(heads, channels, False)
+    parts, inner = lane_parts(channels, heads)
+    masks = [
+        own_channels_of(1, channels // len(parts), channels // heads, h, 1) for h in range(inner)
+    ]
     gated = []
     for r in range(own_rows):
         rows = slice(r * sequences, (r + 1) * sequences)
-        spread = jnp.concatenate(
-            [(query[rows] * mask[h : h + 1]).astype(BF16) for h in range(heads)], 0
-        )
-        weights, scale = softmax_parts(dot_t(spread, key[rows]))
-        whole = dot(weights, value[rows]) * scale
-        mixed = whole[:sequences] * mask[:1]
-        for h in range(1, heads):
-            mixed += whole[h * sequences : (h + 1) * sequences] * mask[h : h + 1]
-        gated.append((gate[rows] * mixed).astype(BF16))
+        mixed = []
+        for part in parts:
+            spread = [picked([query[rows, part]], [mask]).astype(BF16) for mask in masks]
+            weights, scale = softmax_parts(dot_t(jnp.concatenate(spread, 0), key[rows, part]))
+            whole = dot(weights, value[rows, part]) * scale
+            mixed.append(
+                picked(
+                    [whole[h * sequences : (h + 1) * sequences] for h in range(inner)], masks
+                )
+            )
+        gated.append((gate[rows] * jnp.concatenate(mixed, 1)).astype(BF16))
     after = start + dot(jnp.concatenate(gated, 0), readout_ref[...])
     normed = normalized(after, -1).astype(BF16)
     width = factor_ref.shape[0] // 2
@@ -239,7 +297,22 @@
     out_ref[...] = dot(to_sequences, after.astype(BF16)).astype(BF16).reshape(out_ref.shape)
 
 
-def spread_kernel(aligned_ref, left_ref, weight_ref, out_ref, final_ref, sem, *, own_rows, per):
+def half_update(right, spread, own_rows):
+    groups, tall, lanes = right.shape
+    columns = spread.shape[1] * own_rows // tall
+    whole = dot(right.reshape(groups * tall, lanes), spread).reshape(groups, tall, -1)
+    total = whole[:, :own_rows, :columns]
+    for e in range(1, tall // own_rows):
+        total = total + whole[
+            :, e * own_rows : (e + 1) * own_rows, e * columns : (e + 1) * columns
+        ]
+    return total
+
+
+def spread_kernel(
+    aligned_ref, right_ref, left_ref, weight_ref, out_ref, half_ref, final_ref, sem,
+    *, own_rows, per,
+):
     store = pltpu.make_async_copy(aligned_ref, final_ref, sem)
     store.start()
     size, width = left_ref.shape
@@ -250,31 +323,26 @@
     product = dot(left_ref[...], weight_ref[...])
     for d in range(width):
         f, t, e = d // part, d % part // per, d % per
-        at = ((e * (part // per) + t) * fold + f) * sequences
+        at = (t * fold + f) * sequences
         for r in range(own_rows):
-            out_ref[at : at + sequences, r * channels : (r + 1) * channels] = product[
+            to = (e * own_rows + r) * channels
+            out_ref[at : at + sequences, to : to + channels] = product[
                 r * sequences : (r + 1) * sequences, d * channels : (d + 1) * channels
             ].astype(BF16)
+    half_ref[...] = half_update(right_ref[...], out_ref[...], own_rows)
     store.wait()
 
 
 def pair_kernel(
-    second_ref, right_ref, other_ref, spread_ref, pair_ref, weight_ref, gate_weight_ref,
+    second_ref, half_ref, other_ref, spread_ref, pair_ref, weight_ref, gate_weight_ref,
     one_ref, gate_ref, out_ref,
     *, sequences,
 ):
     own_rows, columns, channels = pair_ref.shape
-    first, second = ordered(
-        second_ref[0], right_ref[...].astype(F32), other_ref[...].astype(F32)
-    )
-    right = [
-        jnp.concatenate([first[:, e : e + own_rows], second[:, e : e + own_rows]], 1).reshape(
-            columns, right_ref.shape[-1]
-        )
-        for e in range(0, right_ref.shape[1], own_rows)
-    ]
-    right = jnp.concatenate(right, 1).astype(BF16)
-    update = dot(right, spread_ref[...]) * (1.0 / sequences)
+    halves = ordered(
+        second_ref[0], half_ref[...], half_update(other_ref[...], spread_ref[...], own_rows)
+    )
+    update = jnp.concatenate(halves, 1).reshape(columns, own_rows * channels) * (1.0 / sequences)
     ones = [
         pair_ref[i].astype(F32) + update[:, i * channels : (i + 1) * channels]
         for i in range(own_rows)
@@ -378,7 +446,7 @@
         [
             ((2 * own_sequences, length // 2 * heads, length), F32),
             ((2 * rows, channels), BF16),
-            ((rows, channels), F32),
+            ((rows * max(1, 8 // own_rows), channels), F32),
             ((rows, channels), F32),
             ((channels, channels), BF16),
             ((width * own_rows, own_rows * channels), BF16),
@@ -402,7 +470,7 @@
         fetched=(1, 3, 4, 6, 7, 8, 9),
     )
     (after_rows,) = kernel_call(
-        functools.partial(row_mix_kernel, heads=heads),
+        functools.partial(row_mix_kernel, heads=heads, own_rows=own_rows),
         [((half, 2 * own_sequences * own_rows, channels), BF16)],
         (scores, bias, value, gate, start, readout),
         "row_mix",
@@ -423,14 +491,17 @@
     other = from_other_core(right)
     inside = pl.BlockSpec(memory_space=pltpu.VMEM)
     outside = pl.BlockSpec(memory_space=pl.ANY)
-    spread, alignment_output = pl.pallas_call(
+    spread, update, alignment_output = pl.pallas_call(
         functools.partial(spread_kernel, own_rows=own_rows, per=per),
         out_shape=(
-            jax.ShapeDtypeStruct((width * sequences, own_rows * pair_channels), BF16),
+            jax.ShapeDtypeStruct(
+                (width * sequences // per, per * own_rows * pair_channels), BF16
+            ),
+            jax.ShapeDtypeStruct((half, own_rows, own_rows * pair_channels), F32),
             jax.ShapeDtypeStruct(aligned.shape, BF16),
         ),
-        in_specs=[inside] * 3,
-        out_specs=(inside, outside),
+        in_specs=[inside] * 4,
+        out_specs=(inside, inside, outside),
         scratch_shapes=[pltpu.SemaphoreType.DMA],
         compiler_params=pltpu.CompilerParams(vmem_limit_bytes=VMEM_BYTES),
         cost_estimate=pl.CostEstimate(
@@ -439,7 +510,7 @@
             transcendentals=0,
         ),
         name="spread",
-    )(aligned, left, outer_output_weight.reshape(width, width * pair_channels))
+    )(aligned, right, left, outer_output_weight.reshape(width, width * pair_channels))
     pair_one, gate_out, both = kernel_call(
         functools.partial(pair_kernel, sequences=sequences),
         [
@@ -449,7 +520,7 @@
         ],
         (
             second,
-            right,
+            update,
             other,
             spread,
             pair,

time: 73.9 us -> 73.1 us (0.989)
    pallas_call x7, Pallas kernels: 10.5 us -> 9.74 us  [kernel_call(): pl.pallas_call(fetching if fetched else body, out_shape=tuple((jax.ShapeD...]
  transfers between devices with their start and end apart: 4 -> 4, of which waited for: 3 -> 3; matrix products, arithmetic and copies ran while one was open for 0% -> 0% of each run, Pallas kernels for 4% -> 5%
where the time goes in v5:
time: 73.1 us; the launch traced here: 72.7 us
  blocking collectives  46.9 us (64%)
  Pallas kernels  10.8 us (15%)
  starting transfers between devices  8.9 us (12%)
  waiting for transfers between devices  5.1 us (7%)
  between operations  0.8 us (1%)
    all_to_all x2, blocking collectives, among_class(): return lax.all_to_all(x, 'res', 0, 0, axis_index_groups=groups, tiled=True)  23.5 us
    all_to_all x2, blocking collectives, exchanged(): return lax.all_to_all(x, 'res', split_axis=0, concat_axis=0, tiled=True)  23.4 us
    pallas_call x7, Pallas kernels, kernel_call(): pl.pallas_call(fetching if fetched else body, out_shape=tuple((jax.ShapeD...  9.74 us
    all_to_all x1, starting transfers between devices, among_class(): return lax.all_to_all(x, 'res', 0, 0, axis_index_groups=groups, tiled=True)  8.32 us
    all_to_all x1, waiting for transfers between devices, among_class(): return lax.all_to_all(x, 'res', 0, 0, axis_index_groups=groups, tiled=True)  3.84 us
  transfers between devices with their start and end apart: 4, of which 3 were waited for; matrix products, arithmetic and copies ran while one was open for 0% of the time, Pallas kernels for 5%

profile of v5, /device:TPU:0, one launch (start us, length us, event | category | flops | bytes accessed | tf_op | source)
XLA Modules:
  0.0 72.7 jit_solution(1102425871129665230)
XLA Ops:
  0.6 0.0 copy-start.1
  0.6 0.0 copy-start.2
  0.7 0.0 copy-start.3
  0.7 2.0 %bias.1 = bf16[16,32,128]{2,1,0:T(8,128)(2,1)} custom-call(bf16[4,128,128]{2,1,0:T(8,128)(2,1)} %pair_ref.1, bf16[8,128]{1,0:T(8,128)(2,1)} %bitcast.8), custom_call_target="tpu_custom_call" | custom-call | tf_op jit(solution)/shard_map/bias/pallas_call | solution.py:86
  2.7 8.3 %all-to-all-start = ((bf16[16,32,128]{2,1,0:T(8,128)(2,1)}), bf16[16,32,128]{2,1,0:T(8,128)(2,1)S(1)}, u32[]{:S(2)}, u32[]{:S(2)}) async-start(bf16[16,32,128]{2,1,0:T(8,128)(2,1)} %bias.1), calls=%async_computation | async-start | bytes 262144 | tf_op jit(solution)/shard_map/all_to_all | solution.py:430
  11.0 0.1 collective-permute-start.1
  11.1 0.5 collective-permute-start
  11.6 1.0 %collective-permute-done.refs_2_ = s32[2,128]{1,0:T(2,128)S(1)} collective-permute-done((s32[2,128]{1,0:T(2,128)}, s32[2,128]{1,0:T(2,128)S(1)}, u32[]{:S(2)}, u32[]{:S(2)}) %collective-permute-start) | collective-permute-done | bytes 1056 | tf_op jit(solution)/shard_map/ppermute | solution.py:433
  12.6 0.0 collective-permute-done.1.refs_5_
  12.6 2.3 %row_scores.1 = (f32[4,512,128]{2,1,0:T(8,128)S(1)}, bf16[512,256]{1,0:T(8,128)(2,1)S(1)}, f32[512,256]{1,0:T(8,128)S(1)}, f32[256,256]{1,0:T(8,128)S(1)}, bf16[...) custom-call(s32[1]{0:T(128)} %bitcast.refs_0_.second_ref, s32[2,128]{1,0:T(2,128)} %refs_1_.1, ...), custom_call_target="tpu_custom_call" | custom-call | flops 134217728 | bytes 2097152 | tf_op jit(solution)/shard_map/row_scores/pallas_call | solution.py:86
  15.0 3.8 %all-to-all-done.bias_ref = bf16[16,32,128]{2,1,0:T(8,128)(2,1)S(1)} async-done(((bf16[16,32,128]{2,1,0:T(8,128)(2,1)}), bf16[16,32,128]{2,1,0:T(8,128)(2,1)S(1)}, u32[]{:S(2)}, u32[]{:S(2)}) %all-to-all-start) | async-done | bytes 131104 | tf_op jit(solution)/shard_map/all_to_all | solution.py:430
  18.8 0.0 copy-start.5
  18.8 1.0 %row_mix.1 = bf16[16,16,256]{2,1,0:T(8,128)(2,1)S(1)} custom-call(f32[4,512,128]{2,1,0:T(8,128)S(1)} %get-tuple-element.17.scores_ref, bf16[16,32,128]{2,1,0:T(8,128)(2,1)S(1)} %all-to-all-done.bias_ref, bf16[512,256]{1,0:T(8,128)(2,1)S(1)} %get-tuple-element.18.value_ref, f32[512,256]{1,0:T(8,128)S(1)} %get-tuple-element.19.gate_ref, ...), custom_call_target="tpu_custom_call" | custom-call | tf_op jit(solution)/shard_map/row_mix/pallas_call | solution.py:86
  19.8 0.0 slice-start
  19.8 0.0 copy-start.6
  19.8 0.0 copy-start
  19.8 10.9 %all_to_all.25.state_ref = bf16[16,16,256]{2,1,0:T(8,128)(2,1)S(1)} all-to-all(bf16[16,16,256]{2,1,0:T(8,128)(2,1)S(1)} %row_mix.1), channel_id=1, replica_groups={{0,2,4,6,8,10,12,14,16,18,20,22,24,26,28,30},{1,3,5,7,9,11,13,15,17,19,..., dimensions={0} | all-to-all | bytes 262144 | tf_op jit(solution)/shard_map/all_to_all | solution.py:430
  30.7 0.0 copy-done.1
  30.7 0.0 copy-done.2
  30.7 0.0 copy-done.3
  30.7 1.8 %column.1 = (bf16[64,4,256]{2,1,0:T(4,128)(2,1)S(1)}, bf16[256,32]{1,0:T(8,128)(2,1)S(1)}, bf16[16,8,1024]{2,1,0:T(8,128)(2,1)S(1)}) custom-call(bf16[16,16,256]{2,1,0:T(8,128)(2,1)S(1)} %all_to_all.25.state_ref, bf16[256,1024]{1,0:T(8,128)(2,1)S(1)} %copy-done.1, bf16[256,256]{1,0:T(8,128)(2,1)S(1)} %copy-done.2, bf16[64,256]{1,0:T(8,128)(2,1)S(1)} %bitcast.7, ...), custom_call_target="tpu_custom_call" | custom-call | tf_op jit(solution)/shard_map/column/pallas_call | solution.py:86
  32.5 12.7 %all_to_all.26.right_ref = bf16[16,8,1024]{2,1,0:T(8,128)(2,1)S(1)} all-to-all(bf16[16,8,1024]{2,1,0:T(8,128)(2,1)S(1)} %get-tuple-element.24), channel_id=1, replica_groups={{0,2,4,6,8,10,12,14,16,18,20,22,24,26,28,30},{1,3,5,7,9,11,13,15,17,19,..., dimensions={0} | all-to-all | bytes 524288 | tf_op jit(solution)/shard_map/all_to_all | solution.py:430
  45.2 0.0 collective-permute-start.2
  45.2 0.0 copy-done.5
  45.2 0.0 slice-done
  45.2 0.1 copy.17
  45.3 0.0 copy-done.6
  45.3 0.1 reshape.15.weight_ref
  45.5 1.0 %spread.1 = (bf16[1024,1024]{1,0:T(8,128)(2,1)S(1)}, f32[16,4,512]{2,1,0:T(4,128)S(1)}, bf16[64,4,256]{2,1,0:T(4,128)(2,1)}) custom-call(bf16[64,4,256]{2,1,0:T(4,128)(2,1)S(1)} %get-tuple-element.23.aligned_ref, bf16[16,8,1024]{2,1,0:T(8,128)(2,1)S(1)} %all_to_all.26.right_ref, bf16[256,32]{1,0:T(8,128)(2,1)S(1)} %get-tuple-element.25.left_ref, ...), custom_call_target="tpu_custom_call" | custom-call | flops 67108864 | bytes 2097152 | tf_op jit(solution)/shard_map/spread/pallas_call | solution.py:494
  46.5 0.0 copy-start.4
  46.5 0.2 collective-permute-done.2.other_ref
  46.7 0.0 copy-done
  46.7 1.0 %pair.1 = (f32[512,128]{1,0:T(8,128)S(1)}, f32[512,128]{1,0:T(8,128)S(1)}, bf16[32,4,1024]{2,1,0:T(4,128)(2,1)S(1)}) custom-call(s32[1]{0:T(128)} %bitcast.refs_0_.second_ref, f32[16,4,512]{2,1,0:T(4,128)S(1)} %get-tuple-element.27.half_ref, bf16[16,8,1024]{2,1,0:T(8,128)(2,1)S(1)} %collective-permute-done.2.other_ref, ...), custom_call_target="tpu_custom_call" | custom-call | tf_op jit(solution)/shard_map/pair/pallas_call | solution.py:86
  47.7 12.9 %all_to_all.27.both_ref = bf16[32,4,1024]{2,1,0:T(4,128)(2,1)S(1)} all-to-all(bf16[32,4,1024]{2,1,0:T(4,128)(2,1)S(1)} %get-tuple-element.29), channel_id=1, replica_groups=mesh['crop'=1,'res'=32] {'res'}, dimensions={0} | all-to-all | bytes 524288 | tf_op jit(solution)/shard_map/all_to_all | solution.py:397
  60.6 0.7 triangle.1
  61.3 10.4 %all_to_all.28.back_ref = bf16[32,4,512]{2,1,0:T(4,128)(2,1)S(1)} all-to-all(bf16[32,4,512]{2,1,0:T(4,128)(2,1)S(1)} %triangle.1), channel_id=1, replica_groups=mesh['crop'=1,'res'=32] {'res'}, dimensions={0} | all-to-all | bytes 262144 | tf_op jit(solution)/shard_map/all_to_all | solution.py:397
  71.8 0.0 copy-done.4
  71.8 1.0 %final.1 = bf16[4,128,128]{2,1,0:T(8,128)(2,1)} custom-call(bf16[32,4,512]{2,1,0:T(4,128)(2,1)S(1)} %all_to_all.28.back_ref, f32[512,128]{1,0:T(8,128)S(1)} %get-tuple-element.30.one_ref, f32[512,128]{1,0:T(8,128)S(1)} %get-tuple-element.31.gate_ref, bf16[128,128]{1,0:T(8,128)(2,1)S(1)} %copy-done.4), custom_call_target="tpu_custom_call" | custom-call | tf_op jit(solution)/shard_map/final/pallas_call | solution.py:86
  (1 shorter events, 0.0 us)
Async XLA Ops:
  0.6 30.0 %copy-start.1 = (bf16[256,1024]{1,0:T(8,128)(2,1)S(1)}, bf16[256,1024]{1,0:T(8,128)(2,1)}, u32[]{:S(2)}) copy-start(bf16[256,1024]{1,0:T(8,128)(2,1)} %weight_ref.2) | copy-start | bytes 1572868
  0.6 30.0 %copy-start.2 = (bf16[256,256]{1,0:T(8,128)(2,1)S(1)}, bf16[256,256]{1,0:T(8,128)(2,1)}, u32[]{:S(2)}) copy-start(bf16[256,256]{1,0:T(8,128)(2,1)} %readout_ref.1) | copy-start | bytes 393220
  0.7 30.0 %copy-start.3 = (bf16[256,64]{0,1:T(8,128)(2,1)S(1)}, bf16[256,64]{0,1:T(8,128)(2,1)}, u32[]{:S(2)}) copy-start(bf16[256,64]{0,1:T(8,128)(2,1)} %param.24) | copy-start | bytes 98308
  2.7 16.1 %all-to-all-start = ((bf16[16,32,128]{2,1,0:T(8,128)(2,1)}), bf16[16,32,128]{2,1,0:T(8,128)(2,1)S(1)}, u32[]{:S(2)}, u32[]{:S(2)}) async-start(bf16[16,32,128]{2,1,0:T(8,128)(2,1)} %bias.1), calls=%async_computation | async-start | bytes 262144 | tf_op jit(solution)/shard_map/all_to_all | solution.py:430
  11.0 1.6 %collective-permute-start.1 = (bf16[2,128,256]{2,1,0:T(8,128)(2,1)}, bf16[2,128,256]{2,1,0:T(8,128)(2,1)S(1)}, u32[]{:S(2)}, u32[]{:S(2)}) collective-permute-start(bf16[2,128,256]{2,1,0:T(8,128)(2,1)} %refs_4_.1), channel_id=1, source_target_pairs={{0,1},{1,0},{2,3},{3,2},{4,5},{5,4},{6,7},{7,6},{8,9},{9,8},{10,11... | collective-permute-start | bytes 393224 | tf_op jit(solution)/shard_map/ppermute | solution.py:433
  11.1 1.5 %collective-permute-start = (s32[2,128]{1,0:T(2,128)}, s32[2,128]{1,0:T(2,128)S(1)}, u32[]{:S(2)}, u32[]{:S(2)}) collective-permute-start(s32[2,128]{1,0:T(2,128)} %refs_1_.1), channel_id=1, source_target_pairs={{0,1},{1,0},{2,3},{3,2},{4,5},{5,4},{6,7},{7,6},{8,9},{9,8},{10,11... | collective-permute-start | bytes 3080 | tf_op jit(solution)/shard_map/ppermute | solution.py:433
  18.8 26.4 %copy-start.5 = (bf16[128,640]{1,0:T(8,128)(2,1)S(1)}, bf16[128,640]{1,0:T(8,128)(2,1)}, u32[]{:S(2)}) copy-start(bf16[128,640]{1,0:T(8,128)(2,1)} %param.26) | copy-start | bytes 491524
  19.8 25.4 %slice-start = ((bf16[128,640]{1,0:T(8,128)(2,1)}), bf16[128,512]{1,0:T(8,128)(2,1)S(1)}, s32[]{:S(2)}) async-start(bf16[128,640]{1,0:T(8,128)(2,1)} %param.26), calls=%async_computation.5 | async-start | bytes 262144 | tf_op jit(solution)/shard_map/slice | solution.py:527
  19.8 25.5 %copy-start.6 = (bf16[1024,128]{1,0:T(8,128)(2,1)S(1)}, bf16[1024,128]{1,0:T(8,128)(2,1)}, u32[]{:S(2)}) copy-start(bf16[1024,128]{1,0:T(8,128)(2,1)} %param.25) | copy-start | bytes 786436
  19.8 26.9 %copy-start = (bf16[4,128,128]{2,1,0:T(8,128)(2,1)S(1)}, bf16[4,128,128]{2,1,0:T(8,128)(2,1)}, u32[]{:S(2)}) copy-start(bf16[4,128,128]{2,1,0:T(8,128)(2,1)} %pair_ref.1) | copy-start | bytes 393220
  45.2 1.5 %collective-permute-start.2 = (bf16[16,8,1024]{2,1,0:T(8,128)(2,1)S(1)}, bf16[16,8,1024]{2,1,0:T(8,128)(2,1)S(1)}, u32[]{:S(2)}, u32[]{:S(2)}) collective-permute-start(bf16[16,8,1024]{2,1,0:T(8,128)(2,1)S(1)} %all_to_all.26.right_ref), channel_id=1, source_target_pairs={{0,1},{1,0},{2,3},{3,2},{4,5},{5,4},{6,7},{7,6},{8,9},{9,8},{10,11... | collective-permute-start | bytes 786440 | tf_op jit(solution)/shard_map/ppermute | solution.py:433
  46.5 25.3 %copy-start.4 = (bf16[128,128]{1,0:T(8,128)(2,1)S(1)}, bf16[128,128]{1,0:T(8,128)(2,1)}, u32[]{:S(2)}) copy-start(bf16[128,128]{1,0:T(8,128)(2,1)} %weight_ref.3) | copy-start | bytes 98308

commit v6 on v5

--- a/solution.py
+++ b/solution.py
@@ -62,7 +62,7 @@
     return total
 
 
-def kernel_call(body, outs, args, name, flops=0, nbytes=0, scalars=0, fetched=()):
+def kernel_call(body, outs, args, name, flops=0, nbytes=0, scalars=0, fetched=(), scratch=()):
     inside = pl.BlockSpec(memory_space=pltpu.VMEM)
     outside = pl.BlockSpec(memory_space=pl.ANY)
     scalar = pl.BlockSpec(memory_space=pltpu.SMEM)
@@ -82,7 +82,9 @@
             copy.wait()
         body(*refs)
 
-    scratch = [pltpu.VMEM(args[i].shape, args[i].dtype) for i in fetched]
+    held = [pltpu.VMEM(args[i].shape, args[i].dtype) for i in fetched]
+    if fetched:
+        held.append(pltpu.SemaphoreType.DMA((len(fetched),)))
     return pl.pallas_call(
         fetching if fetched else body,
         out_shape=tuple(jax.ShapeDtypeStruct(s, d) for s, d in outs),
@@ -91,7 +93,7 @@
             for i in range(len(args))
         ],
         out_specs=(inside,) * len(outs),
-        scratch_shapes=scratch + [pltpu.SemaphoreType.DMA((len(fetched),))] if fetched else [],
+        scratch_shapes=held + list(scratch),
         compiler_params=pltpu.CompilerParams(vmem_limit_bytes=VMEM_BYTES),
         cost_estimate=pl.CostEstimate(flops=flops, bytes_accessed=nbytes, transcendentals=0),
         name=name,
@@ -358,31 +360,55 @@
     out_ref[...] = both.reshape(out_ref.shape)
 
 
-def triangle_kernel(both_ref, out_ref, *, own_rows):
+def triangle_kernel(both_ref, out_ref, left_ref, right_ref, ordered_ref, *, own_rows):
     devices, own_channels, lanes = both_ref.shape
     columns = lanes // 2 // own_rows
     size = devices * own_channels
-    both = both_ref[...].reshape(size, lanes)
-    left = jnp.concatenate([both[:, i * columns : (i + 1) * columns] for i in range(own_rows)], 0)
-    right = jnp.concatenate(
-        [both[:, (own_rows + i) * columns : (own_rows + i + 1) * columns] for i in range(own_rows)],
-        0,
-    )
-    total = size * own_rows
-    order = selector(
-        total,
-        lambda p: p % own_rows * size + p % columns // own_rows * own_channels + p // columns,
-    )
-    right = dot(order, right).astype(BF16)
-    channel = iota((total, 1), 0) % own_channels
-    combined = jnp.zeros((total, columns), F32)
+    tile = left_ref.shape[2]
+    tiles = columns // tile
+    both = both_ref[...].reshape(size, lanes).astype(F32)
+    for i in range(own_rows):
+        rows = slice(i * size, (i + 1) * size)
+        for k in range(tiles):
+            at = i * columns + k * tile
+            left_ref[k, rows] = both[:, at : at + tile]
+            at += own_rows * columns
+            right_ref[k, rows] = both[:, at : at + tile]
+
+    def channel_rows(c, i):
+        return pl.ds(i * size + c, devices, stride=own_channels)
+
+    for k in range(tiles):
+        for c in range(own_channels):
+            for i in range(own_rows):
+                ordered_ref[k, pl.ds(c * columns + i, devices, stride=own_rows), :] = right_ref[
+                    k, channel_rows(c, i), :
+                ]
     for c in range(own_channels):
-        part = dot_t(left, right[c * columns : (c + 1) * columns])
-        combined = jnp.where(channel == c, part, combined)
-    combined = combined.astype(BF16)
-    out_ref[...] = jnp.concatenate(
-        [combined[i * size : (i + 1) * size] for i in range(own_rows)], 1
-    ).reshape(out_ref.shape)
+        combined = jnp.zeros((columns, columns), F32)
+        for k in range(tiles):
+            left = jnp.concatenate(
+                [left_ref[k, channel_rows(c, i), :] for i in range(own_rows)], 0
+            )
+            right = ordered_ref[k, c * columns : (c + 1) * columns]
+            combined = combined + dot_t(left.astype(BF16), right.astype(BF16))
+        for i in range(own_rows):
+            for k in range(tiles):
+                right_ref[k, channel_rows(c, i), :] = combined[
+                    i * devices : (i + 1) * devices, k * tile : (k + 1) * tile
+                ]
+    out_ref[...] = (
+        jnp.concatenate(
+            [
+                right_ref[k, i * size : (i + 1) * size]
+                for i in range(own_rows)
+                for k in range(tiles)
+            ],
+            1,
+        )
+        .astype(BF16)
+        .reshape(out_ref.shape)
+    )
 
 
 def final_kernel(back_ref, one_ref, gate_ref, weight_ref, out_ref):
@@ -536,6 +562,10 @@
         [((devices, own_channels, own_rows * columns), BF16)],
         (both,),
         "triangle",
+        scratch=[
+            pltpu.VMEM((-(-columns // 128), pair_channels * own_rows, min(columns, 128)), F32)
+        ]
+        * 3,
     )
     back = exchanged(combined)
     (pair_output,) = kernel_call(

time: 73.1 us -> 72.7 us (level)
  no operation moved by 1% of the time
where the time goes in v6:
time: 72.7 us; the launch traced here: 72.3 us
  blocking collectives  46.9 us (65%)
  Pallas kernels  10.3 us (14%)
  starting transfers between devices  8.9 us (12%)
  waiting for transfers between devices  5.1 us (7%)
  between operations  0.8 us (1%)
    all_to_all x2, blocking collectives, among_class(): return lax.all_to_all(x, 'res', 0, 0, axis_index_groups=groups, tiled=True)  23.5 us
    all_to_all x2, blocking collectives, exchanged(): return lax.all_to_all(x, 'res', split_axis=0, concat_axis=0, tiled=True)  23.4 us
    pallas_call x7, Pallas kernels, kernel_call(): pl.pallas_call(fetching if fetched else body, out_shape=tuple((jax.ShapeD...  9.3 us
    all_to_all x1, starting transfers between devices, among_class(): return lax.all_to_all(x, 'res', 0, 0, axis_index_groups=groups, tiled=True)  8.32 us
    all_to_all x1, waiting for transfers between devices, among_class(): return lax.all_to_all(x, 'res', 0, 0, axis_index_groups=groups, tiled=True)  3.84 us
  transfers between devices with their start and end apart: 4, of which 3 were waited for; matrix products, arithmetic and copies ran while one was open for 0% of the time, Pallas kernels for 5%

profile of v6, /device:TPU:0, one launch (start us, length us, event | category | flops | bytes accessed | tf_op | source)
XLA Modules:
  0.0 72.3 jit_solution(14925181636087070347)
XLA Ops:
  0.6 0.0 copy-start.1
  0.6 0.0 copy-start.2
  0.7 0.0 copy-start.3
  0.7 2.0 %bias.1 = bf16[16,32,128]{2,1,0:T(8,128)(2,1)} custom-call(bf16[4,128,128]{2,1,0:T(8,128)(2,1)} %pair_ref.1, bf16[8,128]{1,0:T(8,128)(2,1)} %bitcast.8), custom_call_target="tpu_custom_call" | custom-call | tf_op jit(solution)/shard_map/bias/pallas_call | solution.py:88
  2.7 8.3 %all-to-all-start = ((bf16[16,32,128]{2,1,0:T(8,128)(2,1)}), bf16[16,32,128]{2,1,0:T(8,128)(2,1)S(1)}, u32[]{:S(2)}, u32[]{:S(2)}) async-start(bf16[16,32,128]{2,1,0:T(8,128)(2,1)} %bias.1), calls=%async_computation | async-start | bytes 262144 | tf_op jit(solution)/shard_map/all_to_all | solution.py:456
  11.0 0.1 collective-permute-start.1
  11.1 0.5 collective-permute-start
  11.6 1.0 %collective-permute-done.refs_2_ = s32[2,128]{1,0:T(2,128)S(1)} collective-permute-done((s32[2,128]{1,0:T(2,128)}, s32[2,128]{1,0:T(2,128)S(1)}, u32[]{:S(2)}, u32[]{:S(2)}) %collective-permute-start) | collective-permute-done | bytes 1056 | tf_op jit(solution)/shard_map/ppermute | solution.py:459
  12.6 0.0 collective-permute-done.1.refs_5_
  12.6 2.3 %row_scores.1 = (f32[4,512,128]{2,1,0:T(8,128)S(1)}, bf16[512,256]{1,0:T(8,128)(2,1)S(1)}, f32[512,256]{1,0:T(8,128)S(1)}, f32[256,256]{1,0:T(8,128)S(1)}, bf16[...) custom-call(s32[1]{0:T(128)} %bitcast.refs_0_.second_ref, s32[2,128]{1,0:T(2,128)} %refs_1_.1, ...), custom_call_target="tpu_custom_call" | custom-call | flops 134217728 | bytes 2097152 | tf_op jit(solution)/shard_map/row_scores/pallas_call | solution.py:88
  15.0 3.8 %all-to-all-done.bias_ref = bf16[16,32,128]{2,1,0:T(8,128)(2,1)S(1)} async-done(((bf16[16,32,128]{2,1,0:T(8,128)(2,1)}), bf16[16,32,128]{2,1,0:T(8,128)(2,1)S(1)}, u32[]{:S(2)}, u32[]{:S(2)}) %all-to-all-start) | async-done | bytes 131104 | tf_op jit(solution)/shard_map/all_to_all | solution.py:456
  18.8 0.0 copy-start.5
  18.8 1.0 %row_mix.1 = bf16[16,16,256]{2,1,0:T(8,128)(2,1)S(1)} custom-call(f32[4,512,128]{2,1,0:T(8,128)S(1)} %get-tuple-element.17.scores_ref, bf16[16,32,128]{2,1,0:T(8,128)(2,1)S(1)} %all-to-all-done.bias_ref, bf16[512,256]{1,0:T(8,128)(2,1)S(1)} %get-tuple-element.18.value_ref, f32[512,256]{1,0:T(8,128)S(1)} %get-tuple-element.19.gate_ref, ...), custom_call_target="tpu_custom_call" | custom-call | tf_op jit(solution)/shard_map/row_mix/pallas_call | solution.py:88
  19.8 0.0 slice-start
  19.8 0.0 copy-start.6
  19.8 0.0 copy-start
  19.8 10.9 %all_to_all.25.state_ref = bf16[16,16,256]{2,1,0:T(8,128)(2,1)S(1)} all-to-all(bf16[16,16,256]{2,1,0:T(8,128)(2,1)S(1)} %row_mix.1), channel_id=1, replica_groups={{0,2,4,6,8,10,12,14,16,18,20,22,24,26,28,30},{1,3,5,7,9,11,13,15,17,19,..., dimensions={0} | all-to-all | bytes 262144 | tf_op jit(solution)/shard_map/all_to_all | solution.py:456
  30.7 0.0 copy-done.1
  30.7 0.0 copy-done.2
  30.7 0.0 copy-done.3
  30.7 1.8 %column.1 = (bf16[64,4,256]{2,1,0:T(4,128)(2,1)S(1)}, bf16[256,32]{1,0:T(8,128)(2,1)S(1)}, bf16[16,8,1024]{2,1,0:T(8,128)(2,1)S(1)}) custom-call(bf16[16,16,256]{2,1,0:T(8,128)(2,1)S(1)} %all_to_all.25.state_ref, bf16[256,1024]{1,0:T(8,128)(2,1)S(1)} %copy-done.1, bf16[256,256]{1,0:T(8,128)(2,1)S(1)} %copy-done.2, bf16[64,256]{1,0:T(8,128)(2,1)S(1)} %bitcast.7, ...), custom_call_target="tpu_custom_call" | custom-call | tf_op jit(solution)/shard_map/column/pallas_call | solution.py:88
  32.5 12.7 %all_to_all.26.right_ref = bf16[16,8,1024]{2,1,0:T(8,128)(2,1)S(1)} all-to-all(bf16[16,8,1024]{2,1,0:T(8,128)(2,1)S(1)} %get-tuple-element.24), channel_id=1, replica_groups={{0,2,4,6,8,10,12,14,16,18,20,22,24,26,28,30},{1,3,5,7,9,11,13,15,17,19,..., dimensions={0} | all-to-all | bytes 524288 | tf_op jit(solution)/shard_map/all_to_all | solution.py:456
  45.2 0.0 collective-permute-start.2
  45.2 0.0 copy-done.5
  45.2 0.0 slice-done
  45.2 0.1 copy.17
  45.3 0.0 copy-done.6
  45.3 0.1 reshape.15.weight_ref
  45.5 1.0 %spread.1 = (bf16[1024,1024]{1,0:T(8,128)(2,1)S(1)}, f32[16,4,512]{2,1,0:T(4,128)S(1)}, bf16[64,4,256]{2,1,0:T(4,128)(2,1)}) custom-call(bf16[64,4,256]{2,1,0:T(4,128)(2,1)S(1)} %get-tuple-element.23.aligned_ref, bf16[16,8,1024]{2,1,0:T(8,128)(2,1)S(1)} %all_to_all.26.right_ref, bf16[256,32]{1,0:T(8,128)(2,1)S(1)} %get-tuple-element.25.left_ref, ...), custom_call_target="tpu_custom_call" | custom-call | flops 67108864 | bytes 2097152 | tf_op jit(solution)/shard_map/spread/pallas_call | solution.py:520
  46.5 0.0 copy-start.4
  46.5 0.2 collective-permute-done.2.other_ref
  46.7 0.0 copy-done
  46.7 1.0 %pair.1 = (f32[512,128]{1,0:T(8,128)S(1)}, f32[512,128]{1,0:T(8,128)S(1)}, bf16[32,4,1024]{2,1,0:T(4,128)(2,1)S(1)}) custom-call(s32[1]{0:T(128)} %bitcast.refs_0_.second_ref, f32[16,4,512]{2,1,0:T(4,128)S(1)} %get-tuple-element.27.half_ref, bf16[16,8,1024]{2,1,0:T(8,128)(2,1)S(1)} %collective-permute-done.2.other_ref, ...), custom_call_target="tpu_custom_call" | custom-call | tf_op jit(solution)/shard_map/pair/pallas_call | solution.py:88
  47.7 12.9 %all_to_all.27.both_ref = bf16[32,4,1024]{2,1,0:T(4,128)(2,1)S(1)} all-to-all(bf16[32,4,1024]{2,1,0:T(4,128)(2,1)S(1)} %get-tuple-element.29), channel_id=1, replica_groups=mesh['crop'=1,'res'=32] {'res'}, dimensions={0} | all-to-all | bytes 524288 | tf_op jit(solution)/shard_map/all_to_all | solution.py:423
  60.6 0.3 triangle.1
  60.9 10.4 %all_to_all.28.back_ref = bf16[32,4,512]{2,1,0:T(4,128)(2,1)S(1)} all-to-all(bf16[32,4,512]{2,1,0:T(4,128)(2,1)S(1)} %triangle.1), channel_id=1, replica_groups=mesh['crop'=1,'res'=32] {'res'}, dimensions={0} | all-to-all | bytes 262144 | tf_op jit(solution)/shard_map/all_to_all | solution.py:423
  71.3 0.0 copy-done.4
  71.3 1.0 %final.1 = bf16[4,128,128]{2,1,0:T(8,128)(2,1)} custom-call(bf16[32,4,512]{2,1,0:T(4,128)(2,1)S(1)} %all_to_all.28.back_ref, f32[512,128]{1,0:T(8,128)S(1)} %get-tuple-element.30.one_ref, f32[512,128]{1,0:T(8,128)S(1)} %get-tuple-element.31.gate_ref, bf16[128,128]{1,0:T(8,128)(2,1)S(1)} %copy-done.4), custom_call_target="tpu_custom_call" | custom-call | tf_op jit(solution)/shard_map/final/pallas_call | solution.py:88
  (1 shorter events, 0.0 us)
Async XLA Ops:
  0.6 30.0 %copy-start.1 = (bf16[256,1024]{1,0:T(8,128)(2,1)S(1)}, bf16[256,1024]{1,0:T(8,128)(2,1)}, u32[]{:S(2)}) copy-start(bf16[256,1024]{1,0:T(8,128)(2,1)} %weight_ref.2) | copy-start | bytes 1572868
  0.6 30.0 %copy-start.2 = (bf16[256,256]{1,0:T(8,128)(2,1)S(1)}, bf16[256,256]{1,0:T(8,128)(2,1)}, u32[]{:S(2)}) copy-start(bf16[256,256]{1,0:T(8,128)(2,1)} %readout_ref.1) | copy-start | bytes 393220
  0.7 30.0 %copy-start.3 = (bf16[256,64]{0,1:T(8,128)(2,1)S(1)}, bf16[256,64]{0,1:T(8,128)(2,1)}, u32[]{:S(2)}) copy-start(bf16[256,64]{0,1:T(8,128)(2,1)} %param.24) | copy-start | bytes 98308
  2.7 16.1 %all-to-all-start = ((bf16[16,32,128]{2,1,0:T(8,128)(2,1)}), bf16[16,32,128]{2,1,0:T(8,128)(2,1)S(1)}, u32[]{:S(2)}, u32[]{:S(2)}) async-start(bf16[16,32,128]{2,1,0:T(8,128)(2,1)} %bias.1), calls=%async_computation | async-start | bytes 262144 | tf_op jit(solution)/shard_map/all_to_all | solution.py:456
  11.0 1.6 %collective-permute-start.1 = (bf16[2,128,256]{2,1,0:T(8,128)(2,1)}, bf16[2,128,256]{2,1,0:T(8,128)(2,1)S(1)}, u32[]{:S(2)}, u32[]{:S(2)}) collective-permute-start(bf16[2,128,256]{2,1,0:T(8,128)(2,1)} %refs_4_.1), channel_id=1, source_target_pairs={{0,1},{1,0},{2,3},{3,2},{4,5},{5,4},{6,7},{7,6},{8,9},{9,8},{10,11... | collective-permute-start | bytes 393224 | tf_op jit(solution)/shard_map/ppermute | solution.py:459
  11.1 1.5 %collective-permute-start = (s32[2,128]{1,0:T(2,128)}, s32[2,128]{1,0:T(2,128)S(1)}, u32[]{:S(2)}, u32[]{:S(2)}) collective-permute-start(s32[2,128]{1,0:T(2,128)} %refs_1_.1), channel_id=1, source_target_pairs={{0,1},{1,0},{2,3},{3,2},{4,5},{5,4},{6,7},{7,6},{8,9},{9,8},{10,11... | collective-permute-start | bytes 3080 | tf_op jit(solution)/shard_map/ppermute | solution.py:459
  18.8 26.4 %copy-start.5 = (bf16[128,640]{1,0:T(8,128)(2,1)S(1)}, bf16[128,640]{1,0:T(8,128)(2,1)}, u32[]{:S(2)}) copy-start(bf16[128,640]{1,0:T(8,128)(2,1)} %param.26) | copy-start | bytes 491524
  19.8 25.4 %slice-start = ((bf16[128,640]{1,0:T(8,128)(2,1)}), bf16[128,512]{1,0:T(8,128)(2,1)S(1)}, s32[]{:S(2)}) async-start(bf16[128,640]{1,0:T(8,128)(2,1)} %param.26), calls=%async_computation.5 | async-start | bytes 262144 | tf_op jit(solution)/shard_map/slice | solution.py:553
  19.8 25.5 %copy-start.6 = (bf16[1024,128]{1,0:T(8,128)(2,1)S(1)}, bf16[1024,128]{1,0:T(8,128)(2,1)}, u32[]{:S(2)}) copy-start(bf16[1024,128]{1,0:T(8,128)(2,1)} %param.25) | copy-start | bytes 786436
  19.8 26.9 %copy-start = (bf16[4,128,128]{2,1,0:T(8,128)(2,1)S(1)}, bf16[4,128,128]{2,1,0:T(8,128)(2,1)}, u32[]{:S(2)}) copy-start(bf16[4,128,128]{2,1,0:T(8,128)(2,1)} %pair_ref.1) | copy-start | bytes 393220
  45.2 1.5 %collective-permute-start.2 = (bf16[16,8,1024]{2,1,0:T(8,128)(2,1)S(1)}, bf16[16,8,1024]{2,1,0:T(8,128)(2,1)S(1)}, u32[]{:S(2)}, u32[]{:S(2)}) collective-permute-start(bf16[16,8,1024]{2,1,0:T(8,128)(2,1)S(1)} %all_to_all.26.right_ref), channel_id=1, source_target_pairs={{0,1},{1,0},{2,3},{3,2},{4,5},{5,4},{6,7},{7,6},{8,9},{9,8},{10,11... | collective-permute-start | bytes 786440 | tf_op jit(solution)/shard_map/ppermute | solution.py:459
  46.5 24.9 %copy-start.4 = (bf16[128,128]{1,0:T(8,128)(2,1)S(1)}, bf16[128,128]{1,0:T(8,128)(2,1)}, u32[]{:S(2)}) copy-start(bf16[128,128]{1,0:T(8,128)(2,1)} %weight_ref.3) | copy-start | bytes 98308

commit v7 on v6

--- a/solution.py
+++ b/solution.py
@@ -62,7 +62,7 @@
     return total
 
 
-def kernel_call(body, outs, args, name, flops=0, nbytes=0, scalars=0, fetched=(), scratch=()):
+def kernel_call(body, outs, args, name, flops=0, nbytes=0, scalars=0, fetched=(), late=(), scratch=()):
     inside = pl.BlockSpec(memory_space=pltpu.VMEM)
     outside = pl.BlockSpec(memory_space=pl.ANY)
     scalar = pl.BlockSpec(memory_space=pltpu.SMEM)
@@ -78,9 +78,18 @@
             copies.append(pltpu.make_async_copy(refs[i], held[k], sems.at[k]))
             copies[-1].start()
             refs[i] = held[k]
-        for copy in copies:
-            copy.wait()
-        body(*refs)
+        later = [copy for copy, i in zip(copies, fetched) if i in late]
+        for copy, i in zip(copies, fetched):
+            if i not in late:
+                copy.wait()
+        if not late:
+            return body(*refs)
+
+        def arrive():
+            for copy in later:
+                copy.wait()
+
+        return body(*refs, arrive=arrive)
 
     held = [pltpu.VMEM(args[i].shape, args[i].dtype) for i in fetched]
     if fetched:
@@ -127,12 +136,11 @@
     second_ref, ids_ref, other_ids_ref, mask_ref, state_ref, other_ref, table_ref, weight_ref,
     readout_ref, factor_ref,
     scores_ref, value_ref, gate_ref, start_ref, held_ref, wide_ref,
-    *, heads, own_rows,
+    *, heads, own_rows, arrive,
 ):
     own_sequences, length, channels = state_ref.shape
     tokens = table_ref.shape[0]
     second = second_ref[0]
-    held_ref[...] = readout_ref[...]
     ids = jnp.concatenate(ordered(second, ids_ref[...], other_ids_ref[...]), 0)
     states = jnp.concatenate(
         ordered(second, state_ref[...].astype(F32), other_ref[...].astype(F32)), 0
@@ -144,6 +152,8 @@
         starts.append(states[s] + t_dot(hot, table_ref[...]))
     start = jnp.concatenate(starts, 0)
     normed = normalized(start, -1)
+    arrive()
+    held_ref[...] = readout_ref[...]
     projected = dot(normed.astype(BF16), weight_ref[:, channels : 3 * channels])
     key = projected[:, :channels].astype(BF16)
     value_ref[...] = projected[:, channels:].astype(BF16)
@@ -255,7 +265,9 @@
     to_rows = selector(size, swapped(sequences, own_rows))
     to_sequences = selector(size, swapped(own_rows, sequences))
     start = dot(to_rows, state_ref[...].reshape(size, channels))
-    projected = dot(normalized(start, -1).astype(BF16), weight_ref[...])
+    centred = start - jnp.mean(start, -1, keepdims=True)
+    inverse = lax.rsqrt(jnp.mean(centred * centred, -1, keepdims=True) + EPSILON)
+    projected = dot(centred.astype(BF16), weight_ref[...]) * inverse
     query = (projected[:, :channels] * (channels // heads) ** (-0.5)).astype(BF16).astype(F32)
     key = projected[:, channels : 2 * channels].astype(BF16)
     value = projected[:, 2 * channels : 3 * channels].astype(BF16)
@@ -494,6 +506,7 @@
         nbytes=1 << 21,
         scalars=1,
         fetched=(1, 3, 4, 6, 7, 8, 9),
+        late=(3, 7, 8, 9),
     )
     (after_rows,) = kernel_call(
         functools.partial(row_mix_kernel, heads=heads, own_rows=own_rows),

time: 72.7 us -> 72.4 us (level)
  transfers between devices with their start and end apart: 4 -> 4, of which waited for: 3 -> 3; matrix products, arithmetic and copies ran while one was open for 0% -> 0% of each run, Pallas kernels for 5% -> 4%
where the time goes in v7:
time: 72.4 us; the launch traced here: 72 us
  blocking collectives  46.7 us (65%)
  Pallas kernels  10 us (14%)
  starting transfers between devices  8.9 us (12%)
  waiting for transfers between devices  5.29 us (7%)
  between operations  0.8 us (1%)
    all_to_all x2, blocking collectives, exchanged(): return lax.all_to_all(x, 'res', split_axis=0, concat_axis=0, tiled=True)  23.4 us
    all_to_all x2, blocking collectives, among_class(): return lax.all_to_all(x, 'res', 0, 0, axis_index_groups=groups, tiled=True)  23.4 us
    pallas_call x7, Pallas kernels, kernel_call(): pl.pallas_call(fetching if fetched else body, out_shape=tuple((jax.ShapeD...  8.99 us
    all_to_all x1, starting transfers between devices, among_class(): return lax.all_to_all(x, 'res', 0, 0, axis_index_groups=groups, tiled=True)  8.32 us
    all_to_all x1, waiting for transfers between devices, among_class(): return lax.all_to_all(x, 'res', 0, 0, axis_index_groups=groups, tiled=True)  4.03 us
  transfers between devices with their start and end apart: 4, of which 3 were waited for; matrix products, arithmetic and copies ran while one was open for 0% of the time, Pallas kernels for 4%

profile of v7, /device:TPU:0, one launch (start us, length us, event | category | flops | bytes accessed | tf_op | source)
XLA Modules:
  0.0 72.0 jit_solution(17691754976950718724)
XLA Ops:
  0.6 0.0 copy-start.1
  0.6 0.0 copy-start.2
  0.7 0.0 copy-start.3
  0.7 2.0 %bias.1 = bf16[16,32,128]{2,1,0:T(8,128)(2,1)} custom-call(bf16[4,128,128]{2,1,0:T(8,128)(2,1)} %pair_ref.1, bf16[8,128]{1,0:T(8,128)(2,1)} %bitcast.8), custom_call_target="tpu_custom_call" | custom-call | tf_op jit(solution)/shard_map/bias/pallas_call | solution.py:97
  2.7 8.3 %all-to-all-start = ((bf16[16,32,128]{2,1,0:T(8,128)(2,1)}), bf16[16,32,128]{2,1,0:T(8,128)(2,1)S(1)}, u32[]{:S(2)}, u32[]{:S(2)}) async-start(bf16[16,32,128]{2,1,0:T(8,128)(2,1)} %bias.1), calls=%async_computation | async-start | bytes 262144 | tf_op jit(solution)/shard_map/all_to_all | solution.py:468
  11.0 0.1 collective-permute-start.1
  11.1 0.5 collective-permute-start
  11.6 1.0 %collective-permute-done.refs_2_ = s32[2,128]{1,0:T(2,128)S(1)} collective-permute-done((s32[2,128]{1,0:T(2,128)}, s32[2,128]{1,0:T(2,128)S(1)}, u32[]{:S(2)}, u32[]{:S(2)}) %collective-permute-start) | collective-permute-done | bytes 1056 | tf_op jit(solution)/shard_map/ppermute | solution.py:471
  12.6 0.0 collective-permute-done.1.refs_5_
  12.6 2.1 %row_scores.1 = (f32[4,512,128]{2,1,0:T(8,128)S(1)}, bf16[512,256]{1,0:T(8,128)(2,1)S(1)}, f32[512,256]{1,0:T(8,128)S(1)}, f32[256,256]{1,0:T(8,128)S(1)}, bf16[...) custom-call(s32[1]{0:T(128)} %bitcast.refs_0_.second_ref, s32[2,128]{1,0:T(2,128)} %refs_1_.1, ...), custom_call_target="tpu_custom_call" | custom-call | flops 134217728 | bytes 2097152 | tf_op jit(solution)/shard_map/row_scores/pallas_call | solution.py:97
  14.8 4.0 %all-to-all-done.bias_ref = bf16[16,32,128]{2,1,0:T(8,128)(2,1)S(1)} async-done(((bf16[16,32,128]{2,1,0:T(8,128)(2,1)}), bf16[16,32,128]{2,1,0:T(8,128)(2,1)S(1)}, u32[]{:S(2)}, u32[]{:S(2)}) %all-to-all-start) | async-done | bytes 131104 | tf_op jit(solution)/shard_map/all_to_all | solution.py:468
  18.8 0.0 copy-start.5
  18.8 1.0 %row_mix.1 = bf16[16,16,256]{2,1,0:T(8,128)(2,1)S(1)} custom-call(f32[4,512,128]{2,1,0:T(8,128)S(1)} %get-tuple-element.17.scores_ref, bf16[16,32,128]{2,1,0:T(8,128)(2,1)S(1)} %all-to-all-done.bias_ref, bf16[512,256]{1,0:T(8,128)(2,1)S(1)} %get-tuple-element.18.value_ref, f32[512,256]{1,0:T(8,128)S(1)} %get-tuple-element.19.gate_ref, ...), custom_call_target="tpu_custom_call" | custom-call | tf_op jit(solution)/shard_map/row_mix/pallas_call | solution.py:97
  19.8 0.0 slice-start
  19.8 0.0 copy-start.6
  19.8 0.0 copy-start
  19.8 10.7 %all_to_all.25.state_ref = bf16[16,16,256]{2,1,0:T(8,128)(2,1)S(1)} all-to-all(bf16[16,16,256]{2,1,0:T(8,128)(2,1)S(1)} %row_mix.1), channel_id=1, replica_groups={{0,2,4,6,8,10,12,14,16,18,20,22,24,26,28,30},{1,3,5,7,9,11,13,15,17,19,..., dimensions={0} | all-to-all | bytes 262144 | tf_op jit(solution)/shard_map/all_to_all | solution.py:468
  30.5 0.0 copy-done.1
  30.5 0.0 copy-done.2
  30.5 0.0 copy-done.3
  30.5 1.7 %column.1 = (bf16[64,4,256]{2,1,0:T(4,128)(2,1)S(1)}, bf16[256,32]{1,0:T(8,128)(2,1)S(1)}, bf16[16,8,1024]{2,1,0:T(8,128)(2,1)S(1)}) custom-call(bf16[16,16,256]{2,1,0:T(8,128)(2,1)S(1)} %all_to_all.25.state_ref, bf16[256,1024]{1,0:T(8,128)(2,1)S(1)} %copy-done.1, bf16[256,256]{1,0:T(8,128)(2,1)S(1)} %copy-done.2, bf16[64,256]{1,0:T(8,128)(2,1)S(1)} %bitcast.7, ...), custom_call_target="tpu_custom_call" | custom-call | tf_op jit(solution)/shard_map/column/pallas_call | solution.py:97
  32.2 12.7 %all_to_all.26.right_ref = bf16[16,8,1024]{2,1,0:T(8,128)(2,1)S(1)} all-to-all(bf16[16,8,1024]{2,1,0:T(8,128)(2,1)S(1)} %get-tuple-element.24), channel_id=1, replica_groups={{0,2,4,6,8,10,12,14,16,18,20,22,24,26,28,30},{1,3,5,7,9,11,13,15,17,19,..., dimensions={0} | all-to-all | bytes 524288 | tf_op jit(solution)/shard_map/all_to_all | solution.py:468
  44.9 0.0 collective-permute-start.2
  44.9 0.0 copy-done.5
  44.9 0.0 slice-done
  44.9 0.1 copy.17
  45.0 0.0 copy-done.6
  45.0 0.1 reshape.15.weight_ref
  45.2 1.0 %spread.1 = (bf16[1024,1024]{1,0:T(8,128)(2,1)S(1)}, f32[16,4,512]{2,1,0:T(4,128)S(1)}, bf16[64,4,256]{2,1,0:T(4,128)(2,1)}) custom-call(bf16[64,4,256]{2,1,0:T(4,128)(2,1)S(1)} %get-tuple-element.23.aligned_ref, bf16[16,8,1024]{2,1,0:T(8,128)(2,1)S(1)} %all_to_all.26.right_ref, bf16[256,32]{1,0:T(8,128)(2,1)S(1)} %get-tuple-element.25.left_ref, ...), custom_call_target="tpu_custom_call" | custom-call | flops 67108864 | bytes 2097152 | tf_op jit(solution)/shard_map/spread/pallas_call | solution.py:533
  46.2 0.0 copy-start.4
  46.2 0.2 collective-permute-done.2.other_ref
  46.4 0.0 copy-done
  46.4 1.0 %pair.1 = (f32[512,128]{1,0:T(8,128)S(1)}, f32[512,128]{1,0:T(8,128)S(1)}, bf16[32,4,1024]{2,1,0:T(4,128)(2,1)S(1)}) custom-call(s32[1]{0:T(128)} %bitcast.refs_0_.second_ref, f32[16,4,512]{2,1,0:T(4,128)S(1)} %get-tuple-element.27.half_ref, bf16[16,8,1024]{2,1,0:T(8,128)(2,1)S(1)} %collective-permute-done.2.other_ref, ...), custom_call_target="tpu_custom_call" | custom-call | tf_op jit(solution)/shard_map/pair/pallas_call | solution.py:97
  47.4 12.9 %all_to_all.27.both_ref = bf16[32,4,1024]{2,1,0:T(4,128)(2,1)S(1)} all-to-all(bf16[32,4,1024]{2,1,0:T(4,128)(2,1)S(1)} %get-tuple-element.29), channel_id=1, replica_groups=mesh['crop'=1,'res'=32] {'res'}, dimensions={0} | all-to-all | bytes 524288 | tf_op jit(solution)/shard_map/all_to_all | solution.py:435
  60.3 0.3 triangle.1
  60.6 10.4 %all_to_all.28.back_ref = bf16[32,4,512]{2,1,0:T(4,128)(2,1)S(1)} all-to-all(bf16[32,4,512]{2,1,0:T(4,128)(2,1)S(1)} %triangle.1), channel_id=1, replica_groups=mesh['crop'=1,'res'=32] {'res'}, dimensions={0} | all-to-all | bytes 262144 | tf_op jit(solution)/shard_map/all_to_all | solution.py:435
  71.0 0.0 copy-done.4
  71.0 1.0 %final.1 = bf16[4,128,128]{2,1,0:T(8,128)(2,1)} custom-call(bf16[32,4,512]{2,1,0:T(4,128)(2,1)S(1)} %all_to_all.28.back_ref, f32[512,128]{1,0:T(8,128)S(1)} %get-tuple-element.30.one_ref, f32[512,128]{1,0:T(8,128)S(1)} %get-tuple-element.31.gate_ref, bf16[128,128]{1,0:T(8,128)(2,1)S(1)} %copy-done.4), custom_call_target="tpu_custom_call" | custom-call | tf_op jit(solution)/shard_map/final/pallas_call | solution.py:97
  (1 shorter events, 0.0 us)
Async XLA Ops:
  0.6 29.9 %copy-start.1 = (bf16[256,1024]{1,0:T(8,128)(2,1)S(1)}, bf16[256,1024]{1,0:T(8,128)(2,1)}, u32[]{:S(2)}) copy-start(bf16[256,1024]{1,0:T(8,128)(2,1)} %weight_ref.2) | copy-start | bytes 1572868
  0.6 29.8 %copy-start.2 = (bf16[256,256]{1,0:T(8,128)(2,1)S(1)}, bf16[256,256]{1,0:T(8,128)(2,1)}, u32[]{:S(2)}) copy-start(bf16[256,256]{1,0:T(8,128)(2,1)} %readout_ref.1) | copy-start | bytes 393220
  0.7 29.8 %copy-start.3 = (bf16[256,64]{0,1:T(8,128)(2,1)S(1)}, bf16[256,64]{0,1:T(8,128)(2,1)}, u32[]{:S(2)}) copy-start(bf16[256,64]{0,1:T(8,128)(2,1)} %param.24) | copy-start | bytes 98308
  2.7 16.1 %all-to-all-start = ((bf16[16,32,128]{2,1,0:T(8,128)(2,1)}), bf16[16,32,128]{2,1,0:T(8,128)(2,1)S(1)}, u32[]{:S(2)}, u32[]{:S(2)}) async-start(bf16[16,32,128]{2,1,0:T(8,128)(2,1)} %bias.1), calls=%async_computation | async-start | bytes 262144 | tf_op jit(solution)/shard_map/all_to_all | solution.py:468
  11.0 1.6 %collective-permute-start.1 = (bf16[2,128,256]{2,1,0:T(8,128)(2,1)}, bf16[2,128,256]{2,1,0:T(8,128)(2,1)S(1)}, u32[]{:S(2)}, u32[]{:S(2)}) collective-permute-start(bf16[2,128,256]{2,1,0:T(8,128)(2,1)} %refs_4_.1), channel_id=1, source_target_pairs={{0,1},{1,0},{2,3},{3,2},{4,5},{5,4},{6,7},{7,6},{8,9},{9,8},{10,11... | collective-permute-start | bytes 393224 | tf_op jit(solution)/shard_map/ppermute | solution.py:471
  11.1 1.5 %collective-permute-start = (s32[2,128]{1,0:T(2,128)}, s32[2,128]{1,0:T(2,128)S(1)}, u32[]{:S(2)}, u32[]{:S(2)}) collective-permute-start(s32[2,128]{1,0:T(2,128)} %refs_1_.1), channel_id=1, source_target_pairs={{0,1},{1,0},{2,3},{3,2},{4,5},{5,4},{6,7},{7,6},{8,9},{9,8},{10,11... | collective-permute-start | bytes 3080 | tf_op jit(solution)/shard_map/ppermute | solution.py:471
  18.8 26.1 %copy-start.5 = (bf16[128,640]{1,0:T(8,128)(2,1)S(1)}, bf16[128,640]{1,0:T(8,128)(2,1)}, u32[]{:S(2)}) copy-start(bf16[128,640]{1,0:T(8,128)(2,1)} %param.26) | copy-start | bytes 491524
  19.8 25.1 %slice-start = ((bf16[128,640]{1,0:T(8,128)(2,1)}), bf16[128,512]{1,0:T(8,128)(2,1)S(1)}, s32[]{:S(2)}) async-start(bf16[128,640]{1,0:T(8,128)(2,1)} %param.26), calls=%async_computation.5 | async-start | bytes 262144 | tf_op jit(solution)/shard_map/slice | solution.py:566
  19.8 25.2 %copy-start.6 = (bf16[1024,128]{1,0:T(8,128)(2,1)S(1)}, bf16[1024,128]{1,0:T(8,128)(2,1)}, u32[]{:S(2)}) copy-start(bf16[1024,128]{1,0:T(8,128)(2,1)} %param.25) | copy-start | bytes 786436
  19.8 26.6 %copy-start = (bf16[4,128,128]{2,1,0:T(8,128)(2,1)S(1)}, bf16[4,128,128]{2,1,0:T(8,128)(2,1)}, u32[]{:S(2)}) copy-start(bf16[4,128,128]{2,1,0:T(8,128)(2,1)} %pair_ref.1) | copy-start | bytes 393220
  44.9 1.5 %collective-permute-start.2 = (bf16[16,8,1024]{2,1,0:T(8,128)(2,1)S(1)}, bf16[16,8,1024]{2,1,0:T(8,128)(2,1)S(1)}, u32[]{:S(2)}, u32[]{:S(2)}) collective-permute-start(bf16[16,8,1024]{2,1,0:T(8,128)(2,1)S(1)} %all_to_all.26.right_ref), channel_id=1, source_target_pairs={{0,1},{1,0},{2,3},{3,2},{4,5},{5,4},{6,7},{7,6},{8,9},{9,8},{10,11... | collective-permute-start | bytes 786440 | tf_op jit(solution)/shard_map/ppermute | solution.py:471
  46.2 24.9 %copy-start.4 = (bf16[128,128]{1,0:T(8,128)(2,1)S(1)}, bf16[128,128]{1,0:T(8,128)(2,1)}, u32[]{:S(2)}) copy-start(bf16[128,128]{1,0:T(8,128)(2,1)} %weight_ref.3) | copy-start | bytes 98308

commit v8 on v7

--- a/solution.py
+++ b/solution.py
@@ -132,28 +132,54 @@
     return jnp.where(flip, other, mine), jnp.where(flip, mine, other)
 
 
-def row_scores_kernel(
-    second_ref, ids_ref, other_ids_ref, mask_ref, state_ref, other_ref, table_ref, weight_ref,
-    readout_ref, factor_ref,
-    scores_ref, value_ref, gate_ref, start_ref, held_ref, wide_ref,
+def own_scores_kernel(
+    second_ref, ids_ref, mask_ref, state_ref, table_ref, weight_ref, readout_ref, factor_ref,
+    scores_ref, value_ref, gate_ref, start_ref,
+    held_mask_ref, held_table_ref, held_weight_ref, held_ref, wide_ref,
     *, heads, own_rows, arrive,
 ):
-    own_sequences, length, channels = state_ref.shape
+    row_scores(
+        second_ref, ids_ref, mask_ref, state_ref, table_ref, weight_ref,
+        scores_ref, value_ref, gate_ref, start_ref,
+        heads=heads, own_rows=own_rows, arrive=arrive,
+    )
+    held_mask_ref[...] = mask_ref[...]
+    held_table_ref[...] = table_ref[...]
+    held_weight_ref[...] = weight_ref[...]
+    held_ref[...] = readout_ref[...]
+    widen(factor_ref, wide_ref, own_rows)
+
+
+def other_scores_kernel(
+    second_ref, ids_ref, mask_ref, state_ref, table_ref, weight_ref,
+    scores_ref, value_ref, gate_ref, start_ref,
+    *, heads, own_rows,
+):
+    row_scores(
+        second_ref, ids_ref, mask_ref, state_ref, table_ref, weight_ref,
+        scores_ref, value_ref, gate_ref, start_ref,
+        heads=heads, own_rows=own_rows, arrive=None,
+    )
+
+
+def row_scores(
+    second_ref, ids_ref, mask_ref, state_ref, table_ref, weight_ref,
+    scores_ref, value_ref, gate_ref, start_ref,
+    *, heads, own_rows, arrive,
+):
+    sequences, length, channels = state_ref.shape
     tokens = table_ref.shape[0]
     second = second_ref[0]
-    ids = jnp.concatenate(ordered(second, ids_ref[...], other_ids_ref[...]), 0)
-    states = jnp.concatenate(
-        ordered(second, state_ref[...].astype(F32), other_ref[...].astype(F32)), 0
-    )
-    sequences = 2 * own_sequences
+    ids = ids_ref[...]
+    states = state_ref[...].astype(F32)
     starts = []
     for s in range(sequences):
         hot = (iota((tokens, length), 0) == ids[s : s + 1, :]).astype(F32).astype(BF16)
         starts.append(states[s] + t_dot(hot, table_ref[...]))
     start = jnp.concatenate(starts, 0)
     normed = normalized(start, -1)
-    arrive()
-    held_ref[...] = readout_ref[...]
+    if arrive is not None:
+        arrive()
     projected = dot(normed.astype(BF16), weight_ref[:, channels : 3 * channels])
     key = projected[:, :channels].astype(BF16)
     value_ref[...] = projected[:, channels:].astype(BF16)
@@ -190,7 +216,9 @@
             scores_ref[s, u * size : (u + 1) * size] = (
                 dot_t(jnp.concatenate(spread, 0), key[s * length : (s + 1) * length, part]) + extra
             )
-    width = factor_ref.shape[0] // 2
+
+def widen(factor_ref, wide_ref, own_rows):
+    width, channels = factor_ref.shape[0] // 2, factor_ref.shape[1]
     right = factor_ref[width:].astype(F32)
     repeated = jnp.broadcast_to(right[:, None, :], (width, own_rows, channels)).reshape(
         width * own_rows, channels
@@ -208,9 +236,13 @@
 
 
 def row_mix_kernel(
-    scores_ref, bias_ref, value_ref, gate_ref, start_ref, weight_ref, out_ref, *, heads, own_rows
-):
-    sequences, expanded, length = scores_ref.shape
+    second_ref, own_scores_ref, own_value_ref, own_gate_ref, own_start_ref,
+    other_scores_ref, other_value_ref, other_gate_ref, other_start_ref,
+    bias_ref, weight_ref, out_ref,
+    *, heads, own_rows,
+):
+    sequences, expanded, length = own_scores_ref.shape
+    value_ref = own_value_ref
     channels = value_ref.shape[1]
     groups = out_ref.shape[0]
     per = max(1, 8 // own_rows)
@@ -232,7 +264,13 @@
     ]
     size = len(masks) * tall
     pieces = []
-    for s in range(sequences):
+    sets = (
+        (own_scores_ref, own_value_ref, own_gate_ref, own_start_ref),
+        (other_scores_ref, other_value_ref, other_gate_ref, other_start_ref),
+    )
+    for (scores_ref, value_ref, gate_ref, start_ref), s in [
+        (refs, s) for refs in sets for s in range(sequences)
+    ]:
         weights, scale = softmax_parts(scores_ref[s] + bias)
         mixed = []
         for u, part in enumerate(parts):
@@ -252,7 +290,8 @@
         for h in range(per):
             after = after + update[:, h * own_rows : (h + 1) * own_rows]
         pieces.append(after)
-    out_ref[...] = jnp.concatenate(pieces, 1).astype(BF16)
+    own, other = jnp.concatenate(pieces[:sequences], 1), jnp.concatenate(pieces[sequences:], 1)
+    out_ref[...] = jnp.concatenate(ordered(second_ref[0], own, other), 1).astype(BF16)
 
 
 def column_kernel(
@@ -479,40 +518,60 @@
     )
     bias = among_class(bias)
     factors = product_factor_matrices.T
-    scores, value, gate, start, readout, wide = kernel_call(
-        functools.partial(row_scores_kernel, heads=heads, own_rows=own_rows),
-        [
-            ((2 * own_sequences, length // 2 * heads, length), F32),
-            ((2 * rows, channels), BF16),
-            ((rows * max(1, 8 // own_rows), channels), F32),
-            ((rows, channels), F32),
+    parts = [
+        ((own_sequences, half * own_rows * heads, length), F32),
+        ((rows, channels), BF16),
+        ((rows // 2 * max(1, 8 // own_rows), channels), F32),
+        ((rows // 2, channels), F32),
+    ]
+    estimate = dict(flops=2 * rows * channels * 4 * channels, nbytes=1 << 21)
+    *own, mask, table, row_weight, readout, wide = kernel_call(
+        functools.partial(own_scores_kernel, heads=heads, own_rows=own_rows),
+        parts
+        + [
+            ((1, length), jnp.int32),
+            (symbol_lookup_matrix.shape, BF16),
+            (row_projection_weight.shape, BF16),
             ((channels, channels), BF16),
             ((width * own_rows, own_rows * channels), BF16),
         ],
         (
             second,
             homolog_symbol_ids,
-            from_other_core(homolog_symbol_ids),
             residue_attend_mask.reshape(1, length),
             alignment_state,
-            from_other_core(alignment_state),
             symbol_lookup_matrix,
             row_projection_weight,
             horizontal_readout_matrix,
             factors,
         ),
-        "row_scores",
-        flops=2 * rows * channels * 4 * channels,
-        nbytes=1 << 21,
+        "own_scores",
         scalars=1,
-        fetched=(1, 3, 4, 6, 7, 8, 9),
-        late=(3, 7, 8, 9),
+        fetched=(1, 3, 4, 2, 5, 6, 7),
+        late=(2, 5, 6, 7),
+        **estimate,
+    )
+    other_scores = kernel_call(
+        functools.partial(other_scores_kernel, heads=heads, own_rows=own_rows),
+        parts,
+        (
+            second,
+            from_other_core(homolog_symbol_ids),
+            mask,
+            from_other_core(alignment_state),
+            table,
+            row_weight,
+        ),
+        "other_scores",
+        scalars=1,
+        **estimate,
     )
     (after_rows,) = kernel_call(
         functools.partial(row_mix_kernel, heads=heads, own_rows=own_rows),
         [((half, 2 * own_sequences * own_rows, channels), BF16)],
-        (scores, bias, value, gate, start, readout),
+        (second, *own, *other_scores, bias, readout),
         "row_mix",
+        scalars=1,
     )
     by_residue = among_class(after_rows)
     per = max(1, 8 // own_rows)

time: 72.4 us -> 71.3 us (0.985)
  blocking collectives: 46.7 us -> 45.8 us
    ppermute x3, waiting for transfers between devices: 1.26 us -> 0.21 us  [from_other_core(): return lax.ppermute(x, 'res', [(i, i ^ 1) for i in range(devices)])]
    all_to_all x2, blocking collectives: 23.4 us -> 22.4 us  [among_class(): return lax.all_to_all(x, 'res', 0, 0, axis_index_groups=groups, tiled=True)]
    pallas_call x7 -> x8, Pallas kernels: 8.99 us -> 9.59 us  [kernel_call(): pl.pallas_call(fetching if fetched else body, out_shape=tuple((jax.ShapeD...]
  transfers between devices with their start and end apart: 4 -> 4, of which waited for: 3 -> 2; matrix products, arithmetic and copies ran while one was open for 0% -> 0% of each run, Pallas kernels for 4% -> 5%
where the time goes in v8:
time: 71.3 us; the launch traced here: 71 us
  blocking collectives  45.8 us (64%)
  Pallas kernels  10.6 us (15%)
  starting transfers between devices  8.9 us (12%)
  waiting for transfers between devices  4.6 us (6%)
  between operations  0.79 us (1%)
    all_to_all x2, blocking collectives, exchanged(): return lax.all_to_all(x, 'res', split_axis=0, concat_axis=0, tiled=True)  23.4 us
    all_to_all x2, blocking collectives, among_class(): return lax.all_to_all(x, 'res', 0, 0, axis_index_groups=groups, tiled=True)  22.4 us
    pallas_call x8, Pallas kernels, kernel_call(): pl.pallas_call(fetching if fetched else body, out_shape=tuple((jax.ShapeD...  9.59 us
    all_to_all x1, starting transfers between devices, among_class(): return lax.all_to_all(x, 'res', 0, 0, axis_index_groups=groups, tiled=True)  8.32 us
    all_to_all x1, waiting for transfers between devices, among_class(): return lax.all_to_all(x, 'res', 0, 0, axis_index_groups=groups, tiled=True)  4.39 us
  transfers between devices with their start and end apart: 4, of which 2 were waited for; matrix products, arithmetic and copies ran while one was open for 0% of the time, Pallas kernels for 5%

profile of v8, /device:TPU:0, one launch (start us, length us, event | category | flops | bytes accessed | tf_op | source)
XLA Modules:
  0.0 71.0 jit_solution(12594487373431179816)
XLA Ops:
  0.6 1.9 %bias.1 = bf16[16,32,128]{2,1,0:T(8,128)(2,1)} custom-call(bf16[4,128,128]{2,1,0:T(8,128)(2,1)} %pair_ref.1, bf16[8,128]{1,0:T(8,128)(2,1)} %bitcast.8), custom_call_target="tpu_custom_call" | custom-call | tf_op jit(solution)/shard_map/bias/pallas_call | solution.py:97
  2.6 8.3 %all-to-all-start = ((bf16[16,32,128]{2,1,0:T(8,128)(2,1)}), bf16[16,32,128]{2,1,0:T(8,128)(2,1)S(1)}, u32[]{:S(2)}, u32[]{:S(2)}) async-start(bf16[16,32,128]{2,1,0:T(8,128)(2,1)} %bias.1), calls=%async_computation | async-start | bytes 262144 | tf_op jit(solution)/shard_map/all_to_all | solution.py:507
  10.9 0.1 collective-permute-start.1
  11.0 0.5 collective-permute-start
  11.5 0.0 copy-start.1
  11.5 0.0 copy-start.2
  11.5 0.0 copy-start.3
  11.5 2.0 %own_scores.1 = (f32[2,512,128]{2,1,0:T(8,128)S(1)}, bf16[256,256]{1,0:T(8,128)(2,1)S(1)}, f32[256,256]{1,0:T(8,128)S(1)}, f32[128,256]{1,0:T(8,128)S(1)}, s32[1...) custom-call(s32[1]{0:T(128)} %bitcast.refs_0_.second_ref, ...), custom_call_target="tpu_custom_call" | custom-call | flops 134217728 | bytes 2097152 | tf_op jit(solution)/shard_map/own_scores/pallas_call | solution.py:97
  13.5 0.0 collective-permute-done.ids_ref
  13.5 0.0 collective-permute-done.1.state_ref
  13.5 0.8 %other_scores.1 = (f32[2,512,128]{2,1,0:T(8,128)S(1)}, bf16[256,256]{1,0:T(8,128)(2,1)S(1)}, f32[256,256]{1,0:T(8,128)S(1)}, f32[128,256]{1,0:T(8,128)S(1)}) custom-call(s32[1]{0:T(128)} %bitcast.refs_0_.second_ref, s32[2,128]{1,0:T(2,128)S(1)} %collective-permute-done.ids_ref, s32[1,128]{1,0:T(1,128)S(1)} %get-tuple-element.28.mask_ref, ...), custom_call_target="tpu_custom_call" | custom-call | flops 134217728 | bytes 2097152 | tf_op jit(solution)/shard_map/other_scores/pallas_call | solution.py:97
  14.3 4.4 %all-to-all-done.bias_ref = bf16[16,32,128]{2,1,0:T(8,128)(2,1)S(1)} async-done(((bf16[16,32,128]{2,1,0:T(8,128)(2,1)}), bf16[16,32,128]{2,1,0:T(8,128)(2,1)S(1)}, u32[]{:S(2)}, u32[]{:S(2)}) %all-to-all-start) | async-done | bytes 131104 | tf_op jit(solution)/shard_map/all_to_all | solution.py:507
  18.7 0.0 copy-start.5
  18.7 0.0 slice-start
  18.7 1.0 %row_mix.1 = bf16[16,16,256]{2,1,0:T(8,128)(2,1)S(1)} custom-call(s32[1]{0:T(128)} %bitcast.refs_0_.second_ref, f32[2,512,128]{2,1,0:T(8,128)S(1)} %get-tuple-element.24.own_scores_ref, bf16[256,256]{1,0:T(8,128)(2,1)S(1)} %get-tuple-element.25.own_value_ref, f32[256,256]{1,0:T(8,128)S(1)} %get-tuple-element.26.own_gate_ref, ...), custom_call_target="tpu_custom_call" | custom-call | tf_op jit(solution)/shard_map/row_mix/pallas_call | solution.py:97
  19.7 0.0 copy-start.6
  19.7 0.0 copy-start
  19.7 10.5 %all_to_all.25.state_ref = bf16[16,16,256]{2,1,0:T(8,128)(2,1)S(1)} all-to-all(bf16[16,16,256]{2,1,0:T(8,128)(2,1)S(1)} %row_mix.1), channel_id=1, replica_groups={{0,2,4,6,8,10,12,14,16,18,20,22,24,26,28,30},{1,3,5,7,9,11,13,15,17,19,..., dimensions={0} | all-to-all | bytes 262144 | tf_op jit(solution)/shard_map/all_to_all | solution.py:507
  30.3 0.0 copy-done.1
  30.3 0.0 copy-done.2
  30.3 0.0 copy-done.3
  30.3 1.7 %column.1 = (bf16[64,4,256]{2,1,0:T(4,128)(2,1)S(1)}, bf16[256,32]{1,0:T(8,128)(2,1)S(1)}, bf16[16,8,1024]{2,1,0:T(8,128)(2,1)S(1)}) custom-call(bf16[16,16,256]{2,1,0:T(8,128)(2,1)S(1)} %all_to_all.25.state_ref, bf16[256,1024]{1,0:T(8,128)(2,1)S(1)} %copy-done.1, bf16[256,256]{1,0:T(8,128)(2,1)S(1)} %copy-done.2, bf16[64,256]{1,0:T(8,128)(2,1)S(1)} %bitcast.7, ...), custom_call_target="tpu_custom_call" | custom-call | tf_op jit(solution)/shard_map/column/pallas_call | solution.py:97
  32.0 11.9 %all_to_all.26.right_ref = bf16[16,8,1024]{2,1,0:T(8,128)(2,1)S(1)} all-to-all(bf16[16,8,1024]{2,1,0:T(8,128)(2,1)S(1)} %get-tuple-element.38), channel_id=1, replica_groups={{0,2,4,6,8,10,12,14,16,18,20,22,24,26,28,30},{1,3,5,7,9,11,13,15,17,19,..., dimensions={0} | all-to-all | bytes 524288 | tf_op jit(solution)/shard_map/all_to_all | solution.py:507
  43.9 0.0 collective-permute-start.2
  43.9 0.0 copy-done.5
  43.9 0.0 copy-done.6
  43.9 0.1 reshape.15.weight_ref
  44.0 0.0 slice-done
  44.0 0.1 copy.17
  44.1 1.0 %spread.1 = (bf16[1024,1024]{1,0:T(8,128)(2,1)S(1)}, f32[16,4,512]{2,1,0:T(4,128)S(1)}, bf16[64,4,256]{2,1,0:T(4,128)(2,1)}) custom-call(bf16[64,4,256]{2,1,0:T(4,128)(2,1)S(1)} %get-tuple-element.37.aligned_ref, bf16[16,8,1024]{2,1,0:T(8,128)(2,1)S(1)} %all_to_all.26.right_ref, bf16[256,32]{1,0:T(8,128)(2,1)S(1)} %get-tuple-element.39.left_ref, ...), custom_call_target="tpu_custom_call" | custom-call | flops 67108864 | bytes 2097152 | tf_op jit(solution)/shard_map/spread/pallas_call | solution.py:592
  45.2 0.0 copy-start.4
  45.2 0.2 collective-permute-done.2.other_ref
  45.4 0.0 copy-done
  45.4 1.0 %pair.1 = (f32[512,128]{1,0:T(8,128)S(1)}, f32[512,128]{1,0:T(8,128)S(1)}, bf16[32,4,1024]{2,1,0:T(4,128)(2,1)S(1)}) custom-call(s32[1]{0:T(128)} %bitcast.refs_0_.second_ref, f32[16,4,512]{2,1,0:T(4,128)S(1)} %get-tuple-element.41.half_ref, bf16[16,8,1024]{2,1,0:T(8,128)(2,1)S(1)} %collective-permute-done.2.other_ref, ...), custom_call_target="tpu_custom_call" | custom-call | tf_op jit(solution)/shard_map/pair/pallas_call | solution.py:97
  46.4 12.9 %all_to_all.27.both_ref = bf16[32,4,1024]{2,1,0:T(4,128)(2,1)S(1)} all-to-all(bf16[32,4,1024]{2,1,0:T(4,128)(2,1)S(1)} %get-tuple-element.43), channel_id=1, replica_groups=mesh['crop'=1,'res'=32] {'res'}, dimensions={0} | all-to-all | bytes 524288 | tf_op jit(solution)/shard_map/all_to_all | solution.py:474
  59.3 0.3 triangle.1
  59.6 10.4 %all_to_all.28.back_ref = bf16[32,4,512]{2,1,0:T(4,128)(2,1)S(1)} all-to-all(bf16[32,4,512]{2,1,0:T(4,128)(2,1)S(1)} %triangle.1), channel_id=1, replica_groups=mesh['crop'=1,'res'=32] {'res'}, dimensions={0} | all-to-all | bytes 262144 | tf_op jit(solution)/shard_map/all_to_all | solution.py:474
  70.0 0.0 copy-done.4
  70.0 1.0 %final.1 = bf16[4,128,128]{2,1,0:T(8,128)(2,1)} custom-call(bf16[32,4,512]{2,1,0:T(4,128)(2,1)S(1)} %all_to_all.28.back_ref, f32[512,128]{1,0:T(8,128)S(1)} %get-tuple-element.44.one_ref, f32[512,128]{1,0:T(8,128)S(1)} %get-tuple-element.45.gate_ref, bf16[128,128]{1,0:T(8,128)(2,1)S(1)} %copy-done.4), custom_call_target="tpu_custom_call" | custom-call | tf_op jit(solution)/shard_map/final/pallas_call | solution.py:97
  (1 shorter events, 0.0 us)
Async XLA Ops:
  2.6 16.1 %all-to-all-start = ((bf16[16,32,128]{2,1,0:T(8,128)(2,1)}), bf16[16,32,128]{2,1,0:T(8,128)(2,1)S(1)}, u32[]{:S(2)}, u32[]{:S(2)}) async-start(bf16[16,32,128]{2,1,0:T(8,128)(2,1)} %bias.1), calls=%async_computation | async-start | bytes 262144 | tf_op jit(solution)/shard_map/all_to_all | solution.py:507
  10.9 2.6 %collective-permute-start.1 = (bf16[2,128,256]{2,1,0:T(8,128)(2,1)}, bf16[2,128,256]{2,1,0:T(8,128)(2,1)S(1)}, u32[]{:S(2)}, u32[]{:S(2)}) collective-permute-start(bf16[2,128,256]{2,1,0:T(8,128)(2,1)} %refs_3_.1), channel_id=1, source_target_pairs={{0,1},{1,0},{2,3},{3,2},{4,5},{5,4},{6,7},{7,6},{8,9},{9,8},{10,11... | collective-permute-start | bytes 393224 | tf_op jit(solution)/shard_map/ppermute | solution.py:510
  11.0 2.5 %collective-permute-start = (s32[2,128]{1,0:T(2,128)}, s32[2,128]{1,0:T(2,128)S(1)}, u32[]{:S(2)}, u32[]{:S(2)}) collective-permute-start(s32[2,128]{1,0:T(2,128)} %refs_1_.1), channel_id=1, source_target_pairs={{0,1},{1,0},{2,3},{3,2},{4,5},{5,4},{6,7},{7,6},{8,9},{9,8},{10,11... | collective-permute-start | bytes 3080 | tf_op jit(solution)/shard_map/ppermute | solution.py:510
  11.5 18.8 %copy-start.1 = (bf16[256,1024]{1,0:T(8,128)(2,1)S(1)}, bf16[256,1024]{1,0:T(8,128)(2,1)}, u32[]{:S(2)}) copy-start(bf16[256,1024]{1,0:T(8,128)(2,1)} %weight_ref.2) | copy-start | bytes 1572868
  11.5 18.8 %copy-start.2 = (bf16[256,256]{1,0:T(8,128)(2,1)S(1)}, bf16[256,256]{1,0:T(8,128)(2,1)}, u32[]{:S(2)}) copy-start(bf16[256,256]{1,0:T(8,128)(2,1)} %readout_ref.1) | copy-start | bytes 393220
  11.5 18.8 %copy-start.3 = (bf16[256,64]{0,1:T(8,128)(2,1)S(1)}, bf16[256,64]{0,1:T(8,128)(2,1)}, u32[]{:S(2)}) copy-start(bf16[256,64]{0,1:T(8,128)(2,1)} %param.24) | copy-start | bytes 98308
  18.7 25.2 %copy-start.5 = (bf16[128,640]{1,0:T(8,128)(2,1)S(1)}, bf16[128,640]{1,0:T(8,128)(2,1)}, u32[]{:S(2)}) copy-start(bf16[128,640]{1,0:T(8,128)(2,1)} %param.26) | copy-start | bytes 491524
  18.7 25.3 %slice-start = ((bf16[128,640]{1,0:T(8,128)(2,1)}), bf16[128,512]{1,0:T(8,128)(2,1)S(1)}, s32[]{:S(2)}) async-start(bf16[128,640]{1,0:T(8,128)(2,1)} %param.26), calls=%async_computation.5 | async-start | bytes 262144 | tf_op jit(solution)/shard_map/slice | solution.py:625
  19.7 24.2 %copy-start.6 = (bf16[1024,128]{1,0:T(8,128)(2,1)S(1)}, bf16[1024,128]{1,0:T(8,128)(2,1)}, u32[]{:S(2)}) copy-start(bf16[1024,128]{1,0:T(8,128)(2,1)} %param.25) | copy-start | bytes 786436
  19.7 25.7 %copy-start = (bf16[4,128,128]{2,1,0:T(8,128)(2,1)S(1)}, bf16[4,128,128]{2,1,0:T(8,128)(2,1)}, u32[]{:S(2)}) copy-start(bf16[4,128,128]{2,1,0:T(8,128)(2,1)} %pair_ref.1) | copy-start | bytes 393220
  43.9 1.5 %collective-permute-start.2 = (bf16[16,8,1024]{2,1,0:T(8,128)(2,1)S(1)}, bf16[16,8,1024]{2,1,0:T(8,128)(2,1)S(1)}, u32[]{:S(2)}, u32[]{:S(2)}) collective-permute-start(bf16[16,8,1024]{2,1,0:T(8,128)(2,1)S(1)} %all_to_all.26.right_ref), channel_id=1, source_target_pairs={{0,1},{1,0},{2,3},{3,2},{4,5},{5,4},{6,7},{7,6},{8,9},{9,8},{10,11... | collective-permute-start | bytes 786440 | tf_op jit(solution)/shard_map/ppermute | solution.py:510
  45.2 24.9 %copy-start.4 = (bf16[128,128]{1,0:T(8,128)(2,1)S(1)}, bf16[128,128]{1,0:T(8,128)(2,1)}, u32[]{:S(2)}) copy-start(bf16[128,128]{1,0:T(8,128)(2,1)} %weight_ref.3) | copy-start | bytes 98308

commit v9 on v8

--- a/solution.py
+++ b/solution.py
@@ -177,10 +177,11 @@
         hot = (iota((tokens, length), 0) == ids[s : s + 1, :]).astype(F32).astype(BF16)
         starts.append(states[s] + t_dot(hot, table_ref[...]))
     start = jnp.concatenate(starts, 0)
-    normed = normalized(start, -1)
+    centred = start - jnp.mean(start, -1, keepdims=True)
+    inverse = lax.rsqrt(jnp.mean(centred * centred, -1, keepdims=True) + EPSILON)
     if arrive is not None:
         arrive()
-    projected = dot(normed.astype(BF16), weight_ref[:, channels : 3 * channels])
+    projected = dot(centred.astype(BF16), weight_ref[:, channels : 3 * channels]) * inverse
     key = projected[:, :channels].astype(BF16)
     value_ref[...] = projected[:, channels:].astype(BF16)
 
@@ -190,7 +191,7 @@
         return ordered(second, low, high)[0].reshape(sequences * length // 2, channels)
 
     start_ref[...] = mine(start)
-    own = mine(normed)
+    own = mine(centred * inverse)
     per = max(1, 8 // own_rows)
     own = own.reshape(own.shape[0] // own_rows, own_rows, channels)
     own = jnp.concatenate([own] * per, 1).reshape(-1, channels).astype(BF16)

time: 71.3 us -> 70.9 us (level)
    all_to_all x2, blocking collectives: 22.4 us -> 21.7 us  [among_class(): return lax.all_to_all(x, 'res', 0, 0, axis_index_groups=groups, tiled=True)]
where the time goes in v9:
time: 70.9 us; the launch traced here: 70.5 us
  blocking collectives  45.3 us (64%)
  Pallas kernels  10.5 us (15%)
  starting transfers between devices  8.9 us (13%)
  waiting for transfers between devices  4.69 us (7%)
  between operations  0.79 us (1%)
    all_to_all x2, blocking collectives, exchanged(): return lax.all_to_all(x, 'res', split_axis=0, concat_axis=0, tiled=True)  23.7 us
    all_to_all x2, blocking collectives, among_class(): return lax.all_to_all(x, 'res', 0, 0, axis_index_groups=groups, tiled=True)  21.7 us
    pallas_call x8, Pallas kernels, kernel_call(): pl.pallas_call(fetching if fetched else body, out_shape=tuple((jax.ShapeD...  9.49 us
    all_to_all x1, starting transfers between devices, among_class(): return lax.all_to_all(x, 'res', 0, 0, axis_index_groups=groups, tiled=True)  8.32 us
    all_to_all x1, waiting for transfers between devices, among_class(): return lax.all_to_all(x, 'res', 0, 0, axis_index_groups=groups, tiled=True)  4.48 us
  transfers between devices with their start and end apart: 4, of which 2 were waited for; matrix products, arithmetic and copies ran while one was open for 0% of the time, Pallas kernels for 5%

profile of v9, /device:TPU:0, one launch (start us, length us, event | category | flops | bytes accessed | tf_op | source)
XLA Modules:
  0.0 70.5 jit_solution(2063433622120883072)
XLA Ops:
  0.6 1.9 %bias.1 = bf16[16,32,128]{2,1,0:T(8,128)(2,1)} custom-call(bf16[4,128,128]{2,1,0:T(8,128)(2,1)} %pair_ref.1, bf16[8,128]{1,0:T(8,128)(2,1)} %bitcast.8), custom_call_target="tpu_custom_call" | custom-call | tf_op jit(solution)/shard_map/bias/pallas_call | solution.py:97
  2.6 8.3 %all-to-all-start = ((bf16[16,32,128]{2,1,0:T(8,128)(2,1)}), bf16[16,32,128]{2,1,0:T(8,128)(2,1)S(1)}, u32[]{:S(2)}, u32[]{:S(2)}) async-start(bf16[16,32,128]{2,1,0:T(8,128)(2,1)} %bias.1), calls=%async_computation | async-start | bytes 262144 | tf_op jit(solution)/shard_map/all_to_all | solution.py:508
  10.9 0.1 collective-permute-start.1
  11.0 0.5 collective-permute-start
  11.5 0.0 copy-start.1
  11.5 0.0 copy-start.2
  11.5 0.0 copy-start.3
  11.5 2.0 %own_scores.1 = (f32[2,512,128]{2,1,0:T(8,128)S(1)}, bf16[256,256]{1,0:T(8,128)(2,1)S(1)}, f32[256,256]{1,0:T(8,128)S(1)}, f32[128,256]{1,0:T(8,128)S(1)}, s32[1...) custom-call(s32[1]{0:T(128)} %bitcast.refs_0_.second_ref, ...), custom_call_target="tpu_custom_call" | custom-call | flops 134217728 | bytes 2097152 | tf_op jit(solution)/shard_map/own_scores/pallas_call | solution.py:97
  13.5 0.0 collective-permute-done.ids_ref
  13.5 0.0 collective-permute-done.1.state_ref
  13.5 0.7 %other_scores.1 = (f32[2,512,128]{2,1,0:T(8,128)S(1)}, bf16[256,256]{1,0:T(8,128)(2,1)S(1)}, f32[256,256]{1,0:T(8,128)S(1)}, f32[128,256]{1,0:T(8,128)S(1)}) custom-call(s32[1]{0:T(128)} %bitcast.refs_0_.second_ref, s32[2,128]{1,0:T(2,128)S(1)} %collective-permute-done.ids_ref, s32[1,128]{1,0:T(1,128)S(1)} %get-tuple-element.28.mask_ref, ...), custom_call_target="tpu_custom_call" | custom-call | flops 134217728 | bytes 2097152 | tf_op jit(solution)/shard_map/other_scores/pallas_call | solution.py:97
  14.2 4.5 %all-to-all-done.bias_ref = bf16[16,32,128]{2,1,0:T(8,128)(2,1)S(1)} async-done(((bf16[16,32,128]{2,1,0:T(8,128)(2,1)}), bf16[16,32,128]{2,1,0:T(8,128)(2,1)S(1)}, u32[]{:S(2)}, u32[]{:S(2)}) %all-to-all-start) | async-done | bytes 131104 | tf_op jit(solution)/shard_map/all_to_all | solution.py:508
  18.7 0.0 copy-start.5
  18.7 0.0 slice-start
  18.7 1.0 %row_mix.1 = bf16[16,16,256]{2,1,0:T(8,128)(2,1)S(1)} custom-call(s32[1]{0:T(128)} %bitcast.refs_0_.second_ref, f32[2,512,128]{2,1,0:T(8,128)S(1)} %get-tuple-element.24.own_scores_ref, bf16[256,256]{1,0:T(8,128)(2,1)S(1)} %get-tuple-element.25.own_value_ref, f32[256,256]{1,0:T(8,128)S(1)} %get-tuple-element.26.own_gate_ref, ...), custom_call_target="tpu_custom_call" | custom-call | tf_op jit(solution)/shard_map/row_mix/pallas_call | solution.py:97
  19.7 0.0 copy-start.6
  19.7 0.0 copy-start
  19.7 10.5 %all_to_all.25.state_ref = bf16[16,16,256]{2,1,0:T(8,128)(2,1)S(1)} all-to-all(bf16[16,16,256]{2,1,0:T(8,128)(2,1)S(1)} %row_mix.1), channel_id=1, replica_groups={{0,2,4,6,8,10,12,14,16,18,20,22,24,26,28,30},{1,3,5,7,9,11,13,15,17,19,..., dimensions={0} | all-to-all | bytes 262144 | tf_op jit(solution)/shard_map/all_to_all | solution.py:508
  30.3 0.0 copy-done.1
  30.3 0.0 copy-done.2
  30.3 0.0 copy-done.3
  30.3 1.7 %column.1 = (bf16[64,4,256]{2,1,0:T(4,128)(2,1)S(1)}, bf16[256,32]{1,0:T(8,128)(2,1)S(1)}, bf16[16,8,1024]{2,1,0:T(8,128)(2,1)S(1)}) custom-call(bf16[16,16,256]{2,1,0:T(8,128)(2,1)S(1)} %all_to_all.25.state_ref, bf16[256,1024]{1,0:T(8,128)(2,1)S(1)} %copy-done.1, bf16[256,256]{1,0:T(8,128)(2,1)S(1)} %copy-done.2, bf16[64,256]{1,0:T(8,128)(2,1)S(1)} %bitcast.7, ...), custom_call_target="tpu_custom_call" | custom-call | tf_op jit(solution)/shard_map/column/pallas_call | solution.py:97
  32.0 11.1 %all_to_all.26.right_ref = bf16[16,8,1024]{2,1,0:T(8,128)(2,1)S(1)} all-to-all(bf16[16,8,1024]{2,1,0:T(8,128)(2,1)S(1)} %get-tuple-element.38), channel_id=1, replica_groups={{0,2,4,6,8,10,12,14,16,18,20,22,24,26,28,30},{1,3,5,7,9,11,13,15,17,19,..., dimensions={0} | all-to-all | bytes 524288 | tf_op jit(solution)/shard_map/all_to_all | solution.py:508
  43.1 0.0 collective-permute-start.2
  43.1 0.0 copy-done.5
  43.1 0.0 copy-done.6
  43.1 0.1 reshape.15.weight_ref
  43.2 0.0 slice-done
  43.2 0.1 copy.17
  43.4 1.0 %spread.1 = (bf16[1024,1024]{1,0:T(8,128)(2,1)S(1)}, f32[16,4,512]{2,1,0:T(4,128)S(1)}, bf16[64,4,256]{2,1,0:T(4,128)(2,1)}) custom-call(bf16[64,4,256]{2,1,0:T(4,128)(2,1)S(1)} %get-tuple-element.37.aligned_ref, bf16[16,8,1024]{2,1,0:T(8,128)(2,1)S(1)} %all_to_all.26.right_ref, bf16[256,32]{1,0:T(8,128)(2,1)S(1)} %get-tuple-element.39.left_ref, ...), custom_call_target="tpu_custom_call" | custom-call | flops 67108864 | bytes 2097152 | tf_op jit(solution)/shard_map/spread/pallas_call | solution.py:593
  44.4 0.0 copy-start.4
  44.4 0.2 collective-permute-done.2.other_ref
  44.6 0.0 copy-done
  44.6 1.0 %pair.1 = (f32[512,128]{1,0:T(8,128)S(1)}, f32[512,128]{1,0:T(8,128)S(1)}, bf16[32,4,1024]{2,1,0:T(4,128)(2,1)S(1)}) custom-call(s32[1]{0:T(128)} %bitcast.refs_0_.second_ref, f32[16,4,512]{2,1,0:T(4,128)S(1)} %get-tuple-element.41.half_ref, bf16[16,8,1024]{2,1,0:T(8,128)(2,1)S(1)} %collective-permute-done.2.other_ref, ...), custom_call_target="tpu_custom_call" | custom-call | tf_op jit(solution)/shard_map/pair/pallas_call | solution.py:97
  45.6 13.2 %all_to_all.27.both_ref = bf16[32,4,1024]{2,1,0:T(4,128)(2,1)S(1)} all-to-all(bf16[32,4,1024]{2,1,0:T(4,128)(2,1)S(1)} %get-tuple-element.43), channel_id=1, replica_groups=mesh['crop'=1,'res'=32] {'res'}, dimensions={0} | all-to-all | bytes 524288 | tf_op jit(solution)/shard_map/all_to_all | solution.py:475
  58.8 0.3 triangle.1
  59.1 10.4 %all_to_all.28.back_ref = bf16[32,4,512]{2,1,0:T(4,128)(2,1)S(1)} all-to-all(bf16[32,4,512]{2,1,0:T(4,128)(2,1)S(1)} %triangle.1), channel_id=1, replica_groups=mesh['crop'=1,'res'=32] {'res'}, dimensions={0} | all-to-all | bytes 262144 | tf_op jit(solution)/shard_map/all_to_all | solution.py:475
  69.5 0.0 copy-done.4
  69.6 1.0 %final.1 = bf16[4,128,128]{2,1,0:T(8,128)(2,1)} custom-call(bf16[32,4,512]{2,1,0:T(4,128)(2,1)S(1)} %all_to_all.28.back_ref, f32[512,128]{1,0:T(8,128)S(1)} %get-tuple-element.44.one_ref, f32[512,128]{1,0:T(8,128)S(1)} %get-tuple-element.45.gate_ref, bf16[128,128]{1,0:T(8,128)(2,1)S(1)} %copy-done.4), custom_call_target="tpu_custom_call" | custom-call | tf_op jit(solution)/shard_map/final/pallas_call | solution.py:97
  (1 shorter events, 0.0 us)
Async XLA Ops:
  2.6 16.1 %all-to-all-start = ((bf16[16,32,128]{2,1,0:T(8,128)(2,1)}), bf16[16,32,128]{2,1,0:T(8,128)(2,1)S(1)}, u32[]{:S(2)}, u32[]{:S(2)}) async-start(bf16[16,32,128]{2,1,0:T(8,128)(2,1)} %bias.1), calls=%async_computation | async-start | bytes 262144 | tf_op jit(solution)/shard_map/all_to_all | solution.py:508
  10.9 2.6 %collective-permute-start.1 = (bf16[2,128,256]{2,1,0:T(8,128)(2,1)}, bf16[2,128,256]{2,1,0:T(8,128)(2,1)S(1)}, u32[]{:S(2)}, u32[]{:S(2)}) collective-permute-start(bf16[2,128,256]{2,1,0:T(8,128)(2,1)} %refs_3_.1), channel_id=1, source_target_pairs={{0,1},{1,0},{2,3},{3,2},{4,5},{5,4},{6,7},{7,6},{8,9},{9,8},{10,11... | collective-permute-start | bytes 393224 | tf_op jit(solution)/shard_map/ppermute | solution.py:511
  11.0 2.5 %collective-permute-start = (s32[2,128]{1,0:T(2,128)}, s32[2,128]{1,0:T(2,128)S(1)}, u32[]{:S(2)}, u32[]{:S(2)}) collective-permute-start(s32[2,128]{1,0:T(2,128)} %refs_1_.1), channel_id=1, source_target_pairs={{0,1},{1,0},{2,3},{3,2},{4,5},{5,4},{6,7},{7,6},{8,9},{9,8},{10,11... | collective-permute-start | bytes 3080 | tf_op jit(solution)/shard_map/ppermute | solution.py:511
  11.5 18.8 %copy-start.1 = (bf16[256,1024]{1,0:T(8,128)(2,1)S(1)}, bf16[256,1024]{1,0:T(8,128)(2,1)}, u32[]{:S(2)}) copy-start(bf16[256,1024]{1,0:T(8,128)(2,1)} %weight_ref.2) | copy-start | bytes 1572868
  11.5 18.8 %copy-start.2 = (bf16[256,256]{1,0:T(8,128)(2,1)S(1)}, bf16[256,256]{1,0:T(8,128)(2,1)}, u32[]{:S(2)}) copy-start(bf16[256,256]{1,0:T(8,128)(2,1)} %readout_ref.1) | copy-start | bytes 393220
  11.5 18.8 %copy-start.3 = (bf16[256,64]{0,1:T(8,128)(2,1)S(1)}, bf16[256,64]{0,1:T(8,128)(2,1)}, u32[]{:S(2)}) copy-start(bf16[256,64]{0,1:T(8,128)(2,1)} %param.24) | copy-start | bytes 98308
  18.7 24.4 %copy-start.5 = (bf16[128,640]{1,0:T(8,128)(2,1)S(1)}, bf16[128,640]{1,0:T(8,128)(2,1)}, u32[]{:S(2)}) copy-start(bf16[128,640]{1,0:T(8,128)(2,1)} %param.26) | copy-start | bytes 491524
  18.7 24.5 %slice-start = ((bf16[128,640]{1,0:T(8,128)(2,1)}), bf16[128,512]{1,0:T(8,128)(2,1)S(1)}, s32[]{:S(2)}) async-start(bf16[128,640]{1,0:T(8,128)(2,1)} %param.26), calls=%async_computation.5 | async-start | bytes 262144 | tf_op jit(solution)/shard_map/slice | solution.py:626
  19.7 23.4 %copy-start.6 = (bf16[1024,128]{1,0:T(8,128)(2,1)S(1)}, bf16[1024,128]{1,0:T(8,128)(2,1)}, u32[]{:S(2)}) copy-start(bf16[1024,128]{1,0:T(8,128)(2,1)} %param.25) | copy-start | bytes 786436
  19.7 24.9 %copy-start = (bf16[4,128,128]{2,1,0:T(8,128)(2,1)S(1)}, bf16[4,128,128]{2,1,0:T(8,128)(2,1)}, u32[]{:S(2)}) copy-start(bf16[4,128,128]{2,1,0:T(8,128)(2,1)} %pair_ref.1) | copy-start | bytes 393220
  43.1 1.5 %collective-permute-start.2 = (bf16[16,8,1024]{2,1,0:T(8,128)(2,1)S(1)}, bf16[16,8,1024]{2,1,0:T(8,128)(2,1)S(1)}, u32[]{:S(2)}, u32[]{:S(2)}) collective-permute-start(bf16[16,8,1024]{2,1,0:T(8,128)(2,1)S(1)} %all_to_all.26.right_ref), channel_id=1, source_target_pairs={{0,1},{1,0},{2,3},{3,2},{4,5},{5,4},{6,7},{7,6},{8,9},{9,8},{10,11... | collective-permute-start | bytes 786440 | tf_op jit(solution)/shard_map/ppermute | solution.py:511
  44.4 25.1 %copy-start.4 = (bf16[128,128]{1,0:T(8,128)(2,1)S(1)}, bf16[128,128]{1,0:T(8,128)(2,1)}, u32[]{:S(2)}) copy-start(bf16[128,128]{1,0:T(8,128)(2,1)} %weight_ref.3) | copy-start | bytes 98308
